TPU v7x, 32 devices: a whole 2x2x4 slice. The times are simulated.
32 devices in a mesh: section: 2 (over x), group: 4 (over z), dp: 4 (over y, core).
Axes of the slice: x: 2, y: 2, z: 4, core: 2. Of those that a mesh axis runs over, the one named last changes fastest.
Arguments:
- inputs_x: bfloat16 [32, 128, 1536], P(('group', 'dp')), may hold values from -6 to 6
- cotangent: bfloat16 [32, 128, 1536], P(('group', 'dp')), may hold values from -6 to 6
- lengths: int32 [32], P(('group', 'dp')), may hold values from 32 to 128, as said below
- attn_gain: bfloat16 [2, 1536], P('section', ('group', 'dp')), may hold values from 0.099609375 to 1.8984375
- qkv_weight: bfloat16 [2, 1536, 3072], P('section', ('group', 'dp')), may hold values from -0.15625 to 0.15625
- out_weight: bfloat16 [2, 1536, 1536], P('section', ('group', 'dp')), may hold values from -0.4375 to 0.4375
- ffn_gain: bfloat16 [2, 1536], P('section', ('group', 'dp')), may hold values from 0.099609375 to 1.8984375
- gate_up: bfloat16 [2, 1536, 8192], P('section', ('group', 'dp')), may hold values from -0.15625 to 0.15625
- down_weight: bfloat16 [2, 4096, 1536], P('section', ('group', 'dp')), may hold values from -0.09375 to 0.09375
Outputs:
- section_out: bfloat16 [2, 32, 128, 1536], P('section', ('group', 'dp'))
- input_grads: float32 [2, 32, 128, 1536], P('section', ('group', 'dp'))
- attn_gain_grad: float32 [2, 1536], P('section', 'group')
- qkv_grad: float32 [2, 1536, 3072], P('section', 'group')
- out_grad: float32 [2, 1536, 1536], P('section', 'group')
- ffn_gain_grad: float32 [2, 1536], P('section', 'group')
- gate_up_grad: float32 [2, 1536, 8192], P('section', 'group')
- down_grad: float32 [2, 4096, 1536], P('section', 'group')
Inputs may be any that keep to these rules, and one draw needn't show every extreme that they name: Sequence b occupies slots 0 to lengths[b] - 1; the rest of its 128 slots is padding. Some sequence is 128 long and some 32 long in every draw.
All inputs are finite; a program needn't handle non-finite values.
Results may differ from a plain program's by a relative error of at most 0.029.
Values may be sent and summed in bfloat16 or wider, within the bound.
A program may use at most 256 MiB of HBM per device.

v0:
```python
import jax
import jax.numpy as jnp
from jax import lax
from jax.sharding import PartitionSpec as P

H = 16
KVH = 8
HD = 96
FF = 4096
MICRO = 2


norm_eps = 1e-05
rope_base = 100000.0
masked_score = -1e30


def passed_along(value, axis, by):
    length = lax.axis_size(axis)
    pairs = [(i, i + by) for i in range(length) if 0 <= i + by < length]
    return lax.ppermute(value, axis, pairs)


def rope_tables(slot_count, head_width):
    half_width = head_width // 2
    frequency = rope_base ** (-(jnp.arange(half_width, dtype=jnp.float32) * 2.0 / head_width))
    angles = jnp.arange(slot_count, dtype=jnp.float32)[:, None] * frequency[None, :]
    return (jnp.cos(angles), jnp.sin(angles))


def rotate(vector, cosines, sine_table):
    half_width = vector.shape[-1] // 2
    front_half = vector[..., :half_width]
    back_half = vector[..., half_width:]
    cos_wide = cosines[:, None, :]
    sin_wide = sine_table[:, None, :]
    return jnp.concatenate(
        [
            front_half * cos_wide - back_half * sin_wide,
            back_half * cos_wide + front_half * sin_wide,
        ],
        -1,
    )


def norm_scale(vector):
    return lax.rsqrt(jnp.mean(vector * vector, -1, keepdims=True) + norm_eps)


def allowed_keys(lengths, slot_count):
    position = jnp.arange(slot_count, dtype=jnp.int32)
    causal = position[None, :] <= position[:, None]
    return causal[None] & (position[None, None, :] < lengths[:, None, None])


def padding(lengths, slot_count):
    position = jnp.arange(slot_count, dtype=jnp.int32)
    return (position[None, :] < lengths[:, None]).astype(jnp.float32)[..., None]


def norm_back(vector, scale, gain, grad_normed):
    scaled = grad_normed * gain.astype(jnp.float32)
    gain_grad = jnp.sum(grad_normed * vector * scale, axis=(0, 1))
    grad_vector = scale * scaled - vector * (scale * scale * scale) * jnp.mean(
        vector * scaled, -1, keepdims=True
    )
    return (gain_grad, grad_vector)


def score_block(query_heads, key_heads, lengths):
    slot_count = query_heads.shape[1]
    scores = jnp.einsum(
        "rqkgh,rpkh->rkgqp", query_heads, key_heads, preferred_element_type=jnp.float32
    ) * HD ** (-0.5)
    allowed = allowed_keys(lengths, slot_count)
    return jnp.where(allowed[:, None, None], scores, masked_score)


def forward_layer(weights, input_rows, lengths):
    gain_one, qkv_w, output_weight, gain_two, gate_up_w, down_w = weights
    row_count, slot_count, width = input_rows.shape
    groups = H // KVH
    cosines, sine_table = rope_tables(slot_count, HD)
    scale_one = norm_scale(input_rows)
    normed_one = (input_rows * scale_one * gain_one.astype(jnp.float32)).astype(jnp.bfloat16)
    qkv_all = jnp.einsum("rsd,de->rse", normed_one, qkv_w, preferred_element_type=jnp.float32)
    query_heads = rotate(
        qkv_all[..., : H * HD].reshape(row_count, slot_count, H, HD), cosines, sine_table
    )
    query_heads = query_heads.astype(jnp.bfloat16).reshape(row_count, slot_count, KVH, groups, HD)
    key_heads = rotate(
        qkv_all[..., H * HD : (H + KVH) * HD].reshape(row_count, slot_count, KVH, HD),
        cosines,
        sine_table,
    )
    key_heads = key_heads.astype(jnp.bfloat16)
    value_heads = (
        qkv_all[..., (H + KVH) * HD :].reshape(row_count, slot_count, KVH, HD).astype(jnp.bfloat16)
    )
    scores = score_block(query_heads, key_heads, lengths)
    row_max = jnp.max(scores, -1, keepdims=True)
    log_total = row_max + jnp.log(jnp.sum(jnp.exp(scores - row_max), -1, keepdims=True))
    prob_low = jnp.exp(scores - log_total).astype(jnp.bfloat16)
    attention_result = jnp.einsum(
        "rkgqp,rpkh->rqkgh", prob_low, value_heads, preferred_element_type=jnp.float32
    )
    attention_result = attention_result.astype(jnp.bfloat16).reshape(row_count, slot_count, H * HD)
    after_attention = input_rows + jnp.einsum(
        "vao,oj->vaj", attention_result, output_weight, preferred_element_type=jnp.float32
    )
    scale_two = norm_scale(after_attention)
    normed_two = (after_attention * scale_two * gain_two.astype(jnp.float32)).astype(jnp.bfloat16)
    gated = jnp.einsum("rsd,de->rse", normed_two, gate_up_w, preferred_element_type=jnp.float32)
    hidden = (jax.nn.silu(gated[..., :FF]) * gated[..., FF:]).astype(jnp.bfloat16)
    result = after_attention + jnp.einsum(
        "rsf,fd->rsd", hidden, down_w, preferred_element_type=jnp.float32
    )
    result = result * padding(lengths, slot_count)
    kept_state = (
        input_rows,
        scale_one,
        normed_one,
        query_heads,
        key_heads,
        value_heads,
        log_total,
        attention_result,
        after_attention,
        scale_two,
        normed_two,
        gated,
        hidden,
        lengths,
    )
    return (result, kept_state)


def backward_layer(weights, kept_state, grad_out):
    gain_one, qkv_w, output_weight, gain_two, gate_up_w, down_w = weights
    (
        input_rows,
        scale_one,
        normed_one,
        query_heads,
        key_heads,
        value_heads,
        log_total,
        attention_result,
        after_attention,
        scale_two,
        normed_two,
        gated,
        hidden,
        lengths,
    ) = kept_state
    row_count, slot_count, width = input_rows.shape
    groups = H // KVH
    score_scale = HD ** (-0.5)
    cosines, sine_table = rope_tables(slot_count, HD)
    grad_masked = grad_out * padding(lengths, slot_count)
    grad_low = grad_masked.astype(jnp.bfloat16)
    grad_hidden = jnp.einsum("rsd,fd->rsf", grad_low, down_w, preferred_element_type=jnp.float32)
    gate_part = gated[..., :FF]
    up_part = gated[..., FF:]
    sigmoid_gate = jax.nn.sigmoid(gate_part)
    grad_gate = grad_hidden * up_part * sigmoid_gate * (1.0 + gate_part * (1.0 - sigmoid_gate))
    grad_up = grad_hidden * (gate_part * sigmoid_gate)
    grad_gated = jnp.concatenate([grad_gate, grad_up], -1).astype(jnp.bfloat16)
    grad_normed_two = jnp.einsum(
        "rse,de->rsd", grad_gated, gate_up_w, preferred_element_type=jnp.float32
    )
    ffn_gain_part, grad_norm_two = norm_back(after_attention, scale_two, gain_two, grad_normed_two)
    grad_after = grad_masked + grad_norm_two
    gradient_after_lowered = grad_after.astype(jnp.bfloat16)
    attention_gradient = jnp.einsum(
        "vol,el->voe", gradient_after_lowered, output_weight, preferred_element_type=jnp.float32
    )
    attention_gradient = attention_gradient.astype(jnp.bfloat16).reshape(
        row_count, slot_count, KVH, groups, HD
    )
    scores = score_block(query_heads, key_heads, lengths)
    prob_full = jnp.exp(scores - log_total)
    prob_low = prob_full.astype(jnp.bfloat16)
    grad_values = jnp.einsum(
        "rkgqp,rqkgh->rpkh", prob_low, attention_gradient, preferred_element_type=jnp.float32
    )
    grad_probs = jnp.einsum(
        "rqkgh,rpkh->rkgqp", attention_gradient, value_heads, preferred_element_type=jnp.float32
    )
    row_dot = jnp.sum(prob_full * grad_probs, -1, keepdims=True)
    grad_scores = (prob_full * (grad_probs - row_dot)).astype(jnp.bfloat16)
    grad_query = (
        jnp.einsum("rkgqp,rpkh->rqkgh", grad_scores, key_heads, preferred_element_type=jnp.float32)
        * score_scale
    )
    grad_query = rotate(grad_query.reshape(row_count, slot_count, H, HD), cosines, -sine_table)
    grad_keys = (
        jnp.einsum(
            "rkgqp,rqkgh->rpkh", grad_scores, query_heads, preferred_element_type=jnp.float32
        )
        * score_scale
    )
    grad_keys = rotate(grad_keys, cosines, -sine_table)
    grad_qkv = jnp.concatenate(
        [
            grad_query.reshape(row_count, slot_count, H * HD),
            grad_keys.reshape(row_count, slot_count, KVH * HD),
            grad_values.reshape(row_count, slot_count, KVH * HD),
        ],
        -1,
    ).astype(jnp.bfloat16)
    grad_normed_one = jnp.einsum("rse,de->rsd", grad_qkv, qkv_w, preferred_element_type=jnp.float32)
    attn_gain_part, grad_norm_one = norm_back(input_rows, scale_one, gain_one, grad_normed_one)
    grad_inputs = grad_after + grad_norm_one
    return (
        grad_inputs,
        (attn_gain_part, ffn_gain_part, grad_low, grad_gated, gradient_after_lowered, grad_qkv),
    )


def weight_grads(kept_state, operands):
    (
        input_rows,
        scale_one,
        normed_one,
        query_heads,
        key_heads,
        value_heads,
        log_total,
        attention_result,
        after_attention,
        scale_two,
        normed_two,
        gated,
        hidden,
        lengths,
    ) = kept_state
    attn_gain_part, ffn_gain_part, grad_low, grad_gated, gradient_after_lowered, grad_qkv = operands
    down_part = jnp.einsum("rsf,rsd->fd", hidden, grad_low, preferred_element_type=jnp.float32)
    gate_up_part = jnp.einsum(
        "rsd,rse->de", normed_two, grad_gated, preferred_element_type=jnp.float32
    )
    out_part = jnp.einsum(
        "jvl,jvc->lc", attention_result, gradient_after_lowered, preferred_element_type=jnp.float32
    )
    qkv_part = jnp.einsum("rsd,rse->de", normed_one, grad_qkv, preferred_element_type=jnp.float32)
    return (attn_gain_part, qkv_part, out_part, ffn_gain_part, gate_up_part, down_part)


def select_rows(array, index, count):
    index = min(max(index, 0), MICRO - 1)
    return array[index * count : (index + 1) * count]


def body(
    inputs_x, cotangent, lengths, attn_gain, qkv_weight, out_weight, ffn_gain, gate_up, down_weight
):
    is_first = lax.axis_index("section") == 0
    rows_each = inputs_x.shape[0] // MICRO
    weights = tuple(
        (
            whole[0]
            for whole in (
                lax.all_gather(attn_gain, ("group", "dp"), axis=1, tiled=True),
                lax.all_gather(qkv_weight, ("group", "dp"), axis=1, tiled=True),
                lax.all_gather(out_weight, ("group", "dp"), axis=1, tiled=True),
                lax.all_gather(ffn_gain, ("group", "dp"), axis=1, tiled=True),
                lax.all_gather(gate_up, ("group", "dp"), axis=1, tiled=True),
                lax.all_gather(down_weight, ("group", "dp"), axis=1, tiled=True),
            )
        )
    )
    recv_act = jnp.zeros((rows_each,) + inputs_x.shape[1:], jnp.bfloat16)
    recv_grad = jnp.zeros((rows_each,) + inputs_x.shape[1:], jnp.bfloat16)
    tick_out = []
    tick_dx = []
    tick_sent = []
    tick_ops = []
    kept_list = []
    for tick_num in range(MICRO + 2):
        forward_ok = jnp.where(is_first, tick_num < MICRO, 1 <= tick_num <= MICRO)
        layer_in = jnp.where(
            is_first,
            select_rows(inputs_x, tick_num, rows_each).astype(jnp.float32),
            recv_act.astype(jnp.float32),
        )
        layer_lens = jnp.where(
            is_first,
            select_rows(lengths, tick_num, rows_each),
            select_rows(lengths, tick_num - 1, rows_each),
        )

        def run_forward(operand):
            return forward_layer(weights, operand[0], operand[1])

        def skip_forward(operand):
            return jax.tree.map(jnp.zeros_like, run_forward(operand))

        result, kept_state = lax.cond(forward_ok, run_forward, skip_forward, (layer_in, layer_lens))
        sent_act = result.astype(jnp.bfloat16)
        tick_out.append(sent_act)
        kept_list.append(kept_state)
        recv_next = passed_along(sent_act, "section", 1)
        backward_ok = jnp.where(is_first, 2 <= tick_num <= MICRO + 1, 1 <= tick_num <= MICRO)
        older = kept_list[tick_num - 2] if tick_num >= 2 else kept_state
        used_state = jax.tree.map(
            lambda early, late: jnp.where(is_first, early, late), older, kept_state
        )
        grad_in = jnp.where(
            is_first,
            recv_grad.astype(jnp.float32),
            select_rows(cotangent, tick_num - 1, rows_each).astype(jnp.float32),
        )

        def run_backward(operand):
            return backward_layer(weights, operand[0], operand[1])

        def skip_backward(operand):
            return jax.tree.map(jnp.zeros_like, run_backward(operand))

        grad_x, operands = lax.cond(backward_ok, run_backward, skip_backward, (used_state, grad_in))
        sent_grad = grad_x.astype(jnp.bfloat16)
        tick_dx.append(grad_x)
        tick_sent.append(sent_grad)
        tick_ops.append(operands)
        recv_grad = passed_along(sent_grad, "section", -1)
        recv_act = recv_next
    section_out = jnp.concatenate(
        [jnp.where(is_first, tick_out[index], tick_out[index + 1]) for index in range(MICRO)], 0
    )[None]
    input_grads = jnp.concatenate(
        [
            jnp.where(is_first, tick_dx[index + 2], tick_sent[index + 1].astype(jnp.float32))
            for index in range(MICRO)
        ],
        0,
    )[None]

    def pick(early, late):
        return jnp.where(is_first, early, late)

    micro_states = [
        jax.tree.map(pick, kept_list[index], kept_list[index + 1]) for index in range(MICRO)
    ]
    micro_ops = [
        jax.tree.map(pick, tick_ops[index + 2], tick_ops[index + 1]) for index in range(MICRO)
    ]
    joined_state = jax.tree.map(lambda *many: jnp.concatenate(many, 0), *micro_states)
    gain_sums = (sum((ops[0] for ops in micro_ops)), sum((ops[1] for ops in micro_ops)))
    joined_ops = tuple(
        (jnp.concatenate([ops[slot] for ops in micro_ops], 0) for slot in range(2, 6))
    )
    totals = weight_grads(joined_state, gain_sums + joined_ops)
    pieces = (
        lax.psum_scatter(totals[0], ("group", "dp"), scatter_dimension=0, tiled=True),
        lax.psum_scatter(totals[1], ("group", "dp"), scatter_dimension=0, tiled=True),
        lax.psum_scatter(totals[2], ("group", "dp"), scatter_dimension=0, tiled=True),
        lax.psum_scatter(totals[3], ("group", "dp"), scatter_dimension=0, tiled=True),
        lax.psum_scatter(totals[4], ("group", "dp"), scatter_dimension=0, tiled=True),
        lax.psum_scatter(totals[5], ("group", "dp"), scatter_dimension=0, tiled=True),
    )
    reduced = (
        lax.all_gather(pieces[0].astype(jnp.bfloat16), "dp", axis=0, tiled=True).astype(
            jnp.float32
        ),
        lax.all_gather(pieces[1].astype(jnp.bfloat16), "dp", axis=0, tiled=True).astype(
            jnp.float32
        ),
        lax.all_gather(pieces[2].astype(jnp.bfloat16), "dp", axis=0, tiled=True).astype(
            jnp.float32
        ),
        lax.all_gather(pieces[3].astype(jnp.bfloat16), "dp", axis=0, tiled=True).astype(
            jnp.float32
        ),
        lax.all_gather(pieces[4].astype(jnp.bfloat16), "dp", axis=0, tiled=True).astype(
            jnp.float32
        ),
        lax.all_gather(pieces[5].astype(jnp.bfloat16), "dp", axis=0, tiled=True).astype(
            jnp.float32
        ),
    )
    return (section_out, input_grads) + tuple((shard_sum[None] for shard_sum in reduced))


def solution(mesh):
    placed = (
        P(("group", "dp"), None, None),
        P(("group", "dp"), None, None),
        P(("group", "dp")),
        P("section", ("group", "dp")),
        P("section", ("group", "dp"), None),
        P("section", ("group", "dp"), None),
        P("section", ("group", "dp")),
        P("section", ("group", "dp"), None),
        P("section", ("group", "dp"), None),
    )
    return jax.shard_map(
        body,
        mesh=mesh,
        in_specs=placed,
        out_specs=(
            P("section", ("group", "dp"), None, None),
            P("section", ("group", "dp"), None, None),
            P("section", "group"),
            P("section", "group", None),
            P("section", "group", None),
            P("section", "group"),
            P("section", "group", None),
            P("section", "group", None),
        ),
        check_vma=False,
    )
```

profile of v0, /device:TPU:0, one launch (start us, length us, event | category | flops | bytes accessed | tf_op | source)
XLA Modules:
  0.0 1872.6 jit_solution(16831568043485802141)
XLA Ops:
  15.8 36.3 %all-reduce.7 = (bf16[1536]{0:T(1024)(128)(2,1)S(1)}, bf16[1536]{0:T(1024)(128)(2,1)S(1)}) all-reduce(bf16[1536]{0:T(1024)(128)(2,1)S(1)} %dynamic-update-slice, bf16[1536]{0:T(1024)(128)(2,1)S(1)} %dynamic-update-slice.1), channel_id=1, replica_groups=mesh['section'=2,'group'=4,'dp'=4] {'group','dp'}, use_global_device_ids=true, to_apply=%add | all-reduce | flops 3072 | bytes 12288 | tf_op jit(solution)/shard_map/squeeze | solution.py:262
  53.8 12.7 all-gather.11.cloned.1.call-done
  66.5 82.6 %all-gather.9.cloned.1.call-done = bf16[1,1536,3072]{2,1,0:T(8,128)(2,1)} async-done(((bf16[1,96,3072]{2,1,0:T(8,128)(2,1)}), bf16[1,1536,3072]{2,1,0:T(8,128)(2,1)}) %all-gather.9.cloned.1.call-update) | async-done | bytes 9437200 | tf_op jit(solution)/shard_map/all_gather | solution.py:265
  149.1 101.2 %all-gather.15.cloned.1.call-done = bf16[1,4096,1536]{2,1,0:T(8,128)(2,1)} async-done(((bf16[1,256,1536]{2,1,0:T(8,128)(2,1)}), bf16[1,4096,1536]{2,1,0:T(8,128)(2,1)}) %all-gather.15.cloned.1.call-update) | async-done | bytes 12582928 | tf_op jit(solution)/shard_map/all_gather | solution.py:269
  250.3 128.2 %all-gather.13.cloned.1.call-done = bf16[1,1536,8192]{2,1,0:T(8,128)(2,1)} async-done(((bf16[1,96,8192]{2,1,0:T(8,128)(2,1)}), bf16[1,1536,8192]{2,1,0:T(8,128)(2,1)}) %all-gather.13.cloned.1.call-update) | async-done | bytes 25165840 | tf_op jit(solution)/shard_map/all_gather | solution.py:268
  379.5 42.0 %conditional.4 = (f32[1,128,1536]{2,1,0:T(8,128)}, f32[1,128,1]{1,2,0:T(1,128)S(1)}, bf16[1,128,1536]{2,1,0:T(8,128)(2,1)S(1)}, bf16[1,128,8,2,96]{1,4,3,2,0:T(8...) conditional(s32[]{:T(128)} %convert_element_type.561, () %tuple.66, ...), branch_computations={%region_0.1_spmd, %region_1.6_spmd} | conditional | flops 6756146688 | bytes 134657088 | solution.py:299
  398.2 13.8 convolution_bitcast_fusion
  421.6 16.3 collective-permute-start
  455.2 10.5 convolution_bitcast_fusion.19
  500.8 30.8 %collective-permute-done.3 = bf16[1,128,1536]{2,1,0:T(8,128)(2,1)} collective-permute-done((bf16[1,128,1536]{2,1,0:T(8,128)(2,1)}, bf16[1,128,1536]{2,1,0:T(8,128)(2,1)}, u32[]{:S(2)}, u32[]{:S(2)}) %collective-permute-start.3) | collective-permute-done | bytes 393248 | tf_op jit(solution)/shard_map/ppermute | solution.py:21
  533.6 10.5 fusion.165
  544.1 14.1 fusion.167
  584.2 51.2 %collective-permute-done.4 = bf16[1,128,1536]{2,1,0:T(8,128)(2,1)S(1)} collective-permute-done((bf16[1,128,1536]{2,1,0:T(8,128)(2,1)S(1)}, bf16[1,128,1536]{2,1,0:T(8,128)(2,1)S(1)}, u32[]{:S(2)}, u32[]{:S(2)}) %collective-permute-start.4) | collective-permute-done | bytes 393248 | tf_op jit(solution)/shard_map/ppermute | solution.py:21
  637.4 57.3 %conditional.7 = (f32[1,128,1536]{2,1,0:T(8,128)}, f32[1536]{0:T(1024)S(1)}, f32[1536]{0:T(1024)S(1)}, bf16[1,128,1536]{2,1,0:T(8,128)(2,1)}, bf16[1,128,8192]{2...) conditional(s32[]{:T(128)} %convert_element_type.561, () %tuple.72, ...), branch_computations={%region_26.27_spmd, %region_27.33_spmd} | conditional | flops 6928741376 | bytes 210511392 | solution.py:321
  644.0 11.6 fusion.96
  655.6 14.7 fusion.115
  717.7 11.0 convolution_bitcast_fusion.17
  734.6 21.3 %convolution_bitcast_fusion.16 = f32[1536,8192]{1,0:T(8,128)} fusion(bf16[1,128,8192]{2,1,0:T(8,128)(2,1)} %get-tuple-element.736, bf16[1,128,8192]{2,1,0:T(8,128)(2,1)S(1)} %get-tuple-element.735, bf16[1,128,1536]{2,1,0:T(8,128)(2,1)S(1)} %broadcast_select_fusion.15, bf16[1,128,1536]{2,1,0:T(8,128)(2,1)S(1)} %copy-done.63), kind=kOutput, calls=%fused_computation.288 | convolution fusion | flops 6444941312 | bytes 55312384 | tf_op jit(solution)/shard_map/rsd,rse->de/dot_general | solution.py:240
  756.0 56.8 %reduce-scatter.7.cloned.1.call-done = f32[96,1536]{1,0:T(8,128)} async-done(((f32[1536,1536]{1,0:T(8,128)}), f32[96,1536]{1,0:T(8,128)}) %reduce-scatter.7.cloned.1.call-update) | async-done | bytes 589840 | tf_op jit(solution)/shard_map/reduce_scatter | solution.py:357
  814.7 197.2 %reduce-scatter.5.cloned.1.call-done = f32[96,3072]{1,0:T(8,128)} async-done(((f32[1536,3072]{1,0:T(8,128)}), f32[96,3072]{1,0:T(8,128)}) %reduce-scatter.5.cloned.1.call-update) | async-done | bytes 1179664 | tf_op jit(solution)/shard_map/reduce_scatter | solution.py:356
  1014.1 245.5 %reduce-scatter.11.cloned.1.call-done = f32[256,1536]{1,0:T(8,128)} async-done(((f32[4096,1536]{1,0:T(8,128)}), f32[256,1536]{1,0:T(8,128)}) %reduce-scatter.11.cloned.1.call-update) | async-done | bytes 1572880 | tf_op jit(solution)/shard_map/reduce_scatter | solution.py:360
  1262.0 469.4 %reduce-scatter.9.cloned.1.call-done = f32[96,8192]{1,0:T(8,128)} async-done(((f32[1536,8192]{1,0:T(8,128)}), f32[96,8192]{1,0:T(8,128)}) %reduce-scatter.9.cloned.1.call-update) | async-done | bytes 3145744 | tf_op jit(solution)/shard_map/reduce_scatter | solution.py:359
  1737.6 60.6 %all-reduce.6 = (bf16[1536]{0:T(1024)(128)(2,1)S(1)}, bf16[1536]{0:T(1024)(128)(2,1)S(1)}) all-reduce(f32[1536]{0:T(1024)S(1)} %get-tuple-element.778, f32[1536]{0:T(1024)S(1)} %get-tuple-element.777), channel_id=2, replica_groups=mesh['section'=2,'group'=4,'dp'=4] {'group','dp'}, use_global_device_ids=true, to_apply=%region_34.35.clone | all-reduce | flops 3072 | bytes 18432
  1822.1 34.3 %all-gather.21.cloned.1.call-done = bf16[384,8192]{1,0:T(8,128)(2,1)} async-done(((bf16[96,8192]{1,0:T(8,128)(2,1)}), bf16[384,8192]{1,0:T(8,128)(2,1)}) %all-gather.21.cloned.1.call-update) | async-done | bytes 6291472 | tf_op jit(solution)/shard_map/all_gather | solution.py:375
  (476 shorter events, 237.1 us)
Async XLA Ops:
  7.2 59.3 %all-gather.11.cloned.1.call-start = ((), (), s32[]{:S(2)}) async-start(), calls=%async_computation.5 | async-start | bytes 5013504 | tf_op jit(solution)/shard_map/all_gather | solution.py:266
  8.0 141.1 %all-gather.9.cloned.1.call-start = ((), (), s32[]{:S(2)}) async-start(), calls=%async_computation.4 | async-start | bytes 10027008 | tf_op jit(solution)/shard_map/all_gather | solution.py:265
  8.7 241.6 %all-gather.15.cloned.1.call-start = ((), (), s32[]{:S(2)}) async-start(), calls=%async_computation.7 | async-start | bytes 13369344 | tf_op jit(solution)/shard_map/all_gather | solution.py:269
  9.4 369.1 %all-gather.13.cloned.1.call-start = ((), (), s32[]{:S(2)}) async-start(), calls=%async_computation.6 | async-start | bytes 26738688 | tf_op jit(solution)/shard_map/all_gather | solution.py:268
  10.0 802.8 %reduce-scatter.7.cloned.1.call-start = ((), (), s32[]{:S(2)}) async-start(), calls=%async_computation.10 | async-start | bytes 10027008 | tf_op jit(solution)/shard_map/reduce_scatter | solution.py:357
  10.8 463.5 %collective-permute-start.2 = (bf16[1,128,1536]{2,1,0:T(8,128)(2,1)}, bf16[1,128,1536]{2,1,0:T(8,128)(2,1)}, u32[]{:S(2)}, u32[]{:S(2)}) collective-permute-start(bf16[1,128,1536]{2,1,0:T(8,128)(2,1)} %broadcast.1197), channel_id=1, source_target_pairs={{16,0},{17,1},{18,2},{19,3},{20,4},{21,5},{22,6},{23,7},{24,8},{25... | collective-permute-start | bytes 1179656 | tf_op jit(solution)/shard_map/ppermute | solution.py:21
  52.1 385.9 %copy-start.89 = (bf16[1536]{0:T(1024)(128)(2,1)}, bf16[1536]{0:T(1024)(128)(2,1)S(1)}, u32[]{:S(2)}) copy-start(bf16[1536]{0:T(1024)(128)(2,1)S(1)} %get-tuple-element.633) | copy-start | bytes 9220
  52.1 385.9 %copy-start.92 = (bf16[1536]{0:T(1024)(128)(2,1)}, bf16[1536]{0:T(1024)(128)(2,1)S(1)}, u32[]{:S(2)}) copy-start(bf16[1536]{0:T(1024)(128)(2,1)S(1)} %get-tuple-element.634) | copy-start | bytes 9220
  421.6 17.7 collective-permute-start
  472.2 14.4 collective-permute-start.1
  485.3 46.3 %collective-permute-start.3 = (bf16[1,128,1536]{2,1,0:T(8,128)(2,1)}, bf16[1,128,1536]{2,1,0:T(8,128)(2,1)}, u32[]{:S(2)}, u32[]{:S(2)}) collective-permute-start(bf16[1,128,1536]{2,1,0:T(8,128)(2,1)} %get-tuple-element.437), channel_id=1, source_target_pairs={{16,0},{17,1},{18,2},{19,3},{20,4},{21,5},{22,6},{23,7},{24,8},{25... | collective-permute-start | bytes 1179656 | tf_op jit(solution)/shard_map/ppermute | solution.py:21
  580.2 55.2 %collective-permute-start.4 = (bf16[1,128,1536]{2,1,0:T(8,128)(2,1)S(1)}, bf16[1,128,1536]{2,1,0:T(8,128)(2,1)S(1)}, u32[]{:S(2)}, u32[]{:S(2)}) collective-permute-start(bf16[1,128,1536]{2,1,0:T(8,128)(2,1)S(1)} %get-tuple-element.660), channel_id=1, source_target_pairs={{16,0},{17,1},{18,2},{19,3},{20,4},{21,5},{22,6},{23,7},{24,8},{25... | collective-permute-start | bytes 1179656 | tf_op jit(solution)/shard_map/ppermute | solution.py:21
  702.3 309.6 %reduce-scatter.5.cloned.1.call-start = ((), (), s32[]{:S(2)}) async-start(), calls=%async_computation.8 | async-start | bytes 20054016 | tf_op jit(solution)/shard_map/reduce_scatter | solution.py:356
  714.8 544.8 %reduce-scatter.11.cloned.1.call-start = ((), (), s32[]{:S(2)}) async-start(), calls=%async_computation.14 | async-start | bytes 26738688 | tf_op jit(solution)/shard_map/reduce_scatter | solution.py:360
  728.7 1002.7 %reduce-scatter.9.cloned.1.call-start = ((), (), s32[]{:S(2)}) async-start(), calls=%async_computation.12 | async-start | bytes 53477376 | tf_op jit(solution)/shard_map/reduce_scatter | solution.py:359
  755.9 1052.6 %all-gather.19.cloned.1.call-start = ((), (), s32[]{:S(2)}) async-start(), calls=%async_computation.11 | async-start | bytes 1474560 | tf_op jit(solution)/shard_map/all_gather | solution.py:369
  814.6 996.9 %all-gather.17.cloned.1.call-start = ((), (), s32[]{:S(2)}) async-start(), calls=%async_computation.9 | async-start | bytes 2949120 | tf_op jit(solution)/shard_map/all_gather | solution.py:366
  1014.1 801.9 %all-gather.23.cloned.1.call-start = ((), (), s32[]{:S(2)}) async-start(), calls=%async_computation.15 | async-start | bytes 3932160 | tf_op jit(solution)/shard_map/all_gather | solution.py:378
  1262.0 472.7 %copy-start.124 = (u32[32]{0:T(128)S(1)}, u32[32]{0:T(128)}, u32[]{:S(2)}) copy-start(u32[32]{0:T(128)} %constant.288) | copy-start | bytes 388
  1262.0 474.6 %copy-start.65 = (bf16[1,128,1536]{2,1,0:T(8,128)(2,1)S(1)}, bf16[1,128,1536]{2,1,0:T(8,128)(2,1)}, u32[]{:S(2)}) copy-start(bf16[1,128,1536]{2,1,0:T(8,128)(2,1)} %get-tuple-element.775) | copy-start | bytes 1179652
  1262.0 474.6 %copy-start.66 = (bf16[1,128,1536]{2,1,0:T(8,128)(2,1)S(1)}, bf16[1,128,1536]{2,1,0:T(8,128)(2,1)}, u32[]{:S(2)}) copy-start(bf16[1,128,1536]{2,1,0:T(8,128)(2,1)} %get-tuple-element.776) | copy-start | bytes 1179652
  1262.0 594.4 %all-gather.21.cloned.1.call-start = ((), (), s32[]{:S(2)}) async-start(), calls=%async_computation.13 | async-start | bytes 7864320 | tf_op jit(solution)/shard_map/all_gather | solution.py:375
  1734.6 71.4 %copy-start.71 = (bf16[1,128,1536]{2,1,0:T(8,128)(2,1)S(1)}, bf16[1,128,1536]{2,1,0:T(8,128)(2,1)}, u32[]{:S(2)}) copy-start(bf16[1,128,1536]{2,1,0:T(8,128)(2,1)} %copy-done.70) | copy-start | bytes 1179652
  1734.7 72.6 %copy-start.47 = (f32[1,128,1536]{2,1,0:T(8,128)S(1)}, f32[1,128,1536]{2,1,0:T(8,128)}, u32[]{:S(2)}) copy-start(f32[1,128,1536]{2,1,0:T(8,128)} %get-tuple-element.659) | copy-start | bytes 2359300
  (114 other events, 1055.9 us)
Sparse Core Ops, SparseCore 0:
  10.3 56.1 all-gather.10
  68.8 80.2 all-gather.8
  151.4 98.8 all-gather.14
  251.8 126.7 all-gather.12
  702.4 110.3 reduce-scatter.6
  817.3 194.5 reduce-scatter.4
  1016.5 242.9 reduce-scatter.10
  1264.4 466.9 reduce-scatter.8
  1733.6 16.7 all-gather.18
  1752.5 24.3 all-gather.16
  1779.1 28.8 all-gather.22
  1810.1 46.2 all-gather.20
where the time goes:
time: 1880 us; the launch traced here: 1870 us
  waiting for transfers between devices  1410 us (75%)
  matrix products  174 us (9%)
  blocking collectives  103 us (5%)
  other arithmetic  94.2 us (5%)
  local copies, waits for them, and re-layouts  45.1 us (2%)
  starting transfers between devices  22.7 us (1%)
  between operations  19 us (1%)
    reduce_scatter x1, waiting for transfers between devices, body(): lax.psum_scatter(totals[4], ('group', 'dp'), scatter_dimension=0, tiled=T...  469 us
    reduce_scatter x1, waiting for transfers between devices, body(): lax.psum_scatter(totals[5], ('group', 'dp'), scatter_dimension=0, tiled=T...  245 us
    reduce_scatter x1, waiting for transfers between devices, body(): lax.psum_scatter(totals[1], ('group', 'dp'), scatter_dimension=0, tiled=T...  197 us
    all_gather x1, waiting for transfers between devices, body(): lax.all_gather(gate_up, ('group', 'dp'), axis=1, tiled=True)  128 us
    all_gather x1, waiting for transfers between devices, body(): lax.all_gather(down_weight, ('group', 'dp'), axis=1, tiled=True)  101 us
    all_gather x1, waiting for transfers between devices, body(): lax.all_gather(qkv_weight, ('group', 'dp'), axis=1, tiled=True)  82.6 us
    ppermute x5, waiting for transfers between devices, passed_along(): return lax.ppermute(value, axis, pairs)  82 us
    unnamed x2, blocking collectives  66.8 us
  transfers between devices with their start and end apart: 17, of which 11 were waited for; matrix products, arithmetic and copies ran while one was open for 10% of the time, Pallas kernels for 0%

commit v1 on v0

--- a/solution.py
+++ b/solution.py
@@ -7,7 +7,6 @@
 KVH = 8
 HD = 96
 FF = 4096
-MICRO = 2
 
 
 norm_eps = 1e-05
@@ -247,16 +246,10 @@
     return (attn_gain_part, qkv_part, out_part, ffn_gain_part, gate_up_part, down_part)
 
 
-def select_rows(array, index, count):
-    index = min(max(index, 0), MICRO - 1)
-    return array[index * count : (index + 1) * count]
-
-
 def body(
     inputs_x, cotangent, lengths, attn_gain, qkv_weight, out_weight, ffn_gain, gate_up, down_weight
 ):
     is_first = lax.axis_index("section") == 0
-    rows_each = inputs_x.shape[0] // MICRO
     weights = tuple(
         (
             whole[0]
@@ -270,115 +263,27 @@
             )
         )
     )
-    recv_act = jnp.zeros((rows_each,) + inputs_x.shape[1:], jnp.bfloat16)
-    recv_grad = jnp.zeros((rows_each,) + inputs_x.shape[1:], jnp.bfloat16)
-    tick_out = []
-    tick_dx = []
-    tick_sent = []
-    tick_ops = []
-    kept_list = []
-    for tick_num in range(MICRO + 2):
-        forward_ok = jnp.where(is_first, tick_num < MICRO, 1 <= tick_num <= MICRO)
-        layer_in = jnp.where(
-            is_first,
-            select_rows(inputs_x, tick_num, rows_each).astype(jnp.float32),
-            recv_act.astype(jnp.float32),
+    inputs_f = inputs_x.astype(jnp.float32)
+    cotangent_f = cotangent.astype(jnp.float32)
+    first_out, _ = forward_layer(weights, inputs_f, lengths)
+    recv_act = passed_along(first_out.astype(jnp.bfloat16), "section", 1)
+    layer_in = jnp.where(is_first, inputs_f, recv_act.astype(jnp.float32))
+    result, kept_state = forward_layer(weights, layer_in, lengths)
+    section_out = result.astype(jnp.bfloat16)[None]
+    second_dx, _ = backward_layer(weights, kept_state, cotangent_f)
+    recv_grad = passed_along(second_dx.astype(jnp.bfloat16), "section", -1)
+    grad_in = jnp.where(is_first, recv_grad.astype(jnp.float32), cotangent_f)
+    grad_x, operands = backward_layer(weights, kept_state, grad_in)
+    input_grads = jnp.where(
+        is_first, grad_x, grad_x.astype(jnp.bfloat16).astype(jnp.float32)
+    )[None]
+    totals = weight_grads(kept_state, operands)
+    reduced = []
+    for total in totals:
+        piece = lax.psum_scatter(
+            total.astype(jnp.bfloat16), ("group", "dp"), scatter_dimension=0, tiled=True
         )
-        layer_lens = jnp.where(
-            is_first,
-            select_rows(lengths, tick_num, rows_each),
-            select_rows(lengths, tick_num - 1, rows_each),
-        )
-
-        def run_forward(operand):
-            return forward_layer(weights, operand[0], operand[1])
-
-        def skip_forward(operand):
-            return jax.tree.map(jnp.zeros_like, run_forward(operand))
-
-        result, kept_state = lax.cond(forward_ok, run_forward, skip_forward, (layer_in, layer_lens))
-        sent_act = result.astype(jnp.bfloat16)
-        tick_out.append(sent_act)
-        kept_list.append(kept_state)
-        recv_next = passed_along(sent_act, "section", 1)
-        backward_ok = jnp.where(is_first, 2 <= tick_num <= MICRO + 1, 1 <= tick_num <= MICRO)
-        older = kept_list[tick_num - 2] if tick_num >= 2 else kept_state
-        used_state = jax.tree.map(
-            lambda early, late: jnp.where(is_first, early, late), older, kept_state
-        )
-        grad_in = jnp.where(
-            is_first,
-            recv_grad.astype(jnp.float32),
-            select_rows(cotangent, tick_num - 1, rows_each).astype(jnp.float32),
-        )
-
-        def run_backward(operand):
-            return backward_layer(weights, operand[0], operand[1])
-
-        def skip_backward(operand):
-            return jax.tree.map(jnp.zeros_like, run_backward(operand))
-
-        grad_x, operands = lax.cond(backward_ok, run_backward, skip_backward, (used_state, grad_in))
-        sent_grad = grad_x.astype(jnp.bfloat16)
-        tick_dx.append(grad_x)
-        tick_sent.append(sent_grad)
-        tick_ops.append(operands)
-        recv_grad = passed_along(sent_grad, "section", -1)
-        recv_act = recv_next
-    section_out = jnp.concatenate(
-        [jnp.where(is_first, tick_out[index], tick_out[index + 1]) for index in range(MICRO)], 0
-    )[None]
-    input_grads = jnp.concatenate(
-        [
-            jnp.where(is_first, tick_dx[index + 2], tick_sent[index + 1].astype(jnp.float32))
-            for index in range(MICRO)
-        ],
-        0,
-    )[None]
-
-    def pick(early, late):
-        return jnp.where(is_first, early, late)
-
-    micro_states = [
-        jax.tree.map(pick, kept_list[index], kept_list[index + 1]) for index in range(MICRO)
-    ]
-    micro_ops = [
-        jax.tree.map(pick, tick_ops[index + 2], tick_ops[index + 1]) for index in range(MICRO)
-    ]
-    joined_state = jax.tree.map(lambda *many: jnp.concatenate(many, 0), *micro_states)
-    gain_sums = (sum((ops[0] for ops in micro_ops)), sum((ops[1] for ops in micro_ops)))
-    joined_ops = tuple(
-        (jnp.concatenate([ops[slot] for ops in micro_ops], 0) for slot in range(2, 6))
-    )
-    totals = weight_grads(joined_state, gain_sums + joined_ops)
-    pieces = (
-        lax.psum_scatter(totals[0], ("group", "dp"), scatter_dimension=0, tiled=True),
-        lax.psum_scatter(totals[1], ("group", "dp"), scatter_dimension=0, tiled=True),
-        lax.psum_scatter(totals[2], ("group", "dp"), scatter_dimension=0, tiled=True),
-        lax.psum_scatter(totals[3], ("group", "dp"), scatter_dimension=0, tiled=True),
-        lax.psum_scatter(totals[4], ("group", "dp"), scatter_dimension=0, tiled=True),
-        lax.psum_scatter(totals[5], ("group", "dp"), scatter_dimension=0, tiled=True),
-    )
-    reduced = (
-        lax.all_gather(pieces[0].astype(jnp.bfloat16), "dp", axis=0, tiled=True).astype(
-            jnp.float32
-        ),
-        lax.all_gather(pieces[1].astype(jnp.bfloat16), "dp", axis=0, tiled=True).astype(
-            jnp.float32
-        ),
-        lax.all_gather(pieces[2].astype(jnp.bfloat16), "dp", axis=0, tiled=True).astype(
-            jnp.float32
-        ),
-        lax.all_gather(pieces[3].astype(jnp.bfloat16), "dp", axis=0, tiled=True).astype(
-            jnp.float32
-        ),
-        lax.all_gather(pieces[4].astype(jnp.bfloat16), "dp", axis=0, tiled=True).astype(
-            jnp.float32
-        ),
-        lax.all_gather(pieces[5].astype(jnp.bfloat16), "dp", axis=0, tiled=True).astype(
-            jnp.float32
-        ),
-    )
+        reduced.append(lax.all_gather(piece, "dp", axis=0, tiled=True).astype(jnp.float32))
     return (section_out, input_grads) + tuple((shard_sum[None] for shard_sum in reduced))
 
 

time: 1880 us -> 1290 us (0.69)
  waiting for transfers between devices: 1410 us -> 905 us
  other arithmetic: 94.2 us -> 42.5 us
  blocking collectives: 103 us -> 74.7 us
  matrix products: 174 us -> 199 us
    reduce_scatter x4, waiting for transfers between devices: 969 us -> 520 us  [body(): lax.psum_scatter(total.astype(jnp.bfloat16), ('group', 'dp'), scatter_dim...]
    ppermute x5 -> x2, waiting for transfers between devices: 82 us -> 36.7 us  [passed_along(): return lax.ppermute(value, axis, pairs)]
    all_gather x1, waiting for transfers between devices: 82.6 us -> 46.1 us  [body(): lax.all_gather(qkv_weight, ('group', 'dp'), axis=1, tiled=True)]
    squeeze x1 -> x0, blocking collectives: 36.3 us -> none  [body(): whole[0]]
    select_n x17 -> x0, other arithmetic: 29.9 us -> none  [the longest x13 21.7 us: pick(): return jnp.where(is_first, early, late)]
    all_gather x1, waiting for transfers between devices: 12.7 us -> 39.5 us  [body(): lax.all_gather(out_weight, ('group', 'dp'), axis=1, tiled=True)]
    convert_element_type x16 -> x4, other arithmetic: 23.3 us -> 2.48 us  [the longest x2 1.21 us: backward_layer(): grad_scores = (prob_full * (grad_probs - row_dot)).astype(jnp.bfloat16)]
    unnamed x2 -> x3, blocking collectives: 66.8 us -> 74.7 us
  transfers between devices with their start and end apart: 17 -> 14, of which waited for: 11 -> 12; matrix products, arithmetic and copies ran while one was open for 10% -> 9% of each run, Pallas kernels for 0% -> 0%
where the time goes in v1:
time: 1290 us; the launch traced here: 1280 us
  waiting for transfers between devices  905 us (70%)
  matrix products  199 us (15%)
  blocking collectives  74.7 us (6%)
  other arithmetic  42.5 us (3%)
  local copies, waits for them, and re-layouts  35.1 us (3%)
  between operations  17.5 us (1%)
    reduce_scatter x4, waiting for transfers between devices, body(): lax.psum_scatter(total.astype(jnp.bfloat16), ('group', 'dp'), scatter_dim...  520 us
    all_gather x1, waiting for transfers between devices, body(): lax.all_gather(gate_up, ('group', 'dp'), axis=1, tiled=True)  125 us
    all_gather x1, waiting for transfers between devices, body(): lax.all_gather(down_weight, ('group', 'dp'), axis=1, tiled=True)  89.3 us
    unnamed x3, blocking collectives  74.7 us
    all_gather x1, waiting for transfers between devices, body(): lax.all_gather(qkv_weight, ('group', 'dp'), axis=1, tiled=True)  46.1 us
    all_gather x4, waiting for transfers between devices, body(): lax.all_gather(piece, 'dp', axis=0, tiled=True).astype(jnp.float32)  45.3 us
    all_gather x1, waiting for transfers between devices, body(): lax.all_gather(out_weight, ('group', 'dp'), axis=1, tiled=True)  39.5 us
    dot_general x2, matrix products, backward_layer(): jnp.einsum('rse,de->rsd', grad_gated, gate_up_w, preferred_element_type=j...  38.5 us
  transfers between devices with their start and end apart: 14, of which 12 were waited for; matrix products, arithmetic and copies ran while one was open for 9% of the time, Pallas kernels for 0%

profile of v1, /device:TPU:0, one launch (start us, length us, event | category | flops | bytes accessed | tf_op | source)
XLA Modules:
  0.0 1279.1 jit_solution(10327369385779181732)
XLA Ops:
  11.9 36.3 %all-reduce.7 = (bf16[1536]{0:T(1024)(128)(2,1)S(1)}, bf16[1536]{0:T(1024)(128)(2,1)S(1)}) all-reduce(bf16[1536]{0:T(1024)(128)(2,1)S(1)} %dynamic-update-slice, bf16[1536]{0:T(1024)(128)(2,1)S(1)} %dynamic-update-slice.1), channel_id=1, replica_groups=mesh['section'=2,'group'=4,'dp'=4] {'group','dp'}, use_global_device_ids=true, to_apply=%add | all-reduce | flops 3072 | bytes 12288
  49.0 46.1 %all-gather.9.cloned.1.call-done = bf16[1,1536,3072]{2,1,0:T(8,128)(2,1)} async-done(((bf16[1,96,3072]{2,1,0:T(8,128)(2,1)}), bf16[1,1536,3072]{2,1,0:T(8,128)(2,1)}) %all-gather.9.cloned.1.call-update) | async-done | bytes 9437200 | tf_op jit(solution)/shard_map/all_gather | solution.py:258
  109.4 39.5 %all-gather.11.cloned.1.call-done = bf16[1,1536,1536]{2,1,0:T(8,128)(2,1)} async-done(((bf16[1,96,1536]{2,1,0:T(8,128)(2,1)}), bf16[1,1536,1536]{2,1,0:T(8,128)(2,1)}) %all-gather.11.cloned.1.call-update) | async-done | bytes 4718608 | tf_op jit(solution)/shard_map/all_gather | solution.py:259
  152.8 124.9 %all-gather.13.cloned.1.call-done = bf16[1,1536,8192]{2,1,0:T(8,128)(2,1)} async-done(((bf16[1,96,8192]{2,1,0:T(8,128)(2,1)}), bf16[1,1536,8192]{2,1,0:T(8,128)(2,1)}) %all-gather.13.cloned.1.call-update) | async-done | bytes 25165840 | tf_op jit(solution)/shard_map/all_gather | solution.py:261
  277.7 13.7 %fusion.6 = f32[2,128,8192]{2,1,0:T(8,128)} fusion(bf16[1,1536,8192]{2,1,0:T(8,128)(2,1)} %all-gather.13.cloned.1.call-done, f32[2,128,1536]{2,1,0:T(8,128)S(1)} %get-tuple-element.53, f32[1536]{0:T(1024)S(1)} %convert_element_type.212, f32[2,128]{1,0:T(2,128)S(1)} %add_rsqrt_fusion.2), kind=kOutput, calls=%fused_computation.8 | convolution fusion | flops 6443630592 | bytes 35134464 | tf_op jit(solution)/shard_map/rsd,de->rse/dot_general | solution.py:112
  291.4 89.3 %all-gather.15.cloned.1.call-done = bf16[1,4096,1536]{2,1,0:T(8,128)(2,1)} async-done(((bf16[1,256,1536]{2,1,0:T(8,128)(2,1)}), bf16[1,4096,1536]{2,1,0:T(8,128)(2,1)}) %all-gather.15.cloned.1.call-update) | async-done | bytes 12582928 | tf_op jit(solution)/shard_map/all_gather | solution.py:262
  380.6 11.4 fusion.64
  395.7 17.2 %collective-permute-done = bf16[2,128,1536]{2,1,0:T(8,128)(2,1)S(1)} collective-permute-done((bf16[2,128,1536]{2,1,0:T(8,128)(2,1)}, bf16[2,128,1536]{2,1,0:T(8,128)(2,1)S(1)}, u32[]{:S(2)}, u32[]{:S(2)}) %collective-permute-start) | collective-permute-done | bytes 786464 | tf_op jit(solution)/shard_map/ppermute | solution.py:20
  431.4 14.3 %fusion.4 = f32[2,128,8192]{2,1,0:T(8,128)} fusion(bf16[1,1536,8192]{2,1,0:T(8,128)(2,1)} %all-gather.13.cloned.1.call-done, f32[2,128,1536]{2,1,0:T(8,128)S(1)} %get-tuple-element.57, f32[1536]{0:T(1024)S(1)} %convert_element_type.212, f32[2,128]{1,0:T(2,128)S(1)} %get-tuple-element.42), kind=kOutput, calls=%fused_computation.6 | convolution fusion | flops 6443630592 | bytes 35134464 | tf_op jit(solution)/shard_map/rsd,de->rse/dot_general | solution.py:112
  445.6 10.5 multiply_convert_fusion.3
  456.2 23.8 %multiply_reduce_fusion.5 = (f32[2,128]{1,0:T(2,128)S(1)}, f32[2,128,1536]{2,1,0:T(8,128)}) fusion(f32[2,128,1536]{2,1,0:T(8,128)S(1)} %get-tuple-element.57, f32[1536]{0:T(1024)S(1)} %convert_element_type.212, bf16[1,1536,8192]{2,1,0:T(8,128)(2,1)} %all-gather.13.cloned.1.call-done, bf16[2,128,4096]{2,1,0:T(8,128)(2,1)} %get-tuple-element.21, ...), kind=kOutput, calls=%fused_computation.109 | convolution fusion | flops 6452019200 | bytes 32513024 | tf_op jit(solution)/shard_map/rse,de->rsd/dot_general | solution.py:168
  514.6 19.5 %collective-permute-done.1 = bf16[2,128,1536]{2,1,0:T(8,128)(2,1)S(1)} collective-permute-done((bf16[2,128,1536]{2,1,0:T(8,128)(2,1)S(1)}, bf16[2,128,1536]{2,1,0:T(8,128)(2,1)S(1)}, u32[]{:S(2)}, u32[]{:S(2)}) %collective-permute-start.1) | collective-permute-done | bytes 786464 | tf_op jit(solution)/shard_map/ppermute | solution.py:20
  534.1 11.0 multiply_convert_fusion.1
  545.1 14.7 %multiply_reduce_fusion = (bf16[1536]{0:T(1024)(128)(2,1)}, f32[2,128]{1,0:T(2,128)S(1)}, f32[2,128,1536]{2,1,0:T(8,128)}) fusion(f32[2,128,1536]{2,1,0:T(8,128)S(1)} %copy-done.2, f32[2,128]{1,0:T(2,128)S(1)} %get-tuple-element.42, f32[1536]{0:T(1024)S(1)} %convert_element_type.212, bf16[1,1536,8192]{2,1,0:T(8,128)(2,1)} %all-gather.13.cloned.1.call-done, ...), kind=kOutput, calls=%fused_computation.100 | convolution fusion | flops 6453196800 | bytes 32517120 | tf_op jit(solution)/shard_map/rse,de->rsd/dot_general | solution.py:168
  605.6 14.2 %bitcast_convert_fusion = bf16[1536,8192]{1,0:T(8,128)(2,1)} fusion(bf16[2,128,4096]{2,1,0:T(8,128)(2,1)} %get-tuple-element.19, bf16[2,128,4096]{2,1,0:T(8,128)(2,1)} %copy-done.26, f32[2,128,1536]{2,1,0:T(8,128)S(1)} %copy-done.3, f32[1536]{0:T(1024)S(1)} %convert_element_type.212, f32[2,128]{1,0:T(2,128)S(1)} %get-tuple-element.42), kind=kOutput, calls=%fused_computation | convolution fusion | flops 6464602112 | bytes 30940160 | tf_op jit(solution)/shard_map/rsd,rse->de/dot_general | solution.py:239
  619.9 19.1 %reduce-scatter.7.cloned.1.call-done = bf16[96,1536]{1,0:T(8,128)(2,1)} async-done(((bf16[1536,1536]{1,0:T(8,128)(2,1)}), bf16[96,1536]{1,0:T(8,128)(2,1)}) %reduce-scatter.7.cloned.1.call-update) | async-done | bytes 294928 | tf_op jit(solution)/shard_map/reduce_scatter | solution.py:283
  639.2 114.9 %reduce-scatter.5.cloned.1.call-done = bf16[96,3072]{1,0:T(8,128)(2,1)} async-done(((bf16[1536,3072]{1,0:T(8,128)(2,1)}), bf16[96,3072]{1,0:T(8,128)(2,1)}) %reduce-scatter.5.cloned.1.call-update) | async-done | bytes 589840 | tf_op jit(solution)/shard_map/reduce_scatter | solution.py:283
  754.1 139.1 %reduce-scatter.11.cloned.1.call-done = bf16[256,1536]{1,0:T(8,128)(2,1)} async-done(((bf16[4096,1536]{1,0:T(8,128)(2,1)}), bf16[256,1536]{1,0:T(8,128)(2,1)}) %reduce-scatter.11.cloned.1.call-update) | async-done | bytes 786448 | tf_op jit(solution)/shard_map/reduce_scatter | solution.py:283
  893.3 247.1 %reduce-scatter.9.cloned.1.call-done = bf16[96,8192]{1,0:T(8,128)(2,1)} async-done(((bf16[1536,8192]{1,0:T(8,128)(2,1)}), bf16[96,8192]{1,0:T(8,128)(2,1)}) %reduce-scatter.9.cloned.1.call-update) | async-done | bytes 1572880 | tf_op jit(solution)/shard_map/reduce_scatter | solution.py:283
  1142.3 8.7 multiply_reduce_fusion.1
  1151.0 32.6 %all-reduce.6 = (bf16[1536]{0:T(1024)(128)(2,1)S(1)}, bf16[1536]{0:T(1024)(128)(2,1)S(1)}) all-reduce(bf16[1536]{0:T(1024)(128)(2,1)} %get-tuple-element.10, bf16[1536]{0:T(1024)(128)(2,1)} %get-tuple-element.8), channel_id=2, replica_groups=mesh['section'=2,'group'=4,'dp'=4] {'group','dp'}, use_global_device_ids=true, to_apply=%region_15.16.clone | all-reduce | flops 3072 | bytes 12288
  1195.6 8.9 fusion.73
  1220.4 42.4 %all-gather.21.cloned.1.call-done = bf16[384,8192]{1,0:T(8,128)(2,1)} async-done(((bf16[96,8192]{1,0:T(8,128)(2,1)}), bf16[384,8192]{1,0:T(8,128)(2,1)}) %all-gather.21.cloned.1.call-update) | async-done | bytes 6291472 | tf_op jit(solution)/shard_map/all_gather | solution.py:286
  1262.7 9.1 bitcast_convert_fusion.4
  (243 shorter events, 153.5 us)
Async XLA Ops:
  7.2 41.4 %copy-start.50 = (s32[2]{0:T(128)S(1)}, s32[2]{0:T(128)}, u32[]{:S(2)}) copy-start(s32[2]{0:T(128)} %param.11) | copy-start | bytes 28
  7.2 87.8 %all-gather.9.cloned.1.call-start = ((), (), s32[]{:S(2)}) async-start(), calls=%async_computation.4 | async-start | bytes 10027008 | tf_op jit(solution)/shard_map/all_gather | solution.py:258
  8.0 141.0 %all-gather.11.cloned.1.call-start = ((), (), s32[]{:S(2)}) async-start(), calls=%async_computation.5 | async-start | bytes 5013504 | tf_op jit(solution)/shard_map/all_gather | solution.py:259
  8.7 269.0 %all-gather.13.cloned.1.call-start = ((), (), s32[]{:S(2)}) async-start(), calls=%async_computation.6 | async-start | bytes 26738688 | tf_op jit(solution)/shard_map/all_gather | solution.py:261
  9.4 371.2 %all-gather.15.cloned.1.call-start = ((), (), s32[]{:S(2)}) async-start(), calls=%async_computation.7 | async-start | bytes 13369344 | tf_op jit(solution)/shard_map/all_gather | solution.py:262
  10.0 629.1 %reduce-scatter.7.cloned.1.call-start = ((), (), s32[]{:S(2)}) async-start(), calls=%async_computation.10 | async-start | bytes 5013504 | tf_op jit(solution)/shard_map/reduce_scatter | solution.py:283
  48.3 365.6 %copy-start.34 = (f32[1536]{0:T(1024)}, f32[1536]{0:T(1024)S(1)}, u32[]{:S(2)}) copy-start(f32[1536]{0:T(1024)S(1)} %convert_element_type.211) | copy-start | bytes 18436
  48.7 332.0 %copy-start.37 = (f32[2,128]{1,0:T(2,128)}, f32[2,128]{1,0:T(2,128)S(1)}, u32[]{:S(2)}) copy-start(f32[2,128]{1,0:T(2,128)S(1)} %get-tuple-element.48) | copy-start | bytes 3076
  48.8 59.2 %copy-start.36 = (pred[2,128,128]{1,2,0:T(8,128)(4,1)}, pred[2,128,128]{1,2,0:T(8,128)(4,1)S(1)}, u32[]{:S(2)}) copy-start(pred[2,128,128]{1,2,0:T(8,128)(4,1)S(1)} %broadcast_and_fusion) | copy-start | bytes 98308
  392.0 20.9 %collective-permute-start = (bf16[2,128,1536]{2,1,0:T(8,128)(2,1)}, bf16[2,128,1536]{2,1,0:T(8,128)(2,1)S(1)}, u32[]{:S(2)}, u32[]{:S(2)}) collective-permute-start(bf16[2,128,1536]{2,1,0:T(8,128)(2,1)} %fusion.64), channel_id=1, source_target_pairs={{0,16},{1,17},{2,18},{3,19},{4,20},{5,21},{6,22},{7,23},{8,24},{9,... | collective-permute-start | bytes 2359304 | tf_op jit(solution)/shard_map/ppermute | solution.py:20
  431.3 48.7 %copy-start.1 = (f32[2,128,1536]{2,1,0:T(8,128)}, f32[2,128,1536]{2,1,0:T(8,128)S(1)}, u32[]{:S(2)}) copy-start(f32[2,128,1536]{2,1,0:T(8,128)S(1)} %get-tuple-element.57) | copy-start | bytes 4718596
  431.3 48.7 %copy-start.45 = (f32[2,128]{1,0:T(2,128)}, f32[2,128]{1,0:T(2,128)S(1)}, u32[]{:S(2)}) copy-start(f32[2,128]{1,0:T(2,128)S(1)} %get-tuple-element.41) | copy-start | bytes 3076
  513.3 20.8 %collective-permute-start.1 = (bf16[2,128,1536]{2,1,0:T(8,128)(2,1)S(1)}, bf16[2,128,1536]{2,1,0:T(8,128)(2,1)S(1)}, u32[]{:S(2)}, u32[]{:S(2)}) collective-permute-start(bf16[2,128,1536]{2,1,0:T(8,128)(2,1)S(1)} %add_convert_fusion), channel_id=1, source_target_pairs={{16,0},{17,1},{18,2},{19,3},{20,4},{21,5},{22,6},{23,7},{24,8},{25... | collective-permute-start | bytes 2359304 | tf_op jit(solution)/shard_map/ppermute | solution.py:20
  566.1 187.9 %reduce-scatter.5.cloned.1.call-start = ((), (), s32[]{:S(2)}) async-start(), calls=%async_computation.8 | async-start | bytes 10027008 | tf_op jit(solution)/shard_map/reduce_scatter | solution.py:283
  594.5 298.7 %reduce-scatter.11.cloned.1.call-start = ((), (), s32[]{:S(2)}) async-start(), calls=%async_computation.14 | async-start | bytes 13369344 | tf_op jit(solution)/shard_map/reduce_scatter | solution.py:283
  604.2 536.1 %reduce-scatter.9.cloned.1.call-start = ((), (), s32[]{:S(2)}) async-start(), calls=%async_computation.12 | async-start | bytes 26738688 | tf_op jit(solution)/shard_map/reduce_scatter | solution.py:283
  619.9 520.5 %copy-start.53 = (u32[32]{0:T(128)S(1)}, u32[32]{0:T(128)}, u32[]{:S(2)}) copy-start(u32[32]{0:T(128)} %constant.63) | copy-start | bytes 388
  619.9 522.4 %copy-start.35 = (f32[1536]{0:T(1024)S(1)}, f32[1536]{0:T(1024)}, u32[]{:S(2)}) copy-start(f32[1536]{0:T(1024)} %copy-done.34) | copy-start | bytes 18436
  619.9 522.4 %copy-start.44 = (f32[2,128]{1,0:T(2,128)S(1)}, f32[2,128]{1,0:T(2,128)}, u32[]{:S(2)}) copy-start(f32[2,128]{1,0:T(2,128)} %copy-done.42) | copy-start | bytes 3076
  619.9 584.6 %all-gather.19.cloned.1.call-start = ((), (), s32[]{:S(2)}) async-start(), calls=%async_computation.11 | async-start | bytes 1474560 | tf_op jit(solution)/shard_map/all_gather | solution.py:286
  639.1 568.4 %all-gather.17.cloned.1.call-start = ((), (), s32[]{:S(2)}) async-start(), calls=%async_computation.9 | async-start | bytes 2949120 | tf_op jit(solution)/shard_map/all_gather | solution.py:286
  754.1 460.8 %all-gather.23.cloned.1.call-start = ((), (), s32[]{:S(2)}) async-start(), calls=%async_computation.15 | async-start | bytes 3932160 | tf_op jit(solution)/shard_map/all_gather | solution.py:286
  893.2 369.5 %all-gather.21.cloned.1.call-start = ((), (), s32[]{:S(2)}) async-start(), calls=%async_computation.13 | async-start | bytes 7864320 | tf_op jit(solution)/shard_map/all_gather | solution.py:286
  1142.3 49.4 %copy-start.41 = (f32[2,128]{1,0:T(2,128)S(1)}, f32[2,128]{1,0:T(2,128)}, u32[]{:S(2)}) copy-start(f32[2,128]{1,0:T(2,128)} %get-tuple-element.39) | copy-start | bytes 3076
  (48 other events, 249.8 us)
Sparse Core Ops, SparseCore 0:
  10.3 84.6 all-gather.8
  97.3 51.5 all-gather.10
  150.5 127.1 all-gather.12
  279.8 100.7 all-gather.14
  566.2 72.8 reduce-scatter.6
  643.6 110.4 reduce-scatter.4
  758.7 134.4 reduce-scatter.10
  897.3 242.9 reduce-scatter.8
  1141.9 16.6 all-gather.18
  1160.0 24.7 all-gather.16
  1186.4 28.4 all-gather.22
  1216.3 46.3 all-gather.20

commit v2 on v1

--- a/solution.py
+++ b/solution.py
@@ -1,6 +1,10 @@
+import functools
+
 import jax
 import jax.numpy as jnp
 from jax import lax
+from jax.experimental import pallas as pl
+from jax.experimental.pallas import tpu as pltpu
 from jax.sharding import PartitionSpec as P
 
 H = 16
@@ -217,51 +221,464 @@
     )
 
 
-def weight_grads(kept_state, operands):
-    (
-        input_rows,
-        scale_one,
-        normed_one,
-        query_heads,
-        key_heads,
-        value_heads,
-        log_total,
-        attention_result,
-        after_attention,
-        scale_two,
-        normed_two,
-        gated,
-        hidden,
-        lengths,
-    ) = kept_state
-    attn_gain_part, ffn_gain_part, grad_low, grad_gated, gradient_after_lowered, grad_qkv = operands
-    down_part = jnp.einsum("rsf,rsd->fd", hidden, grad_low, preferred_element_type=jnp.float32)
-    gate_up_part = jnp.einsum(
-        "rsd,rse->de", normed_two, grad_gated, preferred_element_type=jnp.float32
-    )
-    out_part = jnp.einsum(
-        "jvl,jvc->lc", attention_result, gradient_after_lowered, preferred_element_type=jnp.float32
-    )
-    qkv_part = jnp.einsum("rsd,rse->de", normed_one, grad_qkv, preferred_element_type=jnp.float32)
-    return (attn_gain_part, qkv_part, out_part, ffn_gain_part, gate_up_part, down_part)
+def turned(array):
+    return array.reshape(-1, array.shape[-1]).T
+
+
+def flat(array):
+    return array.reshape(-1, array.shape[-1])
+
+
+MESH = pl.DeviceIdType.MESH
+LANES = 128
+
+
+def grad_plan(groups, dp, tokens, width, hidden, qkv_cols):
+    pairs = dp // 2
+    block = width // groups
+    down_block = hidden // groups
+    gate_cols = 2 * hidden // 2 // pairs
+    qkv_part = qkv_cols // 2 // pairs
+    pieces_gate = gate_cols // LANES
+    pieces_qkv = qkv_part // LANES
+    pieces = pieces_gate + pieces_qkv
+    z_rows = LANES
+    while down_block % z_rows or block % z_rows:
+        z_rows //= 2
+    row_chunks = (down_block + block) // z_rows
+    half = width // 2
+    z_split = max(1, pieces // row_chunks)
+    while half % (z_split * LANES):
+        z_split -= 1
+    return dict(
+        groups=groups, pairs=pairs, tokens=tokens, width=width, hidden=hidden, qkv_cols=qkv_cols, block=block,
+        down_block=down_block, gate_cols=gate_cols, qkv_part=qkv_part, pieces_gate=pieces_gate, pieces=pieces,
+        z_rows=z_rows, z_split=z_split, z_cols=half // z_split, z_pieces=row_chunks * z_split,
+        down_chunks=down_block // z_rows, half=half,
+    )
+
+
+YS_RING = 4
+HOP = 2
+LEAD = 2
+
+
+def grad_kernel(
+    plan, at, ot, n2t, n1t, dz, dy, dg, dq, outy, outz,
+    LT, RH, YS, YR, YRT, YLT, ZRT, ZLT, ZX,
+    own_sem, xs, xr, ys_s, ys_r, yr_s, yr_r, yl_s, yl_r, zr_s, zr_r, zl_s, zl_r,
+    zx_s, zx_r, ag_s, ag_r, sib_s, sib_r, lo,
+):
+    G, A, T = plan["groups"], plan["pairs"], plan["tokens"]
+    width, hidden, half = plan["width"], plan["hidden"], plan["half"]
+    block, nY, nZ = plan["block"], plan["pieces"], plan["z_pieces"]
+    zr, zc = plan["z_rows"], plan["z_cols"]
+    s, z, d = lax.axis_index("section"), lax.axis_index("group"), lax.axis_index("dp")
+    c, a = lax.rem(d, 2), lax.div(d, 2)
+    sib = (s, z, 2 * a + 1 - c)
+    right, left = (s, z + 1, d), (s, z - 1, d)
+
+    def peer(k):
+        return (s, z, 2 * lax.rem(a + k, A) + c)
+
+    def remote(src, dst, ss, rs, dev):
+        return pltpu.make_async_remote_copy(
+            src_ref=src, dst_ref=dst, send_sem=ss, recv_sem=rs, device_id=dev, device_id_type=MESH
+        )
+
+    barrier = pltpu.get_barrier_semaphore()
+    for dev in [sib, (s, lax.rem(z + 1, G), d), (s, lax.rem(z + G - 1, G), d)] + [peer(k) for k in range(1, A)]:
+        pl.semaphore_signal(barrier, inc=1, device_id=dev, device_id_type=MESH)
+    pl.semaphore_wait(barrier, A + 2)
+
+    lhs = [(at, 0, hidden), (ot, hidden, width), (n2t, hidden + width, width), (n1t, hidden + 2 * width, width)]
+    rhs = [(dz, 0, half), (dy, half, half), (dg, width, hidden), (dq, width + hidden, plan["qkv_cols"] // 2)]
+    order = [(0, 0), (2, 2), (1, 1), (3, 3)]
+    own, cross = {}, {}
+    for i, (ref, row, rows) in enumerate(lhs):
+        own[0, i] = pltpu.make_async_copy(ref, LT.at[pl.ds(row, rows), pl.ds(0, T)], own_sem.at[i])
+        cross[0, i] = remote(ref, LT.at[pl.ds(row, rows), pl.ds(T, T)], xs.at[i], xr.at[i], sib)
+    for i, (ref, col, cols) in enumerate(rhs):
+        mine = pl.ds(pl.multiple_of(c * cols, LANES), cols)
+        theirs = pl.ds(pl.multiple_of((1 - c) * cols, LANES), cols)
+        own[1, i] = pltpu.make_async_copy(ref.at[:, mine], RH.at[pl.ds(0, T), pl.ds(col, cols)], own_sem.at[4 + i])
+        cross[1, i] = remote(ref.at[:, theirs], RH.at[pl.ds(T, T), pl.ds(col, cols)], xs.at[4 + i], xr.at[4 + i], sib)
+    for i, _ in order:
+        for side in (0, 1):
+            own[side, i].start()
+            cross[side, i].start()
+
+    def operands_here(i):
+        for side in (0, 1):
+            own[side, i].wait()
+            cross[side, i].wait_recv()
+
+    def product(row, rows, col, cols):
+        return jnp.dot(
+            LT[pl.ds(row, rows), :], RH[:, pl.ds(col, cols)], preferred_element_type=jnp.float32
+        )
+
+    def y_product(q, which, b):
+        is_gate = q < plan["pieces_gate"]
+        row = jnp.where(is_gate, hidden + width, hidden + 2 * width) + b * block
+        col = jnp.where(
+            is_gate,
+            width + which * plan["gate_cols"] + q * LANES,
+            width + hidden + which * plan["qkv_part"] + (q - plan["pieces_gate"]) * LANES,
+        )
+        return product(pl.multiple_of(row, 16), block, pl.multiple_of(col, LANES), LANES)
+
+    def z_product(p, b):
+        r, h = lax.div(p, plan["z_split"]), lax.rem(p, plan["z_split"])
+        is_down = r < plan["down_chunks"]
+        row = jnp.where(
+            is_down, b * plan["down_block"] + r * zr, hidden + b * block + (r - plan["down_chunks"]) * zr
+        )
+        col = jnp.where(is_down, 0, half) + h * zc
+        return product(pl.multiple_of(row, 16), zr, pl.multiple_of(col, LANES), zc)
+
+    def y_out(q, part, core):
+        is_gate = q < plan["pieces_gate"]
+        col = jnp.where(
+            is_gate,
+            core * hidden + part * plan["gate_cols"] + q * LANES,
+            2 * hidden + core * (plan["qkv_cols"] // 2) + part * plan["qkv_part"] + (q - plan["pieces_gate"]) * LANES,
+        )
+        return outy.at[:, pl.ds(pl.multiple_of(col, LANES), LANES)]
+
+    def z_out(p, core):
+        r, h = lax.div(p, plan["z_split"]), lax.rem(p, plan["z_split"])
+        return outz.at[
+            pl.ds(pl.multiple_of(r * zr, 16), zr), pl.ds(pl.multiple_of(core * half + h * zc, LANES), zc)
+        ]
+
+    def y_send(q, k):
+        return remote(YS.at[lax.rem(q, YS_RING), k - 1], YR.at[q, k - 1], ys_s.at[q, k - 1], ys_r.at[q, k - 1], peer(k))
+
+    def line_copies(slots_r, slots_l, r_s, r_r, l_s, l_r, first_r, first_l, p):
+        out_r, in_r, out_l, in_l = [], [], [], []
+        for k in range(G):
+            if k < G - 1:
+                src = first_r(p) if k == 0 else slots_r.at[p, pl.ds(k, G - 1 - k)]
+                out_r.append((k, remote(src, slots_r.at[p, pl.ds(k, G - 1 - k)], r_s.at[p], r_r.at[p], right)))
+                held = slots_l.at[p, pl.ds(0, k + 1)]
+                in_l.append((k, remote(held, held, l_s.at[p], l_r.at[p], left)))
+            if k > 0:
+                src = first_l(p) if k == G - 1 else slots_l.at[p, pl.ds(0, k)]
+                out_l.append((k, remote(src, slots_l.at[p, pl.ds(0, k)], l_s.at[p], l_r.at[p], left)))
+                held = slots_r.at[p, pl.ds(k - 1, G - k)]
+                in_r.append((k, remote(held, held, r_s.at[p], r_r.at[p], right)))
+        return out_r, in_r, out_l, in_l
+
+    def at_place(copies, act):
+        for k, copy in copies:
+            @pl.when(z == k)
+            def _(copy=copy):
+                act(copy)
+
+    def y_line(q):
+        return line_copies(
+            YRT, YLT, yr_s, yr_r, yl_s, yl_r,
+            lambda q: YR.at[q, 0, pl.ds(1, G - 1)], lambda q: YR.at[q, 0, pl.ds(0, G - 1)], q,
+        )
+
+    def z_line(p):
+        return line_copies(
+            ZRT, ZLT, zr_s, zr_r, zl_s, zl_r,
+            lambda p: ZRT.at[p, pl.ds(0, G - 1)], lambda p: ZLT.at[p, pl.ds(0, G - 1)], p,
+        )
+
+    def zx_copy(p, k):
+        return remote(ZX.at[p, a], ZX.at[p, a], zx_s.at[p, k - 1], zx_r.at[p, k - 1], peer(k))
+
+    def ag_copy(q, k):
+        return remote(YR.at[q, 0, z], y_out(q, a, c), ag_s.at[q, k - 1], ag_r.at[q, k - 1], peer(k))
+
+    def sib_own(q):
+        return remote(YR.at[q, 0, z], y_out(q, a, c), sib_s.at[q, 0], sib_r.at[q, 0], sib)
+
+    def sib_pass(q, k):
+        part = lax.rem(a + A - k, A)
+        return remote(y_out(q, part, c), y_out(q, part, c), sib_s.at[q, k], sib_r.at[q, k], sib)
+
+    def own_y(q):
+        return pltpu.make_async_copy(YR.at[q, 0, z], y_out(q, a, c), lo.at[q])
+
+    def own_z(p):
+        return pltpu.make_async_copy(ZX.at[p, a], z_out(p, c), lo.at[nY + p])
+
+    def sib_z(p):
+        return remote(ZX.at[p, a], z_out(p, c), sib_s.at[nY + p, 0], sib_r.at[nY + p, 0], sib)
+
+    f32, bf16 = jnp.float32, jnp.bfloat16
+    far = jnp.maximum(z, G - 1 - z)
+
+    def live(index, count):
+        return (index >= 0) & (index < count)
+
+    def step(t, carry):
+        @pl.when(t == 0)
+        def _():
+            operands_here(0)
+            operands_here(2)
+
+        @pl.when(t == 1)
+        def _():
+            operands_here(1)
+            operands_here(3)
+
+        q1 = t
+
+        @pl.when(live(q1, nY))
+        def _():
+            for k in range(1, A):
+                @pl.when(q1 >= YS_RING)
+                def _():
+                    y_send(q1 - YS_RING, k).wait_send()
+
+                @pl.loop(0, G)
+                def _(b):
+                    YS[lax.rem(q1, YS_RING), k - 1, b] = y_product(q1, lax.rem(a + k, A), b).astype(bf16)
+
+                y_send(q1, k).start()
+
+        pr = t - HOP * z
+
+        @pl.when(live(pr, nZ))
+        def _():
+            out_r, in_r, _, _ = z_line(pr)
+            at_place(in_r, lambda copy: copy.wait_recv())
+
+            @pl.loop(0, G)
+            def _(b):
+                @pl.when((b > z) & (z > 0))
+                def _():
+                    ZRT[pr, b - 1] = (z_product(pr, b) + ZRT[pr, b - 1].astype(f32)).astype(bf16)
+
+                @pl.when((b > z) & (z == 0))
+                def _():
+                    ZRT[pr, b - 1] = z_product(pr, b).astype(bf16)
+
+            at_place(out_r, lambda copy: copy.start())
+
+        pL = t - HOP * (G - 1 - z)
+
+        @pl.when(live(pL, nZ))
+        def _():
+            _, _, out_l, in_l = z_line(pL)
+            at_place(in_l, lambda copy: copy.wait_recv())
+
+            @pl.loop(0, G)
+            def _(b):
+                @pl.when((b < z) & (z < G - 1))
+                def _():
+                    ZLT[pL, b] = (z_product(pL, b) + ZLT[pL, b].astype(f32)).astype(bf16)
+
+                @pl.when((b < z) & (z == G - 1))
+                def _():
+                    ZLT[pL, b] = z_product(pL, b).astype(bf16)
+
+            at_place(out_l, lambda copy: copy.start())
+
+        q2 = t - LEAD
+
+        @pl.when(live(q2, nY))
+        def _():
+            for k in range(1, A):
+                y_send(q2, k).wait_recv()
+
+            @pl.loop(0, G)
+            def _(b):
+                total = y_product(q2, a, b)
+                for k in range(1, A):
+                    total += YR[q2, k - 1, b].astype(f32)
+                YR[q2, 0, b] = total.astype(bf16)
+
+        qr = t - LEAD - HOP * z
+
+        @pl.when(live(qr, nY))
+        def _():
+            out_r, in_r, _, _ = y_line(qr)
+            at_place(in_r, lambda copy: copy.wait_recv())
+
+            @pl.loop(0, G)
+            def _(b):
+                @pl.when((b > z) & (z > 0))
+                def _():
+                    YRT[qr, b - 1] = (YR[qr, 0, b].astype(f32) + YRT[qr, b - 1].astype(f32)).astype(bf16)
+
+            at_place(out_r, lambda copy: copy.start())
+
+        qL = t - LEAD - HOP * (G - 1 - z)
+
+        @pl.when(live(qL, nY))
+        def _():
+            _, _, out_l, in_l = y_line(qL)
+            at_place(in_l, lambda copy: copy.wait_recv())
+
+            @pl.loop(0, G)
+            def _(b):
+                @pl.when((b < z) & (z < G - 1))
+                def _():
+                    YLT[qL, b] = (YR[qL, 0, b].astype(f32) + YLT[qL, b].astype(f32)).astype(bf16)
+
+            at_place(out_l, lambda copy: copy.start())
+
+        pf = t - HOP * far
+
+        @pl.when(live(pf, nZ))
+        def _():
+            mine = z_product(pf, z)
+            from_left = ZRT[pf, jnp.maximum(z - 1, 0)].astype(f32)
+            from_right = ZLT[pf, jnp.minimum(z, G - 2)].astype(f32)
+            mine = mine + jnp.where(z > 0, from_left, 0.0) + jnp.where(z < G - 1, from_right, 0.0)
+            ZX[pf, a] = mine.astype(bf16)
+            for k in range(1, A):
+                zx_copy(pf, k).start()
+
+        pg = t - HOP * far - LEAD
+
+        @pl.when(live(pg, nZ))
+        def _():
+            for k in range(1, A):
+                remote(
+                    ZX.at[pg, lax.rem(a + A - k, A)], ZX.at[pg, lax.rem(a + A - k, A)],
+                    zx_s.at[pg, k - 1], zx_r.at[pg, k - 1], peer(k),
+                ).wait_recv()
+            total = ZX[pg, 0].astype(f32)
+            for k in range(1, A):
+                total += ZX[pg, k].astype(f32)
+            for k in range(1, A):
+                zx_copy(pg, k).wait_send()
+            ZX[pg, a] = total.astype(bf16)
+            own_z(pg).start()
+            sib_z(pg).start()
+
+        qf = t - LEAD - HOP * far
+
+        @pl.when(live(qf, nY))
+        def _():
+            total = YR[qf, 0, z].astype(f32)
+            from_left = YRT[qf, jnp.maximum(z - 1, 0)].astype(f32)
+            from_right = YLT[qf, jnp.minimum(z, G - 2)].astype(f32)
+            total = total + jnp.where(z > 0, from_left, 0.0) + jnp.where(z < G - 1, from_right, 0.0)
+            YR[qf, 0, z] = total.astype(bf16)
+            for k in range(1, A):
+                ag_copy(qf, k).start()
+            own_y(qf).start()
+            sib_own(qf).start()
+
+        qg = t - LEAD - HOP * far - LEAD
+
+        @pl.when(live(qg, nY))
+        def _():
+            for k in range(1, A):
+                here = y_out(qg, lax.rem(a + A - k, A), c)
+                remote(here, here, ag_s.at[qg, k - 1], ag_r.at[qg, k - 1], peer(k)).wait_recv()
+                sib_pass(qg, k).start()
+
+        return carry
+
+    steps = max(nY, nZ) + 2 * LEAD + HOP * (G - 1)
+    lax.fori_loop(0, steps, step, 0)
+
+    for i in range(4):
+        for side in (0, 1):
+            cross[side, i].wait_send()
+
+    def drain_y(q, carry):
+        for k in range(1, A):
+            @pl.when(q >= nY - YS_RING)
+            def _():
+                y_send(q, k).wait_send()
+
+            ag_copy(q, k).wait_send()
+            sib_pass(q, k).wait_send()
+            there = y_out(q, lax.rem(a + A - k, A), 1 - c)
+            remote(there, there, sib_s.at[q, k], sib_r.at[q, k], sib).wait_recv()
+        out_r, _, out_l, _ = y_line(q)
+        at_place(out_r, lambda copy: copy.wait_send())
+        at_place(out_l, lambda copy: copy.wait_send())
+        own_y(q).wait()
+        sib_own(q).wait_send()
+        there = y_out(q, a, 1 - c)
+        remote(there, there, sib_s.at[q, 0], sib_r.at[q, 0], sib).wait_recv()
+        return carry
+
+    lax.fori_loop(0, nY, drain_y, 0)
+
+    def drain_z(p, carry):
+        out_r, _, out_l, _ = z_line(p)
+        at_place(out_r, lambda copy: copy.wait_send())
+        at_place(out_l, lambda copy: copy.wait_send())
+        own_z(p).wait()
+        sib_z(p).wait_send()
+        there = z_out(p, 1 - c)
+        remote(there, there, sib_s.at[nY + p, 0], sib_r.at[nY + p, 0], sib).wait_recv()
+        return carry
+
+    lax.fori_loop(0, nZ, drain_z, 0)
+
+
+def summed_grads(groups, dp, at, ot, n2t, n1t, dz, dy, dg, dq):
+    hidden, tokens = at.shape
+    width, qkv_cols = ot.shape[0], dq.shape[1]
+    plan = grad_plan(groups, dp, tokens, width, hidden, qkv_cols)
+    G, A, nY, nZ = groups, plan["pairs"], plan["pieces"], plan["z_pieces"]
+    block, zr, zc = plan["block"], plan["z_rows"], plan["z_cols"]
+    bf16, DMA = jnp.bfloat16, pltpu.SemaphoreType.DMA
+    any_space = pl.BlockSpec(memory_space=pl.ANY)
+    return pl.pallas_call(
+        functools.partial(grad_kernel, plan),
+        out_shape=(
+            jax.ShapeDtypeStruct((block, 2 * hidden + qkv_cols), bf16),
+            jax.ShapeDtypeStruct((plan["down_block"] + block, width), bf16),
+        ),
+        in_specs=[any_space] * 8,
+        out_specs=(any_space, any_space),
+        scratch_shapes=[
+            pltpu.VMEM((hidden + 3 * width, 2 * tokens), bf16),
+            pltpu.VMEM((2 * tokens, width + hidden + qkv_cols // 2), bf16),
+            pltpu.VMEM((YS_RING, A - 1, G, block, LANES), bf16),
+            pltpu.VMEM((nY, A - 1, G, block, LANES), bf16),
+            pltpu.VMEM((nY, G - 1, block, LANES), bf16),
+            pltpu.VMEM((nY, G - 1, block, LANES), bf16),
+            pltpu.VMEM((nZ, G - 1, zr, zc), bf16),
+            pltpu.VMEM((nZ, G - 1, zr, zc), bf16),
+            pltpu.VMEM((nZ, A, zr, zc), bf16),
+            DMA((8,)), DMA((8,)), DMA((8,)),
+            DMA((nY, A - 1)), DMA((nY, A - 1)),
+            DMA((nY,)), DMA((nY,)), DMA((nY,)), DMA((nY,)),
+            DMA((nZ,)), DMA((nZ,)), DMA((nZ,)), DMA((nZ,)),
+            DMA((nZ, A - 1)), DMA((nZ, A - 1)),
+            DMA((nY, A - 1)), DMA((nY, A - 1)),
+            DMA((nY + nZ, A)), DMA((nY + nZ, A)),
+            DMA((nY + nZ,)),
+        ],
+        compiler_params=pltpu.CompilerParams(
+            collective_id=3, has_side_effects=True, vmem_limit_bytes=63 * 1024 * 1024
+        ),
+        cost_estimate=pl.CostEstimate(
+            flops=2 * 2 * tokens * (width * (2 * hidden + qkv_cols + width) + hidden * width) // 2,
+            bytes_accessed=40_000_000, transcendentals=0,
+        ),
+    )(at, ot, n2t, n1t, dz, dy, dg, dq)
 
 
 def body(
     inputs_x, cotangent, lengths, attn_gain, qkv_weight, out_weight, ffn_gain, gate_up, down_weight
 ):
     is_first = lax.axis_index("section") == 0
-    weights = tuple(
-        (
-            whole[0]
-            for whole in (
-                lax.all_gather(attn_gain, ("group", "dp"), axis=1, tiled=True),
-                lax.all_gather(qkv_weight, ("group", "dp"), axis=1, tiled=True),
-                lax.all_gather(out_weight, ("group", "dp"), axis=1, tiled=True),
-                lax.all_gather(ffn_gain, ("group", "dp"), axis=1, tiled=True),
-                lax.all_gather(gate_up, ("group", "dp"), axis=1, tiled=True),
-                lax.all_gather(down_weight, ("group", "dp"), axis=1, tiled=True),
-            )
-        )
+    everyone = ("group", "dp")
+    gains = lax.all_gather(jnp.concatenate([attn_gain, ffn_gain], 0), everyone)
+    gains = gains.transpose(1, 0, 2).reshape(2, -1)
+    weights = (
+        gains[0],
+        lax.all_gather(qkv_weight[0], everyone, axis=0, tiled=True),
+        lax.all_gather(out_weight[0], everyone, axis=0, tiled=True),
+        gains[1],
+        lax.all_gather(gate_up[0], everyone, axis=0, tiled=True),
+        lax.all_gather(down_weight[0], everyone, axis=0, tiled=True),
     )
     inputs_f = inputs_x.astype(jnp.float32)
     cotangent_f = cotangent.astype(jnp.float32)
@@ -277,13 +694,35 @@
     input_grads = jnp.where(
         is_first, grad_x, grad_x.astype(jnp.bfloat16).astype(jnp.float32)
     )[None]
-    totals = weight_grads(kept_state, operands)
-    reduced = []
-    for total in totals:
-        piece = lax.psum_scatter(
-            total.astype(jnp.bfloat16), ("group", "dp"), scatter_dimension=0, tiled=True
-        )
-        reduced.append(lax.all_gather(piece, "dp", axis=0, tiled=True).astype(jnp.float32))
+    (_, _, normed_one, _, _, _, _, attention_result, _, _, normed_two, _, hidden, _) = kept_state
+    attn_gain_part, ffn_gain_part, grad_low, grad_gated, gradient_after_lowered, grad_qkv = operands
+    gain_parts = lax.all_gather(jnp.stack([attn_gain_part, ffn_gain_part]), ("group", "dp"))
+    gate_qkv_sum, down_out_sum = summed_grads(
+        lax.axis_size("group"),
+        lax.axis_size("dp"),
+        turned(hidden),
+        turned(attention_result),
+        turned(normed_two),
+        turned(normed_one),
+        flat(grad_low),
+        flat(gradient_after_lowered),
+        flat(grad_gated),
+        flat(grad_qkv),
+    )
+    gain_cols = attn_gain.shape[1] * lax.axis_size("dp")
+    gain_sums = lax.dynamic_slice_in_dim(
+        jnp.sum(gain_parts, 0), lax.axis_index("group") * gain_cols, gain_cols, 1
+    )
+    gate_width = gate_up.shape[2]
+    down_rows = down_weight.shape[1] * lax.axis_size("dp")
+    reduced = (
+        gain_sums[0],
+        gate_qkv_sum[:, gate_width:].astype(jnp.float32),
+        down_out_sum[down_rows:].astype(jnp.float32),
+        gain_sums[1],
+        gate_qkv_sum[:, :gate_width].astype(jnp.float32),
+        down_out_sum[:down_rows].astype(jnp.float32),
+    )
     return (section_out, input_grads) + tuple((shard_sum[None] for shard_sum in reduced))
 
 

time: 1290 us -> 979 us (0.76)
  waiting for transfers between devices: 905 us -> 346 us
  Pallas kernels: 0 us -> 313 us
  matrix products: 199 us -> 153 us
  blocking collectives: 74.7 us -> 42.6 us
  local copies, waits for them, and re-layouts: 35.1 us -> 49.3 us
    reduce_scatter x4 -> x0, waiting for transfers between devices: 520 us -> none  [body(): lax.psum_scatter(total.astype(jnp.bfloat16), ('group', 'dp'), scatter_dim...]
    pallas_call x0 -> x1, Pallas kernels: none -> 313 us  [summed_grads(): pl.pallas_call(functools.partial(grad_kernel, plan), out_shape=(jax.Shape...]
    unnamed x3 -> x0, blocking collectives: 74.7 us -> none
    all_gather x0 -> x2, blocking collectives: none -> 42.6 us  [the longest x1 23.1 us: body(): gains = lax.all_gather(jnp.concatenate([attn_gain, ffn_gain], 0), everyone)]
    dot_general x4 -> x0, matrix products: 33.4 us -> none  [the longest x1 14.2 us: weight_grads(): jnp.einsum('rsd,rse->de', normed_two, grad_gated, preferred_element_type=...]
    all_gather x8 -> x4, waiting for transfers between devices: 345 us -> 313 us  [the longest x1 125 us: body(): lax.all_gather(gate_up[0], everyone, axis=0, tiled=True)]
  transfers between devices with their start and end apart: 14 -> 6, of which waited for: 12 -> 6; matrix products, arithmetic and copies ran while one was open for 9% -> 4% of each run, Pallas kernels for 0% -> 0%
where the time goes in v2:
time: 979 us; the launch traced here: 970 us
  waiting for transfers between devices  346 us (35%)
  Pallas kernels  313 us (32%)
  matrix products  153 us (16%)
  local copies, waits for them, and re-layouts  49.3 us (5%)
  other arithmetic  46.1 us (5%)
  blocking collectives  42.6 us (4%)
  between operations  15.2 us (2%)
    pallas_call x1, Pallas kernels, summed_grads(): pl.pallas_call(functools.partial(grad_kernel, plan), out_shape=(jax.Shape...  313 us
    all_gather x1, waiting for transfers between devices, body(): lax.all_gather(gate_up[0], everyone, axis=0, tiled=True)  125 us
    all_gather x1, waiting for transfers between devices, body(): lax.all_gather(down_weight[0], everyone, axis=0, tiled=True)  89.3 us
    all_gather x1, waiting for transfers between devices, body(): lax.all_gather(qkv_weight[0], everyone, axis=0, tiled=True)  60.5 us
    all_gather x1, waiting for transfers between devices, body(): lax.all_gather(out_weight[0], everyone, axis=0, tiled=True)  38.5 us
    ppermute x2, waiting for transfers between devices, passed_along(): return lax.ppermute(value, axis, pairs)  29.8 us
    dot_general x2, matrix products, backward_layer(): jnp.einsum('rse,de->rsd', grad_gated, gate_up_w, preferred_element_type=j...  28.6 us
    dot_general x2, matrix products, forward_layer(): jnp.einsum('rsd,de->rse', normed_two, gate_up_w, preferred_element_type=j...  27.8 us
  transfers between devices with their start and end apart: 6, of which 6 were waited for; matrix products, arithmetic and copies ran while one was open for 4% of the time, Pallas kernels for 0%

profile of v2, /device:TPU:0, one launch (start us, length us, event | category | flops | bytes accessed | tf_op | source)
XLA Modules:
  0.0 969.5 jit_solution(15901419913661244847)
XLA Ops:
  10.0 23.1 %all-gather.6 = bf16[16,2,96]{2,1,0:T(2,128)(2,1)S(1)} all-gather(bf16[1,2,96]{2,1,0:T(2,128)(2,1)S(1)} %maximum_bitcast_fusion.7), channel_id=2, replica_groups=mesh['section'=2,'group'=4,'dp'=4] {'group','dp'}, dimensions={0}, use_global_device_ids=true | all-gather | bytes 6528 | tf_op jit(solution)/shard_map/all_gather | solution.py:673
  34.0 60.5 %all-gather.13.cloned.1.call-done = bf16[1,1536,3072]{2,1,0:T(8,128)(2,1)} async-done(((bf16[1,96,3072]{2,1,0:T(8,128)(2,1)}), bf16[1,1536,3072]{2,1,0:T(8,128)(2,1)}) %all-gather.13.cloned.1.call-update) | async-done | bytes 9437200 | tf_op jit(solution)/shard_map/all_gather | solution.py:677
  94.5 5.2 fusion.22
  109.9 38.5 %all-gather.15.cloned.1.call-done = bf16[1,1536,1536]{2,1,0:T(8,128)(2,1)} async-done(((bf16[1,96,1536]{2,1,0:T(8,128)(2,1)}), bf16[1,1536,1536]{2,1,0:T(8,128)(2,1)}) %all-gather.15.cloned.1.call-update) | async-done | bytes 4718608 | tf_op jit(solution)/shard_map/all_gather | solution.py:678
  152.2 124.9 %all-gather.17.cloned.1.call-done = bf16[1,1536,8192]{2,1,0:T(8,128)(2,1)} async-done(((bf16[1,96,8192]{2,1,0:T(8,128)(2,1)}), bf16[1,1536,8192]{2,1,0:T(8,128)(2,1)}) %all-gather.17.cloned.1.call-update) | async-done | bytes 25165840 | tf_op jit(solution)/shard_map/all_gather | solution.py:680
  277.1 13.7 %fusion.6 = f32[2,128,8192]{2,1,0:T(8,128)} fusion(bf16[1,1536,8192]{2,1,0:T(8,128)(2,1)} %all-gather.17.cloned.1.call-done, f32[2,128,1536]{2,1,0:T(8,128)S(1)} %get-tuple-element.55, f32[1536]{0:T(1024)S(1)} %reshape.356, f32[2,128]{1,0:T(2,128)S(1)} %add_rsqrt_fusion.2), kind=kOutput, calls=%fused_computation.6 | convolution fusion | flops 6443630592 | bytes 35134464 | tf_op jit(solution)/shard_map/rsd,de->rse/dot_general | solution.py:116
  290.8 89.3 %all-gather.19.cloned.1.call-done = bf16[1,4096,1536]{2,1,0:T(8,128)(2,1)} async-done(((bf16[1,256,1536]{2,1,0:T(8,128)(2,1)}), bf16[1,4096,1536]{2,1,0:T(8,128)(2,1)}) %all-gather.19.cloned.1.call-update) | async-done | bytes 12582928 | tf_op jit(solution)/shard_map/all_gather | solution.py:681
  380.1 11.4 %fusion.67 = bf16[2,128,1536]{2,1,0:T(8,128)(2,1)} fusion(f32[2,128,1536]{2,1,0:T(8,128)S(1)} %get-tuple-element.55, bf16[1,4096,1536]{2,1,0:T(8,128)(2,1)} %all-gather.19.cloned.1.call-done, f32[2,128,8192]{2,1,0:T(8,128)} %fusion.6, f32[2,128]{1,0:T(2,128)S(1)} %get-tuple-element.50), kind=kOutput, calls=%fused_computation.63 | convolution fusion | flops 3228696576 | bytes 23331840 | tf_op jit(solution)/shard_map/rsf,fd->rsd/dot_general | solution.py:118
  394.9 17.5 %collective-permute-done = bf16[2,128,1536]{2,1,0:T(8,128)(2,1)S(1)} collective-permute-done((bf16[2,128,1536]{2,1,0:T(8,128)(2,1)}, bf16[2,128,1536]{2,1,0:T(8,128)(2,1)S(1)}, u32[]{:S(2)}, u32[]{:S(2)}) %collective-permute-start) | collective-permute-done | bytes 786464 | tf_op jit(solution)/shard_map/ppermute | solution.py:24
  413.6 5.6 fusion.20
  436.9 14.2 %fusion.4 = f32[2,128,8192]{2,1,0:T(8,128)} fusion(bf16[2,128,1536]{2,1,0:T(8,128)(2,1)S(1)} %multiply_convert_fusion.5, bf16[1,1536,8192]{2,1,0:T(8,128)(2,1)} %all-gather.17.cloned.1.call-done), kind=kOutput, calls=%fused_computation.4 | convolution fusion | flops 6442450944 | bytes 34340864 | tf_op jit(solution)/shard_map/rsd,de->rse/dot_general | solution.py:116
  451.1 10.7 %multiply_convert_fusion.3 = (bf16[2,128,4096]{2,1,0:T(8,128)(2,1)}, bf16[2,128,4096]{2,1,0:T(8,128)(2,1)}) fusion(f32[2,128,8192]{2,1,0:T(8,128)} %fusion.4, bf16[1,4096,1536]{2,1,0:T(8,128)(2,1)} %all-gather.19.cloned.1.call-done, bf16[2,128,1536]{2,1,0:T(8,128)(2,1)S(1)} %copy-done.14, f32[2,128]{1,0:T(2,128)S(1)} %copy-done.53), kind=kOutput, calls=%fused_computation.45 | convolution fusion | flops 3236036608 | bytes 25953280 | tf_op jit(solution)/shard_map/rsd,fd->rsf/dot_general | solution.py:165
  461.8 14.1 %multiply_reduce_fusion.5 = (f32[2,128]{1,0:T(2,128)S(1)}, f32[2,128,1536]{2,1,0:T(8,128)}) fusion(f32[2,128,1536]{2,1,0:T(8,128)S(1)} %get-tuple-element.59, f32[1536]{0:T(1024)S(1)} %copy-done.44, bf16[1,1536,8192]{2,1,0:T(8,128)(2,1)} %all-gather.17.cloned.1.call-done, bf16[2,128,4096]{2,1,0:T(8,128)(2,1)} %get-tuple-element.23, ...), kind=kOutput, calls=%fused_computation.114 | convolution fusion | flops 6452019200 | bytes 32513024 | tf_op jit(solution)/shard_map/rse,de->rsd/dot_general | solution.py:172
  498.6 7.2 multiply_reduce_fusion.4
  516.5 12.3 %collective-permute-done.1 = bf16[2,128,1536]{2,1,0:T(8,128)(2,1)} collective-permute-done((bf16[2,128,1536]{2,1,0:T(8,128)(2,1)}, bf16[2,128,1536]{2,1,0:T(8,128)(2,1)}, u32[]{:S(2)}, u32[]{:S(2)}) %collective-permute-start.1) | collective-permute-done | bytes 786464 | tf_op jit(solution)/shard_map/ppermute | solution.py:24
  530.5 11.6 %multiply_convert_fusion.1 = (bf16[2,128,4096]{2,1,0:T(8,128)(2,1)}, bf16[2,128,4096]{2,1,0:T(8,128)(2,1)}, bf16[2,128,4096]{2,1,0:T(8,128)(2,1)}) fusion(f32[2,128,8192]{2,1,0:T(8,128)} %fusion.4, bf16[2,128,1536]{2,1,0:T(8,128)(2,1)S(1)} %fusion.103, bf16[1,4096,1536]{2,1,0:T(8,128)(2,1)} %all-gather.19.cloned.1.call-done), kind=kOutput, calls=%fused_computation.43 | convolution fusion | flops 3236954112 | bytes 28049408 | tf_op jit(solution)/shard_map/rsd,fd->rsf/dot_general | solution.py:165
  542.1 14.5 %multiply_reduce_fusion = (f32[1536]{0:T(1024)}, f32[2,128]{1,0:T(2,128)S(1)}, f32[2,128,1536]{2,1,0:T(8,128)}) fusion(f32[2,128,1536]{2,1,0:T(8,128)S(1)} %copy-done.3, f32[2,128]{1,0:T(2,128)S(1)} %copy-done.51, f32[1536]{0:T(1024)S(1)} %copy-done.44, bf16[1,1536,8192]{2,1,0:T(8,128)(2,1)} %all-gather.17.cloned.1.call-done, ...), kind=kOutput, calls=%fused_computation.105 | convolution fusion | flops 6453196800 | bytes 32520192 | tf_op jit(solution)/shard_map/rse,de->rsd/dot_general | solution.py:172
  579.1 4.4 copy.145
  588.9 312.5 %shard_map.152 = (bf16[384,11264]{1,0:T(8,128)(2,1)}, bf16[1408,1536]{1,0:T(8,128)(2,1)}) custom-call(bf16[4096,256]{1,0:T(8,128)(2,1)} %bitcast.302, bf16[1536,256]{1,0:T(8,128)(2,1)} %bitcast.309, bf16[1536,256]{1,0:T(8,128)(2,1)} %bitcast.308, bf16[1536,256]{1,0:T(8,128)(2,1)} %bitcast.310, bf16[256,1536]{1,0:T(8,128)(2,1)} %bitcast.311, ...), custom_call_target="tpu_custom_call" | custom-call | flops 13287555072 | bytes 40000000 | tf_op jit(solution)/shard_map/pallas_call | solution.py:631
  901.5 9.3 bitcast_convert_fusion
  910.7 4.4 bitcast_convert_fusion.2
  922.8 8.1 multiply_reduce_fusion.1
  931.0 19.5 %all-gather.7 = f32[16,2,1536]{2,1,0:T(2,128)S(1)} all-gather(f32[1,2,1536]{2,1,0:T(2,128)S(1)} %maximum_bitcast_fusion.6), channel_id=7, replica_groups=mesh['section'=2,'group'=4,'dp'=4] {'group','dp'}, dimensions={0}, use_global_device_ids=true | all-gather | bytes 208896 | tf_op jit(solution)/shard_map/all_gather | solution.py:699
  951.2 9.6 fusion.76
  (261 shorter events, 112.1 us)
Async XLA Ops:
  7.2 26.2 %copy-start = (bf16[2,128,1536]{2,1,0:T(8,128)(2,1)S(1)}, bf16[2,128,1536]{2,1,0:T(8,128)(2,1)}, u32[]{:S(2)}) copy-start(bf16[2,128,1536]{2,1,0:T(8,128)(2,1)} %param.9) | copy-start | bytes 2359300
  7.2 26.4 %copy-start.65 = (s32[2]{0:T(128)S(1)}, s32[2]{0:T(128)}, u32[]{:S(2)}) copy-start(s32[2]{0:T(128)} %param.11) | copy-start | bytes 28
  7.2 87.3 %all-gather.13.cloned.1.call-start = ((), (), s32[]{:S(2)}) async-start(), calls=%async_computation | async-start | bytes 10027008 | tf_op jit(solution)/shard_map/all_gather | solution.py:677
  7.9 140.4 %all-gather.15.cloned.1.call-start = ((), (), s32[]{:S(2)}) async-start(), calls=%async_computation.1 | async-start | bytes 5013504 | tf_op jit(solution)/shard_map/all_gather | solution.py:678
  8.7 268.4 %all-gather.17.cloned.1.call-start = ((), (), s32[]{:S(2)}) async-start(), calls=%async_computation.2 | async-start | bytes 26738688 | tf_op jit(solution)/shard_map/all_gather | solution.py:680
  9.4 370.6 %all-gather.19.cloned.1.call-start = ((), (), s32[]{:S(2)}) async-start(), calls=%async_computation.3 | async-start | bytes 13369344 | tf_op jit(solution)/shard_map/all_gather | solution.py:681
  33.3 243.8 %copy-start.43 = (f32[1536]{0:T(1024)}, f32[1536]{0:T(1024)S(1)}, u32[]{:S(2)}) copy-start(f32[1536]{0:T(1024)S(1)} %reshape.356) | copy-start | bytes 18436
  33.7 346.3 %copy-start.52 = (f32[2,128]{1,0:T(2,128)}, f32[2,128]{1,0:T(2,128)S(1)}, u32[]{:S(2)}) copy-start(f32[2,128]{1,0:T(2,128)S(1)} %get-tuple-element.50) | copy-start | bytes 3076
  33.8 74.5 %copy-start.45 = (pred[2,128,128]{1,2,0:T(8,128)(4,1)}, pred[2,128,128]{1,2,0:T(8,128)(4,1)S(1)}, u32[]{:S(2)}) copy-start(pred[2,128,128]{1,2,0:T(8,128)(4,1)S(1)} %broadcast_and_fusion) | copy-start | bytes 98308
  391.5 20.9 %collective-permute-start = (bf16[2,128,1536]{2,1,0:T(8,128)(2,1)}, bf16[2,128,1536]{2,1,0:T(8,128)(2,1)S(1)}, u32[]{:S(2)}, u32[]{:S(2)}) collective-permute-start(bf16[2,128,1536]{2,1,0:T(8,128)(2,1)} %fusion.67), channel_id=1, source_target_pairs={{0,16},{1,17},{2,18},{3,19},{4,20},{5,21},{6,22},{7,23},{8,24},{9,... | collective-permute-start | bytes 2359304 | tf_op jit(solution)/shard_map/ppermute | solution.py:24
  436.6 39.3 %copy-start.1 = (f32[2,128,1536]{2,1,0:T(8,128)}, f32[2,128,1536]{2,1,0:T(8,128)S(1)}, u32[]{:S(2)}) copy-start(f32[2,128,1536]{2,1,0:T(8,128)S(1)} %get-tuple-element.59) | copy-start | bytes 4718596
  436.6 39.3 %copy-start.49 = (f32[2,128]{1,0:T(2,128)}, f32[2,128]{1,0:T(2,128)S(1)}, u32[]{:S(2)}) copy-start(f32[2,128]{1,0:T(2,128)S(1)} %get-tuple-element.46) | copy-start | bytes 3076
  436.6 39.3 %copy-start.59 = (f32[2,128]{1,0:T(2,128)}, f32[2,128]{1,0:T(2,128)S(1)}, u32[]{:S(2)}) copy-start(f32[2,128]{1,0:T(2,128)S(1)} %get-tuple-element.45) | copy-start | bytes 3076
  436.8 14.2 %copy-start.31 = (bf16[2,128,1536]{2,1,0:T(8,128)(2,1)}, bf16[2,128,1536]{2,1,0:T(8,128)(2,1)S(1)}, u32[]{:S(2)}) copy-start(bf16[2,128,1536]{2,1,0:T(8,128)(2,1)S(1)} %multiply_convert_fusion.5) | copy-start | bytes 2359300
  436.8 14.2 %copy-start.14 = (bf16[2,128,1536]{2,1,0:T(8,128)(2,1)S(1)}, bf16[2,128,1536]{2,1,0:T(8,128)(2,1)}, u32[]{:S(2)}) copy-start(bf16[2,128,1536]{2,1,0:T(8,128)(2,1)} %param.10) | copy-start | bytes 2359300
  451.1 25.4 %slice-start = ((s8[4718592]{0:T(1024)(128)(4,1)}), s8[4194304]{0:T(1024)(128)(4,1)S(1)}, s32[]{:S(2)}) async-start(s8[4718592]{0:T(1024)(128)(4,1)} %bitcast.265), calls=%async_computation.4 | async-start | bytes 8388608
  461.8 14.7 %slice-start.1 = ((s8[4718592]{0:T(1024)(128)(4,1)}), s8[524288]{0:T(1024)(128)(4,1)S(1)}, s32[]{:S(2)}) async-start(s8[4718592]{0:T(1024)(128)(4,1)} %bitcast.265), calls=%async_computation.5 | async-start | bytes 1048576
  507.7 21.1 %collective-permute-start.1 = (bf16[2,128,1536]{2,1,0:T(8,128)(2,1)}, bf16[2,128,1536]{2,1,0:T(8,128)(2,1)}, u32[]{:S(2)}, u32[]{:S(2)}) collective-permute-start(bf16[2,128,1536]{2,1,0:T(8,128)(2,1)} %add_convert_fusion), channel_id=1, source_target_pairs={{16,0},{17,1},{18,2},{19,3},{20,4},{21,5},{22,6},{23,7},{24,8},{25... | collective-permute-start | bytes 2359304 | tf_op jit(solution)/shard_map/ppermute | solution.py:24
  530.4 30.8 %slice-start.2 = ((s8[4718592]{0:T(1024)(128)(4,1)}), s8[4194304]{0:T(1024)(128)(4,1)S(1)}, s32[]{:S(2)}) async-start(s8[4718592]{0:T(1024)(128)(4,1)} %bitcast.267), calls=%async_computation.6 | async-start | bytes 8388608
  542.1 14.6 %copy-start.55 = (f32[2,128]{1,0:T(2,128)S(1)}, f32[2,128]{1,0:T(2,128)}, u32[]{:S(2)}) copy-start(f32[2,128]{1,0:T(2,128)} %copy-done.52) | copy-start | bytes 3076
  542.1 14.6 %copy-start.61 = (f32[2,128]{1,0:T(2,128)S(1)}, f32[2,128]{1,0:T(2,128)}, u32[]{:S(2)}) copy-start(f32[2,128]{1,0:T(2,128)} %copy-done.59) | copy-start | bytes 3076
  542.1 19.1 %slice-start.3 = ((s8[4718592]{0:T(1024)(128)(4,1)}), s8[524288]{0:T(1024)(128)(4,1)S(1)}, s32[]{:S(2)}) async-start(s8[4718592]{0:T(1024)(128)(4,1)} %bitcast.267), calls=%async_computation.7 | async-start | bytes 1048576
  922.8 28.4 %copy-start.4 = (f32[2,128,1536]{2,1,0:T(8,128)S(1)}, f32[2,128,1536]{2,1,0:T(8,128)}, u32[]{:S(2)}) copy-start(f32[2,128,1536]{2,1,0:T(8,128)} %copy-done.1) | copy-start | bytes 4718596
  922.8 28.4 %copy-start.56 = (f32[2,128]{1,0:T(2,128)S(1)}, f32[2,128]{1,0:T(2,128)}, u32[]{:S(2)}) copy-start(f32[2,128]{1,0:T(2,128)} %copy-done.52) | copy-start | bytes 3076
  (57 other events, 296.4 us)
Sparse Core Ops, SparseCore 0:
  10.3 84.1 all-gather.12
  96.8 51.5 all-gather.14
  149.9 127.1 all-gather.16
  279.3 100.7 all-gather.18

commit v3 on v2

--- a/solution.py
+++ b/solution.py
@@ -264,10 +264,11 @@
 
 
 def grad_kernel(
-    plan, at, ot, n2t, n1t, dz, dy, dg, dq, outy, outz,
+    plan, at, ot, n2t, n1t, dz, dy, dg, dq, gp, outy, outz, outg,
     LT, RH, YS, YR, YRT, YLT, ZRT, ZLT, ZX,
     own_sem, xs, xr, ys_s, ys_r, yr_s, yr_r, yl_s, yl_r, zr_s, zr_r, zl_s, zl_r,
     zx_s, zx_r, ag_s, ag_r, sib_s, sib_r, lo,
+    GC, GA, GS, GR, GL, gc_sem, ga_s, ga_r, gr_sem, gl_sem,
 ):
     G, A, T = plan["groups"], plan["pairs"], plan["tokens"]
     width, hidden, half = plan["width"], plan["hidden"], plan["half"]
@@ -416,7 +417,78 @@
     def live(index, count):
         return (index >= 0) & (index < count)
 
+    def gain_core():
+        return remote(gp, GC, gc_sem.at[0], gc_sem.at[1], sib)
+
+    def gain_part(k):
+        return remote(GA.at[a], GA.at[a], ga_s.at[k - 1], ga_r.at[k - 1], peer(k))
+
+    def gain_right():
+        return remote(GS.at[1], GR, gr_sem.at[0], gr_sem.at[1], right)
+
+    def gain_left():
+        return remote(GS.at[2], GL, gl_sem.at[0], gl_sem.at[1], left)
+
+    def gain_step(t):
+        @pl.when(t == 0)
+        def _():
+            gain_core().start()
+
+        @pl.when(t == 1)
+        def _():
+            gain_core().wait_recv()
+            GA[a] = gp[...] + GC[...]
+            for k in range(1, A):
+                gain_part(k).start()
+
+        @pl.when(t == 2)
+        def _():
+            for k in range(1, A):
+                remote(
+                    GA.at[lax.rem(a + A - k, A)], GA.at[lax.rem(a + A - k, A)], ga_s.at[k - 1], ga_r.at[k - 1], peer(k)
+                ).wait_recv()
+            total = GA[0]
+            for k in range(1, A):
+                total += GA[k]
+            GS[0] = total
+
+        @pl.when(t == 2 + HOP * z)
+        def _():
+            @pl.when(z > 0)
+            def _():
+                gain_right().wait_recv()
+                GS[1] = GS[0] + GR[...]
+
+            @pl.when(z == 0)
+            def _():
+                GS[1] = GS[0]
+
+            @pl.when(z < G - 1)
+            def _():
+                gain_right().start()
+
+        @pl.when(t == 2 + HOP * (G - 1 - z))
+        def _():
+            @pl.when(z < G - 1)
+            def _():
+                gain_left().wait_recv()
+                GS[2] = GS[0] + GL[...]
+
+            @pl.when(z == G - 1)
+            def _():
+                GS[2] = GS[0]
+
+            @pl.when(z > 0)
+            def _():
+                gain_left().start()
+
+        @pl.when(t == 3 + HOP * (G - 1))
+        def _():
+            outg[...] = GS[1] + jnp.where(z < G - 1, GL[...], 0.0)
+
     def step(t, carry):
+        gain_step(t)
+
         @pl.when(t == 0)
         def _():
             operands_here(0)
@@ -582,6 +654,18 @@
     steps = max(nY, nZ) + 2 * LEAD + HOP * (G - 1)
     lax.fori_loop(0, steps, step, 0)
 
+    gain_core().wait_send()
+    for k in range(1, A):
+        gain_part(k).wait_send()
+
+    @pl.when(z < G - 1)
+    def _():
+        gain_right().wait_send()
+
+    @pl.when(z > 0)
+    def _():
+        gain_left().wait_send()
+
     for i in range(4):
         for side in (0, 1):
             cross[side, i].wait_send()
@@ -620,7 +704,7 @@
     lax.fori_loop(0, nZ, drain_z, 0)
 
 
-def summed_grads(groups, dp, at, ot, n2t, n1t, dz, dy, dg, dq):
+def summed_grads(groups, dp, at, ot, n2t, n1t, dz, dy, dg, dq, gain_parts):
     hidden, tokens = at.shape
     width, qkv_cols = ot.shape[0], dq.shape[1]
     plan = grad_plan(groups, dp, tokens, width, hidden, qkv_cols)
@@ -628,14 +712,16 @@
     block, zr, zc = plan["block"], plan["z_rows"], plan["z_cols"]
     bf16, DMA = jnp.bfloat16, pltpu.SemaphoreType.DMA
     any_space = pl.BlockSpec(memory_space=pl.ANY)
+    in_vmem, f32, gain_shape = pl.BlockSpec(memory_space=pltpu.VMEM), jnp.float32, gain_parts.shape
     return pl.pallas_call(
         functools.partial(grad_kernel, plan),
         out_shape=(
             jax.ShapeDtypeStruct((block, 2 * hidden + qkv_cols), bf16),
             jax.ShapeDtypeStruct((plan["down_block"] + block, width), bf16),
+            jax.ShapeDtypeStruct(gain_parts.shape, f32),
         ),
-        in_specs=[any_space] * 8,
-        out_specs=(any_space, any_space),
+        in_specs=[any_space] * 8 + [in_vmem],
+        out_specs=(any_space, any_space, in_vmem),
         scratch_shapes=[
             pltpu.VMEM((hidden + 3 * width, 2 * tokens), bf16),
             pltpu.VMEM((2 * tokens, width + hidden + qkv_cols // 2), bf16),
@@ -654,6 +740,12 @@
             DMA((nY, A - 1)), DMA((nY, A - 1)),
             DMA((nY + nZ, A)), DMA((nY + nZ, A)),
             DMA((nY + nZ,)),
+            pltpu.VMEM(gain_shape, f32),
+            pltpu.VMEM((A,) + gain_shape, f32),
+            pltpu.VMEM((3,) + gain_shape, f32),
+            pltpu.VMEM(gain_shape, f32),
+            pltpu.VMEM(gain_shape, f32),
+            DMA((2,)), DMA((max(A - 1, 1),)), DMA((max(A - 1, 1),)), DMA((2,)), DMA((2,)),
         ],
         compiler_params=pltpu.CompilerParams(
             collective_id=3, has_side_effects=True, vmem_limit_bytes=63 * 1024 * 1024
@@ -662,23 +754,220 @@
             flops=2 * 2 * tokens * (width * (2 * hidden + qkv_cols + width) + hidden * width) // 2,
             bytes_accessed=40_000_000, transcendentals=0,
         ),
-    )(at, ot, n2t, n1t, dz, dy, dg, dq)
+    )(at, ot, n2t, n1t, dz, dy, dg, dq, gain_parts)
+
+
+W_HOP = 2
+gather_families = (
+    (1, True, False),
+    (2, True, True),
+    (1, True, False),
+    (8, True, False),
+    (4, False, False),
+)
+
+
+def gather_kernel(groups, pairs, families, *refs):
+    G, A, F = groups, pairs, len(families)
+    shards, wholes = refs[:F], refs[F : 2 * F]
+    sems = refs[2 * F :]
+    s, z, d = lax.axis_index("section"), lax.axis_index("group"), lax.axis_index("dp")
+    c, a = lax.rem(d, 2), lax.div(d, 2)
+    sib = (s, z, 2 * a + 1 - c)
+    right, left = (s, z + 1, d), (s, z - 1, d)
+
+    def peer(part):
+        return (s, z, 2 * part + c)
+
+    barrier = pltpu.get_barrier_semaphore()
+    others = [peer(lax.rem(a + k, A)) for k in range(1, A)]
+    for dev in [sib, (s, lax.rem(z + 1, G), d), (s, lax.rem(z + G - 1, G), d)] + others:
+        pl.semaphore_signal(barrier, inc=1, device_id=dev, device_id_type=MESH)
+    pl.semaphore_wait(barrier, A + 2)
+
+    def cut(f, ref, i):
+        pieces, by_columns, _ = families[f]
+        rows, cols = ref.shape
+        if pieces == 1:
+            return ref
+        if by_columns:
+            size = cols // pieces
+            return ref.at[:, pl.ds(pl.multiple_of(i * size, 128), size)]
+        size = rows // pieces
+        return ref.at[pl.ds(pl.multiple_of(i * size, 16), size), :]
+
+    def placed(f, i, o, part, core):
+        return cut(f, wholes[f].at[(o * A + part) * 2 + core], i)
+
+    def copy(f, i, o, part, kind, index, dev, own=False, core=None):
+        core = c if core is None else core
+        there = placed(f, i, o, part, core)
+        src = cut(f, shards[f], i) if own else there
+        send, recv = sems[f * 9 + 2 * kind], sems[f * 9 + 2 * kind + 1]
+        return pltpu.make_async_remote_copy(
+            src_ref=src, dst_ref=there, send_sem=send.at[index], recv_sem=recv.at[index], device_id=dev, device_id_type=MESH
+        )
+
+    def to_right(f, i, o, part, own=False):
+        return copy(f, i, o, part, 0, (i, o, lax.rem(part + A - a, A)), right, own)
+
+    def to_left(f, i, o, part, own=False):
+        return copy(f, i, o, part, 1, (i, o, lax.rem(part + A - a, A)), left, own)
+
+    def to_part(f, i, o, k, own=False):
+        return copy(f, i, o, a, 2, (i, o, k - 1), peer(lax.rem(a + k, A)), own)
+
+    def from_part(f, i, o, k):
+        return copy(f, i, o, lax.rem(a + A - k, A), 2, (i, o, k - 1), peer(lax.rem(a + A - k, A)))
+
+    def to_core(f, i, o, part, own=False):
+        return copy(f, i, o, part, 3, (i, o, lax.rem(part + A - a, A)), sib, own)
+
+    def from_core(f, i, o, k):
+        part = lax.rem(a + k, A)
+        return copy(f, i, o, part, 3, (i, o, k), sib, core=1 - c)
+
+    def own_copy(f, i):
+        return pltpu.make_async_copy(cut(f, shards[f], i), placed(f, i, z, a, c), sems[f * 9 + 8].at[i])
+
+    def along(f, i, o, part, own, go_right, go_left):
+        if go_right:
+            @pl.when(z < G - 1)
+            def _():
+                to_right(f, i, o, part, own).start()
+        if go_left:
+            @pl.when(z > 0)
+            def _():
+                to_left(f, i, o, part, own).start()
+
+    first = []
+    total = 0
+    for pieces, _, _ in families:
+        first.append(total)
+        total += pieces
+
+    def step(t, carry):
+        for f, (pieces, _, parts_first) in enumerate(families):
+            i0 = t - first[f]
+
+            @pl.when((i0 >= 0) & (i0 < pieces))
+            def _(f=f, i0=i0):
+                along(f, i0, z, a, True, True, True)
+                for k in range(1, A):
+                    to_part(f, i0, z, k, True).start()
+                to_core(f, i0, z, a, True).start()
+                own_copy(f, i0).start()
+
+        for f, (pieces, _, parts_first) in enumerate(families):
+            for h in range(G):
+                for k in range(A if parts_first else 1):
+                    if h == 0:
+                        continue
+                    i = t - first[f] - W_HOP * h - (W_HOP if k > 0 else 0)
+                    part = lax.rem(a + k, A)
+                    for sign in (-1, 1):
+                        o = z + sign * h
+
+                        @pl.when((i >= 0) & (i < pieces) & (o >= 0) & (o < G))
+                        def _(f=f, i=i, o=o, part=part, sign=sign, parts_first=parts_first):
+                            if sign < 0:
+                                to_right(f, i, o, part).wait_recv()
+                                along(f, i, o, part, False, True, False)
+                            else:
+                                to_left(f, i, o, part).wait_recv()
+                                along(f, i, o, part, False, False, True)
+                            if not parts_first:
+                                for j in range(1, A):
+                                    to_part(f, i, o, j).start()
+                            to_core(f, i, o, part).start()
+
+                if parts_first and h > 0:
+                    continue
+                i = t - first[f] - W_HOP * (h + 1)
+                for sign in (-1, 1) if h else (1,):
+                    o = z + sign * h
+
+                    @pl.when((i >= 0) & (i < pieces) & (o >= 0) & (o < G))
+                    def _(f=f, i=i, o=o, parts_first=parts_first):
+                        for k in range(1, A):
+                            from_part(f, i, o, k).wait_recv()
+                            part = lax.rem(a + A - k, A)
+                            if parts_first:
+                                along(f, i, o, part, False, True, True)
+                            to_core(f, i, o, part).start()
+        return carry
+
+    lax.fori_loop(0, total + W_HOP * (G + 1), step, 0)
+
+    for f, (pieces, _, parts_first) in enumerate(families):
+        def drain(i, carry, f=f, parts_first=parts_first):
+            own_copy(f, i).wait()
+
+            def by_group(o, carry):
+                for k in range(A):
+                    part = lax.rem(a + k, A)
+                    to_core(f, i, o, part).wait_send()
+                    from_core(f, i, o, k).wait_recv()
+                    if parts_first or k == 0:
+                        @pl.when((z < G - 1) & (o <= z))
+                        def _(part=part):
+                            to_right(f, i, o, part).wait_send()
+
+                        @pl.when((z > 0) & (o >= z))
+                        def _(part=part):
+                            to_left(f, i, o, part).wait_send()
+                for k in range(1, A):
+                    if parts_first:
+                        @pl.when(o == z)
+                        def _(k=k):
+                            to_part(f, i, o, k).wait_send()
+                    else:
+                        to_part(f, i, o, k).wait_send()
+                return carry
+
+            return lax.fori_loop(0, G, by_group, carry)
+
+        lax.fori_loop(0, pieces, drain, 0)
+
+
+def gathered(groups, dp, shards, families):
+    A, DMA = dp // 2, pltpu.SemaphoreType.DMA
+    any_space = pl.BlockSpec(memory_space=pl.ANY)
+    scratch = []
+    for pieces, _, parts_first in families:
+        on_line = (pieces, groups, A if parts_first else 1)
+        scratch += [DMA(on_line)] * 4 + [DMA((pieces, groups, max(A - 1, 1)))] * 2 + [DMA((pieces, groups, A))] * 2
+        scratch += [DMA((pieces,))]
+    return pl.pallas_call(
+        functools.partial(gather_kernel, groups, A, families),
+        out_shape=tuple(jax.ShapeDtypeStruct((groups * dp,) + x.shape, x.dtype) for x in shards),
+        in_specs=[any_space] * len(shards),
+        out_specs=(any_space,) * len(shards),
+        scratch_shapes=scratch,
+        compiler_params=pltpu.CompilerParams(collective_id=5, has_side_effects=True),
+    )(*shards)
 
 
 def body(
     inputs_x, cotangent, lengths, attn_gain, qkv_weight, out_weight, ffn_gain, gate_up, down_weight
 ):
     is_first = lax.axis_index("section") == 0
-    everyone = ("group", "dp")
-    gains = lax.all_gather(jnp.concatenate([attn_gain, ffn_gain], 0), everyone)
-    gains = gains.transpose(1, 0, 2).reshape(2, -1)
+    gains = jnp.concatenate([attn_gain, ffn_gain], 0)
+    gains = jnp.pad(gains, ((0, 14), (0, -gains.shape[1] % 128)))
+    gains, qkv_all, out_all, gate_up_all, down_all = gathered(
+        lax.axis_size("group"),
+        lax.axis_size("dp"),
+        (gains, qkv_weight[0], out_weight[0], gate_up[0], down_weight[0]),
+        gather_families,
+    )
+    gain_part = attn_gain.shape[1]
     weights = (
-        gains[0],
-        lax.all_gather(qkv_weight[0], everyone, axis=0, tiled=True),
-        lax.all_gather(out_weight[0], everyone, axis=0, tiled=True),
-        gains[1],
-        lax.all_gather(gate_up[0], everyone, axis=0, tiled=True),
-        lax.all_gather(down_weight[0], everyone, axis=0, tiled=True),
+        gains[:, 0, :gain_part].reshape(-1),
+        flat(qkv_all),
+        flat(out_all),
+        gains[:, 1, :gain_part].reshape(-1),
+        flat(gate_up_all),
+        flat(down_all),
     )
     inputs_f = inputs_x.astype(jnp.float32)
     cotangent_f = cotangent.astype(jnp.float32)
@@ -689,6 +978,7 @@
     section_out = result.astype(jnp.bfloat16)[None]
     second_dx, _ = backward_layer(weights, kept_state, cotangent_f)
     recv_grad = passed_along(second_dx.astype(jnp.bfloat16), "section", -1)
+    recv_grad, section_out = lax.optimization_barrier((recv_grad, section_out))
     grad_in = jnp.where(is_first, recv_grad.astype(jnp.float32), cotangent_f)
     grad_x, operands = backward_layer(weights, kept_state, grad_in)
     input_grads = jnp.where(
@@ -696,8 +986,8 @@
     )[None]
     (_, _, normed_one, _, _, _, _, attention_result, _, _, normed_two, _, hidden, _) = kept_state
     attn_gain_part, ffn_gain_part, grad_low, grad_gated, gradient_after_lowered, grad_qkv = operands
-    gain_parts = lax.all_gather(jnp.stack([attn_gain_part, ffn_gain_part]), ("group", "dp"))
-    gate_qkv_sum, down_out_sum = summed_grads(
+    gain_parts = jnp.pad(jnp.stack([attn_gain_part, ffn_gain_part]), ((0, 6), (0, 0)))
+    gate_qkv_sum, down_out_sum, gain_sums = summed_grads(
         lax.axis_size("group"),
         lax.axis_size("dp"),
         turned(hidden),
@@ -708,10 +998,11 @@
         flat(gradient_after_lowered),
         flat(grad_gated),
         flat(grad_qkv),
+        gain_parts,
     )
     gain_cols = attn_gain.shape[1] * lax.axis_size("dp")
     gain_sums = lax.dynamic_slice_in_dim(
-        jnp.sum(gain_parts, 0), lax.axis_index("group") * gain_cols, gain_cols, 1
+        gain_sums, lax.axis_index("group") * gain_cols, gain_cols, 1
     )
     gate_width = gate_up.shape[2]
     down_rows = down_weight.shape[1] * lax.axis_size("dp")

time: 979 us -> 893 us (0.912)
  waiting for transfers between devices: 346 us -> 17.2 us
  Pallas kernels: 313 us -> 607 us
  blocking collectives: 42.6 us -> 0 us
  between operations: 15.2 us -> 2.09 us
    all_gather x4 -> x0, waiting for transfers between devices: 313 us -> none  [the longest x1 125 us: body(): lax.all_gather(gate_up[0], everyone, axis=0, tiled=True)]
    pallas_call x0 -> x1, Pallas kernels: none -> 291 us  [gathered(): pl.pallas_call(functools.partial(gather_kernel, groups, A, families), out...]
    all_gather x2 -> x0, blocking collectives: 42.6 us -> none  [the longest x1 23.1 us: body(): gains = lax.all_gather(jnp.concatenate([attn_gain, ffn_gain], 0), everyone)]
    ppermute x2, waiting for transfers between devices: 29.8 us -> 17.2 us  [passed_along(): return lax.ppermute(value, axis, pairs)]
  transfers between devices with their start and end apart: 6 -> 2, of which waited for: 6 -> 1; matrix products, arithmetic and copies ran while one was open for 4% -> 2% of each run, Pallas kernels for 0% -> 0%
where the time goes in v3:
time: 893 us; the launch traced here: 883 us
  Pallas kernels  607 us (68%)
  matrix products  149 us (17%)
  local copies, waits for them, and re-layouts  52.4 us (6%)
  other arithmetic  50.6 us (6%)
  waiting for transfers between devices  17.2 us (2%)
    pallas_call x1, Pallas kernels, summed_grads(): pl.pallas_call(functools.partial(grad_kernel, plan), out_shape=(jax.Shape...  316 us
    pallas_call x1, Pallas kernels, gathered(): pl.pallas_call(functools.partial(gather_kernel, groups, A, families), out...  291 us
    dot_general x2, matrix products, backward_layer(): jnp.einsum('rse,de->rsd', grad_gated, gate_up_w, preferred_element_type=j...  29 us
    dot_general x2, matrix products, forward_layer(): jnp.einsum('rsd,de->rse', normed_two, gate_up_w, preferred_element_type=j...  28.2 us
    dot_general x2, matrix products, backward_layer(): jnp.einsum('rsd,fd->rsf', grad_low, down_w, preferred_element_type=jnp.fl...  22 us
    broadcast_in_dim x4, other arithmetic, body(): shard_sum[None]  19 us
    dot_general x2, matrix products, forward_layer(): jnp.einsum('rsf,fd->rsd', hidden, down_w, preferred_element_type=jnp.floa...  18.1 us
  transfers between devices with their start and end apart: 2, of which 1 were waited for; matrix products, arithmetic and copies ran while one was open for 2% of the time, Pallas kernels for 0%

profile of v3, /device:TPU:0, one launch (start us, length us, event | category | flops | bytes accessed | tf_op | source)
XLA Modules:
  0.0 882.8 jit_solution(8100069636182642057)
XLA Ops:
  2.0 291.1 %shard_map.152 = (bf16[16,16,128]{2,1,0:T(8,128)(2,1)}, bf16[16,96,3072]{2,1,0:T(8,128)(2,1)}, bf16[16,96,1536]{2,1,0:T(8,128)(2,1)}, bf16[16,96,8192]{2,1,0:T(8,128)(2,1)}, bf16[16,256,1536]{2,1,0:T(8,128)(2,1)}) custom-call(bf16[16,128]{1,0:T(8,128)(2,1)} %fusion.75.refs_0_, bf16[96,3072]{1,0:T(8,128)(2,1)} %bitcast.271, bf16[96,1536]{1,0:T(8,128)(2,1)} %bitcast.274, ...), custom_call_target="tpu_custom_call" | custom-call | tf_op jit(solution)/shard_map/pallas_call | solution.py:941
  294.9 5.2 fusion.52
  316.1 14.0 %fusion.51 = f32[2,128,8192]{2,1,0:T(8,128)} fusion(bf16[1536,8192,1]{1,0,2:T(8,128)(2,1)} %bitcast.280, f32[2,128,1536]{2,1,0:T(8,128)S(1)} %get-tuple-element.71, f32[1536]{0:T(1024)S(1)} %copy-done.37, f32[2,128]{1,0:T(2,128)S(1)} %add_rsqrt_fusion.2), kind=kOutput, calls=%fused_computation.110 | convolution fusion | flops 6443630592 | bytes 35134464 | tf_op jit(solution)/shard_map/rsd,de->rse/dot_general | solution.py:116
  330.2 8.1 fusion.14
  338.3 3.4 collective-permute-start
  341.8 17.2 %collective-permute-done = bf16[2,128,1536]{2,1,0:T(8,128)(2,1)S(1)} collective-permute-done((bf16[2,128,1536]{2,1,0:T(8,128)(2,1)}, bf16[2,128,1536]{2,1,0:T(8,128)(2,1)S(1)}, u32[]{:S(2)}, u32[]{:S(2)}) %collective-permute-start) | collective-permute-done | bytes 786464 | tf_op jit(solution)/shard_map/ppermute | solution.py:24
  360.2 5.4 fusion.93
  378.2 14.2 %fusion.94 = f32[2,128,8192]{2,1,0:T(8,128)} fusion(bf16[2,128,1536]{2,1,0:T(8,128)(2,1)S(1)} %multiply_convert_fusion.5, bf16[1536,8192,1]{1,0,2:T(8,128)(2,1)} %bitcast.281), kind=kOutput, calls=%fused_computation.199 | convolution fusion | flops 6442450944 | bytes 34340864 | tf_op jit(solution)/shard_map/rsd,de->rse/dot_general | solution.py:116
  392.4 11.1 %multiply_convert_fusion.4 = (bf16[2,128,4096]{2,1,0:T(8,128)(2,1)}, bf16[2,128,4096]{2,1,0:T(8,128)(2,1)}, bf16[2,128,4096]{2,1,0:T(8,128)(2,1)}) fusion(f32[2,128,8192]{2,1,0:T(8,128)} %fusion.94, bf16[4096,1536,1]{1,0,2:T(8,128)(2,1)} %bitcast.284, bf16[2,128,1536]{2,1,0:T(8,128)(2,1)S(1)} %copy-done.11, f32[2,128]{1,0:T(2,128)S(1)} %copy-done.47), kind=kOutput, calls=%fused_computation.16 | convolution fusion | flops 3238133760 | bytes 28050432 | tf_op jit(solution)/shard_map/rsd,fd->rsf/dot_general | solution.py:165
  403.5 14.3 %multiply_reduce_fusion.5 = (f32[2,128]{1,0:T(2,128)S(1)}, f32[2,128,1536]{2,1,0:T(8,128)}) fusion(f32[2,128,1536]{2,1,0:T(8,128)S(1)} %get-tuple-element.75, f32[1536]{0:T(1024)S(1)} %copy-done.38, bf16[1536,8192,1]{1,0,2:T(8,128)(2,1)} %bitcast.282, bf16[2,128,4096]{2,1,0:T(8,128)(2,1)} %get-tuple-element.39, bf16[2,128,4096]{2,1,0:T(8,128)(2,1)} %get-tuple-element.38), kind=kOutput, calls=%fused_computation.85 | convolution fusion | flops 6452019200 | bytes 32513024 | tf_op jit(solution)/shard_map/rse,de->rsd/dot_general | solution.py:172
  418.4 4.1 convolution_convert_fusion.1
  424.8 2.7 fusion.47
  442.9 7.2 multiply_reduce_fusion.4
  453.3 4.3 copy.111
  465.2 9.9 %fusion.16 = bf16[1,2,128,1536]{3,2,1,0:T(8,128)(2,1)} fusion(f32[2,128,1536]{2,1,0:T(8,128)} %copy-done.1, bf16[2,128,4096]{2,1,0:T(8,128)(2,1)} %get-tuple-element.40, bf16[4096,1536,1]{1,0,2:T(8,128)(2,1)} %bitcast.285, f32[2,128]{1,0:T(2,128)} %get-tuple-element.67), kind=kOutput, calls=%fused_computation.36 | convolution fusion | flops 3222405120 | bytes 17040384 | tf_op jit(solution)/shard_map/rsf,fd->rsd/dot_general | solution.py:118
  476.6 10.9 %multiply_convert_fusion.1 = (bf16[2,128,4096]{2,1,0:T(8,128)(2,1)}, bf16[2,128,4096]{2,1,0:T(8,128)(2,1)}) fusion(f32[2,128,8192]{2,1,0:T(8,128)} %fusion.94, bf16[2,128,1536]{2,1,0:T(8,128)(2,1)S(1)} %fusion.42, bf16[4096,1536,1]{1,0,2:T(8,128)(2,1)} %bitcast.286), kind=kOutput, calls=%fused_computation.13 | convolution fusion | flops 3234856960 | bytes 25952256 | tf_op jit(solution)/shard_map/rsd,fd->rsf/dot_general | solution.py:165
  487.5 14.7 %multiply_reduce_fusion = (f32[1536]{0:T(1024)}, f32[2,128]{1,0:T(2,128)S(1)}, f32[2,128,1536]{2,1,0:T(8,128)}) fusion(f32[2,128,1536]{2,1,0:T(8,128)S(1)} %copy-done.3, f32[2,128]{1,0:T(2,128)S(1)} %copy-done.45, f32[1536]{0:T(1024)S(1)} %copy-done.38, bf16[1536,8192,1]{1,0,2:T(8,128)(2,1)} %bitcast.283, bf16[2,128,4096]{2,1,0:T(8,128)(2,1)} %get-tuple-element.37, ...), kind=kOutput, calls=%fused_computation.76 | convolution fusion | flops 6453196800 | bytes 32520192 | tf_op jit(solution)/shard_map/rse,de->rsd/dot_general | solution.py:172
  502.3 3.6 fusion.89
  511.4 2.8 fusion.48
  531.8 8.3 multiply_reduce_fusion.1
  544.4 315.8 %shard_map.153 = (bf16[384,11264]{1,0:T(8,128)(2,1)}, bf16[1408,1536]{1,0:T(8,128)(2,1)}, f32[8,1536]{1,0:T(8,128)}) custom-call(bf16[4096,256]{1,0:T(8,128)(2,1)} %bitcast.252, bf16[1536,256]{1,0:T(8,128)(2,1)} %bitcast.260, bf16[1536,256]{1,0:T(8,128)(2,1)} %bitcast.261, bf16[1536,256]{1,0:T(8,128)(2,1)} %bitcast.262, bf16[256,1536]{1,0:T(8,128)(2,1)} %bitcast.264, ...), custom_call_target="tpu_custom_call" | custom-call | flops 13287555072 | bytes 40000000 | tf_op jit(solution)/shard_map/pallas_call | solution.py:716
  860.2 4.6 bitcast_convert_fusion.2
  864.8 9.2 %bitcast_convert_fusion = f32[1,384,8192]{2,1,0:T(8,128)} fusion(bf16[384,11264]{1,0:T(8,128)(2,1)} %get-tuple-element.26), kind=kLoop, calls=%fused_computation | loop fusion | flops 3145728 | bytes 18874368 | tf_op jit(solution)/shard_map/broadcast_in_dim | solution.py:1017
  875.7 3.6 bitcast_convert_fusion.1
  (241 shorter events, 94.8 us)
Async XLA Ops:
  0.6 294.1 %copy-start = (bf16[2,128,1536]{2,1,0:T(8,128)(2,1)S(1)}, bf16[2,128,1536]{2,1,0:T(8,128)(2,1)}, u32[]{:S(2)}) copy-start(bf16[2,128,1536]{2,1,0:T(8,128)(2,1)} %param.9) | copy-start | bytes 2359300
  314.5 15.6 %slice-start.9 = ((s8[12582912]{0:T(1024)(128)(4,1)}), s8[4194304]{0:T(1024)(128)(4,1)S(1)}, s32[]{:S(2)}) async-start(s8[12582912]{0:T(1024)(128)(4,1)} %bitcast.287), calls=%async_computation.9 | async-start | bytes 8388608
  316.1 14.1 %copy-start.46 = (f32[2,128]{1,0:T(2,128)S(1)}, f32[2,128]{1,0:T(2,128)}, u32[]{:S(2)}) copy-start(f32[2,128]{1,0:T(2,128)} %get-tuple-element.67) | copy-start | bytes 3076
  316.1 14.1 %slice-start.10 = ((s8[12582912]{0:T(1024)(128)(4,1)}), s8[4194304]{0:T(1024)(128)(4,1)S(1)}, s32[]{:S(2)}) async-start(s8[12582912]{0:T(1024)(128)(4,1)} %bitcast.287), calls=%async_computation.10 | async-start | bytes 8388608
  316.1 14.1 %slice-start.11 = ((s8[12582912]{0:T(1024)(128)(4,1)}), s8[4194304]{0:T(1024)(128)(4,1)S(1)}, s32[]{:S(2)}) async-start(s8[12582912]{0:T(1024)(128)(4,1)} %bitcast.287), calls=%async_computation.11 | async-start | bytes 8388608
  338.3 20.7 %collective-permute-start = (bf16[2,128,1536]{2,1,0:T(8,128)(2,1)}, bf16[2,128,1536]{2,1,0:T(8,128)(2,1)S(1)}, u32[]{:S(2)}, u32[]{:S(2)}) collective-permute-start(bf16[2,128,1536]{2,1,0:T(8,128)(2,1)} %fusion.14), channel_id=1, source_target_pairs={{0,16},{1,17},{2,18},{3,19},{4,20},{5,21},{6,22},{7,23},{8,24},{9,... | collective-permute-start | bytes 2359304 | tf_op jit(solution)/shard_map/ppermute | solution.py:24
  377.9 39.9 %copy-start.1 = (f32[2,128,1536]{2,1,0:T(8,128)}, f32[2,128,1536]{2,1,0:T(8,128)S(1)}, u32[]{:S(2)}) copy-start(f32[2,128,1536]{2,1,0:T(8,128)S(1)} %get-tuple-element.75) | copy-start | bytes 4718596
  378.0 39.9 %copy-start.43 = (f32[2,128]{1,0:T(2,128)}, f32[2,128]{1,0:T(2,128)S(1)}, u32[]{:S(2)}) copy-start(f32[2,128]{1,0:T(2,128)S(1)} %get-tuple-element.62) | copy-start | bytes 3076
  378.0 39.9 %copy-start.52 = (f32[2,128]{1,0:T(2,128)}, f32[2,128]{1,0:T(2,128)S(1)}, u32[]{:S(2)}) copy-start(f32[2,128]{1,0:T(2,128)S(1)} %get-tuple-element.61) | copy-start | bytes 3076
  378.2 14.2 %copy-start.25 = (bf16[2,128,1536]{2,1,0:T(8,128)(2,1)}, bf16[2,128,1536]{2,1,0:T(8,128)(2,1)S(1)}, u32[]{:S(2)}) copy-start(bf16[2,128,1536]{2,1,0:T(8,128)(2,1)S(1)} %multiply_convert_fusion.5) | copy-start | bytes 2359300
  378.2 14.2 %copy-start.11 = (bf16[2,128,1536]{2,1,0:T(8,128)(2,1)S(1)}, bf16[2,128,1536]{2,1,0:T(8,128)(2,1)}, u32[]{:S(2)}) copy-start(bf16[2,128,1536]{2,1,0:T(8,128)(2,1)} %param.10) | copy-start | bytes 2359300
  378.2 14.2 %copy-start.47 = (f32[2,128]{1,0:T(2,128)S(1)}, f32[2,128]{1,0:T(2,128)}, u32[]{:S(2)}) copy-start(f32[2,128]{1,0:T(2,128)} %get-tuple-element.67) | copy-start | bytes 3076
  452.0 23.1 %collective-permute-start.1 = (bf16[2,128,1536]{2,1,0:T(8,128)(2,1)}, bf16[2,128,1536]{2,1,0:T(8,128)(2,1)}, u32[]{:S(2)}, u32[]{:S(2)}) collective-permute-start(bf16[2,128,1536]{2,1,0:T(8,128)(2,1)} %add_convert_fusion), channel_id=1, source_target_pairs={{16,0},{17,1},{18,2},{19,3},{20,4},{21,5},{22,6},{23,7},{24,8},{25... | collective-permute-start | bytes 2359304 | tf_op jit(solution)/shard_map/ppermute | solution.py:24
  465.2 10.0 %copy-start.13 = (bf16[2,128,1536]{2,1,0:T(8,128)(2,1)S(1)}, bf16[2,128,1536]{2,1,0:T(8,128)(2,1)}, u32[]{:S(2)}) copy-start(bf16[2,128,1536]{2,1,0:T(8,128)(2,1)} %param.10) | copy-start | bytes 2359300
  465.2 10.0 %copy-start.49 = (f32[2,128]{1,0:T(2,128)S(1)}, f32[2,128]{1,0:T(2,128)}, u32[]{:S(2)}) copy-start(f32[2,128]{1,0:T(2,128)} %get-tuple-element.67) | copy-start | bytes 3076
  476.6 11.0 %copy-start.35 = (bf16[2,128,1536]{2,1,0:T(8,128)(2,1)}, bf16[2,128,1536]{2,1,0:T(8,128)(2,1)S(1)}, u32[]{:S(2)}) copy-start(bf16[2,128,1536]{2,1,0:T(8,128)(2,1)S(1)} %fusion.42) | copy-start | bytes 2359300
  476.6 10.9 %copy-start.3 = (f32[2,128,1536]{2,1,0:T(8,128)S(1)}, f32[2,128,1536]{2,1,0:T(8,128)}, u32[]{:S(2)}) copy-start(f32[2,128,1536]{2,1,0:T(8,128)} %copy-done.1) | copy-start | bytes 4718596
  476.6 10.9 %copy-start.45 = (f32[2,128]{1,0:T(2,128)S(1)}, f32[2,128]{1,0:T(2,128)}, u32[]{:S(2)}) copy-start(f32[2,128]{1,0:T(2,128)} %copy-done.43) | copy-start | bytes 3076
  476.6 30.2 %slice-start.4 = ((s8[4718592]{0:T(1024)(128)(4,1)}), s8[4194304]{0:T(1024)(128)(4,1)S(1)}, s32[]{:S(2)}) async-start(s8[4718592]{0:T(1024)(128)(4,1)} %bitcast.217), calls=%async_computation.4 | async-start | bytes 8388608
  487.5 14.8 %copy-start.54 = (f32[2,128]{1,0:T(2,128)S(1)}, f32[2,128]{1,0:T(2,128)}, u32[]{:S(2)}) copy-start(f32[2,128]{1,0:T(2,128)} %copy-done.52) | copy-start | bytes 3076
  487.5 19.3 %slice-start.5 = ((s8[4718592]{0:T(1024)(128)(4,1)}), s8[524288]{0:T(1024)(128)(4,1)S(1)}, s32[]{:S(2)}) async-start(s8[4718592]{0:T(1024)(128)(4,1)} %bitcast.217), calls=%async_computation.5 | async-start | bytes 1048576
  531.8 8.3 copy-start.26
  860.2 13.7 %slice-start.6 = ((s8[4325376]{0:T(1024)(128)(4,1)}), s8[4194304]{0:T(1024)(128)(4,1)S(1)}, s32[]{:S(2)}) async-start(s8[4325376]{0:T(1024)(128)(4,1)} %bitcast.234), calls=%async_computation.6 | async-start | bytes 8388608
  864.8 9.2 %slice-start.7 = ((s8[4325376]{0:T(1024)(128)(4,1)}), s8[131072]{0:T(1024)(128)(4,1)S(1)}, s32[]{:S(2)}) async-start(s8[4325376]{0:T(1024)(128)(4,1)} %bitcast.234), calls=%async_computation.7 | async-start | bytes 262144
  (49 other events, 192.2 us)

commit v4 on v3

--- a/solution.py
+++ b/solution.py
@@ -16,6 +16,7 @@
 norm_eps = 1e-05
 rope_base = 100000.0
 masked_score = -1e30
+across = (((1,), (1,)), ((), ()))
 
 
 def passed_along(value, axis, by):
@@ -79,8 +80,8 @@
     return jnp.where(allowed[:, None, None], scores, masked_score)
 
 
-def forward_layer(weights, input_rows, lengths):
-    gain_one, qkv_w, output_weight, gain_two, gate_up_w, down_w = weights
+def attention_forward(weights, input_rows, lengths):
+    gain_one, qkv_w, output_weight = weights[:3]
     row_count, slot_count, width = input_rows.shape
     groups = H // KVH
     cosines, sine_table = rope_tables(slot_count, HD)
@@ -111,14 +112,6 @@
     after_attention = input_rows + jnp.einsum(
         "vao,oj->vaj", attention_result, output_weight, preferred_element_type=jnp.float32
     )
-    scale_two = norm_scale(after_attention)
-    normed_two = (after_attention * scale_two * gain_two.astype(jnp.float32)).astype(jnp.bfloat16)
-    gated = jnp.einsum("rsd,de->rse", normed_two, gate_up_w, preferred_element_type=jnp.float32)
-    hidden = (jax.nn.silu(gated[..., :FF]) * gated[..., FF:]).astype(jnp.bfloat16)
-    result = after_attention + jnp.einsum(
-        "rsf,fd->rsd", hidden, down_w, preferred_element_type=jnp.float32
-    )
-    result = result * padding(lengths, slot_count)
     kept_state = (
         input_rows,
         scale_one,
@@ -128,18 +121,13 @@
         value_heads,
         log_total,
         attention_result,
-        after_attention,
-        scale_two,
-        normed_two,
-        gated,
-        hidden,
         lengths,
     )
-    return (result, kept_state)
-
-
-def backward_layer(weights, kept_state, grad_out):
-    gain_one, qkv_w, output_weight, gain_two, gate_up_w, down_w = weights
+    return (after_attention, kept_state)
+
+
+def attention_backward(weights, kept_state, grad_after, gradient_after_lowered):
+    gain_one, qkv_w, output_weight = weights[:3]
     (
         input_rows,
         scale_one,
@@ -149,32 +137,12 @@
         value_heads,
         log_total,
         attention_result,
-        after_attention,
-        scale_two,
-        normed_two,
-        gated,
-        hidden,
         lengths,
     ) = kept_state
     row_count, slot_count, width = input_rows.shape
     groups = H // KVH
     score_scale = HD ** (-0.5)
     cosines, sine_table = rope_tables(slot_count, HD)
-    grad_masked = grad_out * padding(lengths, slot_count)
-    grad_low = grad_masked.astype(jnp.bfloat16)
-    grad_hidden = jnp.einsum("rsd,fd->rsf", grad_low, down_w, preferred_element_type=jnp.float32)
-    gate_part = gated[..., :FF]
-    up_part = gated[..., FF:]
-    sigmoid_gate = jax.nn.sigmoid(gate_part)
-    grad_gate = grad_hidden * up_part * sigmoid_gate * (1.0 + gate_part * (1.0 - sigmoid_gate))
-    grad_up = grad_hidden * (gate_part * sigmoid_gate)
-    grad_gated = jnp.concatenate([grad_gate, grad_up], -1).astype(jnp.bfloat16)
-    grad_normed_two = jnp.einsum(
-        "rse,de->rsd", grad_gated, gate_up_w, preferred_element_type=jnp.float32
-    )
-    ffn_gain_part, grad_norm_two = norm_back(after_attention, scale_two, gain_two, grad_normed_two)
-    grad_after = grad_masked + grad_norm_two
-    gradient_after_lowered = grad_after.astype(jnp.bfloat16)
     attention_gradient = jnp.einsum(
         "vol,el->voe", gradient_after_lowered, output_weight, preferred_element_type=jnp.float32
     )
@@ -214,11 +182,145 @@
     ).astype(jnp.bfloat16)
     grad_normed_one = jnp.einsum("rse,de->rsd", grad_qkv, qkv_w, preferred_element_type=jnp.float32)
     attn_gain_part, grad_norm_one = norm_back(input_rows, scale_one, gain_one, grad_normed_one)
-    grad_inputs = grad_after + grad_norm_one
-    return (
-        grad_inputs,
-        (attn_gain_part, ffn_gain_part, grad_low, grad_gated, gradient_after_lowered, grad_qkv),
-    )
+    return (grad_after + grad_norm_one, attn_gain_part, grad_qkv)
+
+
+FF_CHUNK = 512
+across = (((1,), (1,)), ((), ()))
+
+
+def scaled_norm(value, gain):
+    scale = lax.rsqrt(jnp.mean(value * value, -1, keepdims=True) + norm_eps)
+    return scale, (value * scale * gain).astype(jnp.bfloat16)
+
+
+def ffn_forward_kernel(y, gain, mask, wg, wu, wd, out, n2, acc):
+    j = pl.program_id(0)
+
+    @pl.when(j == 0)
+    def _():
+        n2[...] = scaled_norm(y[...], gain[...])[1]
+        acc[...] = y[...]
+
+    gate = jnp.dot(n2[...], wg[...], preferred_element_type=jnp.float32)
+    up = jnp.dot(n2[...], wu[...], preferred_element_type=jnp.float32)
+    hidden = (gate / (1.0 + jnp.exp(-gate)) * up).astype(jnp.bfloat16)
+    acc[...] += jnp.dot(hidden, wd[...], preferred_element_type=jnp.float32)
+
+    @pl.when(j == pl.num_programs(0) - 1)
+    def _():
+        out[...] = (acc[...] * mask[...]).astype(jnp.bfloat16)
+
+
+def ffn_specs(tokens, width, hidden):
+    steps = hidden // FF_CHUNK
+    whole = pl.BlockSpec((tokens, width), lambda j: (0, 0))
+    row = pl.BlockSpec((1, width), lambda j: (0, 0))
+    weights = [
+        pl.BlockSpec((width, FF_CHUNK), lambda j: (0, j)),
+        pl.BlockSpec((width, FF_CHUNK), lambda j: (0, j + steps)),
+        pl.BlockSpec((FF_CHUNK, width), lambda j: (j, 0)),
+    ]
+    return steps, whole, row, weights
+
+
+def ffn_forward(y, gain, mask, gate_up_w, down_w):
+    tokens, width = y.shape
+    hidden = down_w.shape[0]
+    steps, whole, row, weights = ffn_specs(tokens, width, hidden)
+    return pl.pallas_call(
+        ffn_forward_kernel,
+        grid=(steps,),
+        out_shape=jax.ShapeDtypeStruct((tokens, width), jnp.bfloat16),
+        in_specs=[whole, row, pl.BlockSpec((tokens, 1), lambda j: (0, 0))] + weights,
+        out_specs=whole,
+        scratch_shapes=[pltpu.VMEM((tokens, width), jnp.bfloat16), pltpu.VMEM((tokens, width), jnp.float32)],
+        compiler_params=pltpu.CompilerParams(vmem_limit_bytes=40 * 1024 * 1024),
+        cost_estimate=pl.CostEstimate(
+            flops=6 * tokens * width * hidden, bytes_accessed=6 * width * hidden, transcendentals=tokens * hidden
+        ),
+    )(y, gain, mask, gate_up_w, gate_up_w, down_w)
+
+
+def ffn_backward_kernel(keep, y, dz, gain, mask, wg, wu, wd, dy, dyb, gain_grad, *rest):
+    if keep:
+        at, dgate, dup, n2t, out, n2, scale, acc, zacc = rest
+    else:
+        n2, scale, acc = rest
+    j = pl.program_id(0)
+    bf16, f32 = jnp.bfloat16, jnp.float32
+
+    @pl.when(j == 0)
+    def _():
+        r, n = scaled_norm(y[...], gain[...])
+        n2[...] = n
+        scale[...] = r
+        acc[...] = jnp.zeros_like(acc)
+        if keep:
+            n2t[...] = n.T
+            zacc[...] = y[...]
+
+    gate = jnp.dot(n2[...], wg[...], preferred_element_type=f32)
+    up = jnp.dot(n2[...], wu[...], preferred_element_type=f32)
+    grad = lax.dot_general(dz[...], wd[...], across, preferred_element_type=f32)
+    sig = 1.0 / (1.0 + jnp.exp(-gate))
+    silu = gate * sig
+    grad_gate = (grad * up * sig * (1.0 + gate * (1.0 - sig))).astype(bf16)
+    grad_up = (grad * silu).astype(bf16)
+    if keep:
+        hidden = (silu * up).astype(bf16)
+        at[...] = hidden.T
+        dgate[...] = grad_gate
+        dup[...] = grad_up
+        zacc[...] += jnp.dot(hidden, wd[...], preferred_element_type=f32)
+    acc[...] += lax.dot_general(grad_gate, wg[...], across, preferred_element_type=f32) + lax.dot_general(
+        grad_up, wu[...], across, preferred_element_type=f32
+    )
+
+    @pl.when(j == pl.num_programs(0) - 1)
+    def _():
+        value, r, grad_normed = y[...], scale[...], acc[...]
+        scaled = grad_normed * gain[...]
+        gain_grad[...] = jnp.sum(grad_normed * value * r, axis=0, keepdims=True)
+        inner = jnp.mean(value * scaled, -1, keepdims=True)
+        total = dz[...].astype(f32) + r * scaled - value * (r * r * r) * inner
+        dy[...] = total
+        dyb[...] = total.astype(bf16)
+        if keep:
+            out[...] = (zacc[...] * mask[...]).astype(bf16)
+
+
+def ffn_backward(y, dz, gain, mask, gate_up_w, down_w, keep):
+    tokens, width = y.shape
+    hidden = down_w.shape[0]
+    steps, whole, row, weights = ffn_specs(tokens, width, hidden)
+    shape, bf16, f32 = jax.ShapeDtypeStruct, jnp.bfloat16, jnp.float32
+    outs = [shape((tokens, width), f32), shape((tokens, width), bf16), shape((1, width), f32)]
+    out_specs = [whole, whole, row]
+    scratch = [pltpu.VMEM((tokens, width), bf16), pltpu.VMEM((tokens, 1), f32), pltpu.VMEM((tokens, width), f32)]
+    if keep:
+        part = pl.BlockSpec((tokens, FF_CHUNK), lambda j: (0, j))
+        outs += [
+            shape((hidden, tokens), bf16), shape((tokens, hidden), bf16), shape((tokens, hidden), bf16),
+            shape((width, tokens), bf16), shape((tokens, width), bf16),
+        ]
+        out_specs += [
+            pl.BlockSpec((FF_CHUNK, tokens), lambda j: (j, 0)), part, part,
+            pl.BlockSpec((width, tokens), lambda j: (0, 0)), whole,
+        ]
+        scratch += [pltpu.VMEM((tokens, width), f32)]
+    return pl.pallas_call(
+        functools.partial(ffn_backward_kernel, keep),
+        grid=(steps,),
+        out_shape=tuple(outs),
+        in_specs=[whole, whole, row, pl.BlockSpec((tokens, 1), lambda j: (0, 0))] + weights,
+        out_specs=tuple(out_specs),
+        scratch_shapes=scratch,
+        compiler_params=pltpu.CompilerParams(vmem_limit_bytes=48 * 1024 * 1024),
+        cost_estimate=pl.CostEstimate(
+            flops=10 * tokens * width * hidden, bytes_accessed=6 * width * hidden, transcendentals=tokens * hidden
+        ),
+    )(y, dz, gain, mask, gate_up_w, gate_up_w, down_w)
 
 
 def turned(array):
@@ -264,7 +366,7 @@
 
 
 def grad_kernel(
-    plan, at, ot, n2t, n1t, dz, dy, dg, dq, gp, outy, outz, outg,
+    plan, at, ot, n2t, n1t, dz, dy, dgate, dup, dq, gp, outy, outz, outg,
     LT, RH, YS, YR, YRT, YLT, ZRT, ZLT, ZX,
     own_sem, xs, xr, ys_s, ys_r, yr_s, yr_r, yl_s, yl_r, zr_s, zr_r, zl_s, zl_r,
     zx_s, zx_r, ag_s, ag_r, sib_s, sib_r, lo,
@@ -293,21 +395,35 @@
     pl.semaphore_wait(barrier, A + 2)
 
     lhs = [(at, 0, hidden), (ot, hidden, width), (n2t, hidden + width, width), (n1t, hidden + 2 * width, width)]
-    rhs = [(dz, 0, half), (dy, half, half), (dg, width, hidden), (dq, width + hidden, plan["qkv_cols"] // 2)]
+    rhs = [(dz, 0, half), (dy, half, half), (None, width, hidden), (dq, width + hidden, plan["qkv_cols"] // 2)]
     order = [(0, 0), (2, 2), (1, 1), (3, 3)]
     own, cross = {}, {}
     for i, (ref, row, rows) in enumerate(lhs):
         own[0, i] = pltpu.make_async_copy(ref, LT.at[pl.ds(row, rows), pl.ds(0, T)], own_sem.at[i])
         cross[0, i] = remote(ref, LT.at[pl.ds(row, rows), pl.ds(T, T)], xs.at[i], xr.at[i], sib)
     for i, (ref, col, cols) in enumerate(rhs):
+        if ref is None:
+            continue
         mine = pl.ds(pl.multiple_of(c * cols, LANES), cols)
         theirs = pl.ds(pl.multiple_of((1 - c) * cols, LANES), cols)
         own[1, i] = pltpu.make_async_copy(ref.at[:, mine], RH.at[pl.ds(0, T), pl.ds(col, cols)], own_sem.at[4 + i])
         cross[1, i] = remote(ref.at[:, theirs], RH.at[pl.ds(T, T), pl.ds(col, cols)], xs.at[4 + i], xr.at[4 + i], sib)
+    col, cols = rhs[2][1:]
+    for core, (mine, theirs) in enumerate(((dgate, dup), (dup, dgate))):
+        own[1, 2, core] = pltpu.make_async_copy(mine, RH.at[pl.ds(0, T), pl.ds(col, cols)], own_sem.at[6])
+        cross[1, 2, core] = remote(theirs, RH.at[pl.ds(T, T), pl.ds(col, cols)], xs.at[6], xr.at[6], sib)
+    own[1, 2], cross[1, 2] = own[1, 2, 0], cross[1, 2, 0]
     for i, _ in order:
         for side in (0, 1):
-            own[side, i].start()
-            cross[side, i].start()
+            if (side, i) == (1, 2):
+                for core in (0, 1):
+                    @pl.when(c == core)
+                    def _(core=core):
+                        own[1, 2, core].start()
+                        cross[1, 2, core].start()
+            else:
+                own[side, i].start()
+                cross[side, i].start()
 
     def operands_here(i):
         for side in (0, 1):
@@ -704,7 +820,7 @@
     lax.fori_loop(0, nZ, drain_z, 0)
 
 
-def summed_grads(groups, dp, at, ot, n2t, n1t, dz, dy, dg, dq, gain_parts):
+def summed_grads(groups, dp, at, ot, n2t, n1t, dz, dy, dgate, dup, dq, gain_parts):
     hidden, tokens = at.shape
     width, qkv_cols = ot.shape[0], dq.shape[1]
     plan = grad_plan(groups, dp, tokens, width, hidden, qkv_cols)
@@ -720,7 +836,7 @@
             jax.ShapeDtypeStruct((plan["down_block"] + block, width), bf16),
             jax.ShapeDtypeStruct(gain_parts.shape, f32),
         ),
-        in_specs=[any_space] * 8 + [in_vmem],
+        in_specs=[any_space] * 9 + [in_vmem],
         out_specs=(any_space, any_space, in_vmem),
         scratch_shapes=[
             pltpu.VMEM((hidden + 3 * width, 2 * tokens), bf16),
@@ -754,7 +870,7 @@
             flops=2 * 2 * tokens * (width * (2 * hidden + qkv_cols + width) + hidden * width) // 2,
             bytes_accessed=40_000_000, transcendentals=0,
         ),
-    )(at, ot, n2t, n1t, dz, dy, dg, dq, gain_parts)
+    )(at, ot, n2t, n1t, dz, dy, dgate, dup, dq, gain_parts)
 
 
 W_HOP = 2
@@ -969,34 +1085,56 @@
         flat(gate_up_all),
         flat(down_all),
     )
+    slots = inputs_x.shape[1]
     inputs_f = inputs_x.astype(jnp.float32)
-    cotangent_f = cotangent.astype(jnp.float32)
-    first_out, _ = forward_layer(weights, inputs_f, lengths)
-    recv_act = passed_along(first_out.astype(jnp.bfloat16), "section", 1)
+    mask = padding(lengths, slots)
+    mask_rows = mask.reshape(-1, 1)
+    ffn_gain_row = weights[3].astype(jnp.float32).reshape(1, -1)
+    gate_up_w, down_w = weights[4:]
+    dz_given = (cotangent.astype(jnp.float32) * mask).astype(jnp.bfloat16)
+    after_one, _ = attention_forward(weights, inputs_f, lengths)
+    first_out = ffn_forward(flat(after_one), ffn_gain_row, mask_rows, gate_up_w, down_w)
+    recv_act = passed_along(first_out, "section", 1).reshape(inputs_x.shape)
     layer_in = jnp.where(is_first, inputs_f, recv_act.astype(jnp.float32))
-    result, kept_state = forward_layer(weights, layer_in, lengths)
-    section_out = result.astype(jnp.bfloat16)[None]
-    second_dx, _ = backward_layer(weights, kept_state, cotangent_f)
+    after, kept_state = attention_forward(weights, layer_in, lengths)
+    dy, dy_low, _ = ffn_backward(
+        flat(after), flat(dz_given), ffn_gain_row, mask_rows, gate_up_w, down_w, False
+    )
+    second_dx, _, _ = attention_backward(
+        weights, kept_state, dy.reshape(inputs_x.shape), dy_low.reshape(inputs_x.shape)
+    )
     recv_grad = passed_along(second_dx.astype(jnp.bfloat16), "section", -1)
-    recv_grad, section_out = lax.optimization_barrier((recv_grad, section_out))
-    grad_in = jnp.where(is_first, recv_grad.astype(jnp.float32), cotangent_f)
-    grad_x, operands = backward_layer(weights, kept_state, grad_in)
+    normed_one, attention_result = kept_state[2], kept_state[7]
+    attention_turned, normed_turned = turned(attention_result), turned(normed_one)
+    recv_grad, attention_turned, normed_turned = lax.optimization_barrier(
+        (recv_grad, attention_turned, normed_turned)
+    )
+    dz = jnp.where(is_first, (recv_grad.astype(jnp.float32) * mask).astype(jnp.bfloat16), dz_given)
+    dz = flat(dz)
+    dy, dy_low, ffn_gain_part, hidden_turned, grad_gate, grad_up, normed_two_turned, result = ffn_backward(
+        flat(after), dz, ffn_gain_row, mask_rows, gate_up_w, down_w, True
+    )
+    grad_x, attn_gain_part, grad_qkv = attention_backward(
+        weights, kept_state, dy.reshape(inputs_x.shape), dy_low.reshape(inputs_x.shape)
+    )
+    section_out = result.reshape((1,) + inputs_x.shape)
     input_grads = jnp.where(
         is_first, grad_x, grad_x.astype(jnp.bfloat16).astype(jnp.float32)
     )[None]
-    (_, _, normed_one, _, _, _, _, attention_result, _, _, normed_two, _, hidden, _) = kept_state
-    attn_gain_part, ffn_gain_part, grad_low, grad_gated, gradient_after_lowered, grad_qkv = operands
-    gain_parts = jnp.pad(jnp.stack([attn_gain_part, ffn_gain_part]), ((0, 6), (0, 0)))
+    gain_parts = jnp.pad(
+        jnp.concatenate([attn_gain_part[None], ffn_gain_part], 0), ((0, 6), (0, 0))
+    )
     gate_qkv_sum, down_out_sum, gain_sums = summed_grads(
         lax.axis_size("group"),
         lax.axis_size("dp"),
-        turned(hidden),
-        turned(attention_result),
-        turned(normed_two),
-        turned(normed_one),
-        flat(grad_low),
-        flat(gradient_after_lowered),
-        flat(grad_gated),
+        hidden_turned,
+        attention_turned,
+        normed_two_turned,
+        normed_turned,
+        dz,
+        dy_low,
+        grad_gate,
+        grad_up,
         flat(grad_qkv),
         gain_parts,
     )

time: 893 us -> 857 us (0.960)
  matrix products: 149 us -> 50.4 us
  Pallas kernels: 607 us -> 676 us
  waiting for transfers between devices: 17.2 us -> 30.8 us
  other arithmetic: 50.6 us -> 40.3 us
    dot_general x26 -> x18, matrix products: 145 us -> 48.2 us  [the longest x2 15.2 us: attention_backward(): jnp.einsum('rse,de->rsd', grad_qkv, qkv_w, preferred_element_type=jnp.flo...]
    pallas_call x0 -> x3, Pallas kernels: none -> 69.1 us  [the longest x2 51.2 us: ffn_backward(): pl.pallas_call(functools.partial(ffn_backward_kernel, keep), grid=(steps,...]
    ppermute x2, waiting for transfers between devices: 17.2 us -> 30.8 us  [passed_along(): return lax.ppermute(value, axis, pairs)]
  transfers between devices with their start and end apart: 2 -> 2, of which waited for: 1 -> 2; matrix products, arithmetic and copies ran while one was open for 2% -> 1% of each run, Pallas kernels for 0% -> 0%
where the time goes in v4:
time: 857 us; the launch traced here: 848 us
  Pallas kernels  676 us (79%)
  matrix products  50.4 us (6%)
  local copies, waits for them, and re-layouts  44.8 us (5%)
  other arithmetic  40.3 us (5%)
  waiting for transfers between devices  30.8 us (4%)
    pallas_call x1, Pallas kernels, summed_grads(): pl.pallas_call(functools.partial(grad_kernel, plan), out_shape=(jax.Shape...  315 us
    pallas_call x1, Pallas kernels, gathered(): pl.pallas_call(functools.partial(gather_kernel, groups, A, families), out...  291 us
    pallas_call x2, Pallas kernels, ffn_backward(): pl.pallas_call(functools.partial(ffn_backward_kernel, keep), grid=(steps,...  51.2 us
    ppermute x2, waiting for transfers between devices, passed_along(): return lax.ppermute(value, axis, pairs)  30.8 us
    broadcast_in_dim x4, other arithmetic, body(): shard_sum[None]  19 us
    pallas_call x1, Pallas kernels, ffn_forward(): pl.pallas_call(ffn_forward_kernel, grid=(steps,), out_shape=jax.ShapeDtyp...  18 us
  transfers between devices with their start and end apart: 2, of which 2 were waited for; matrix products, arithmetic and copies ran while one was open for 1% of the time, Pallas kernels for 0%

profile of v4, /device:TPU:0, one launch (start us, length us, event | category | flops | bytes accessed | tf_op | source)
XLA Modules:
  0.0 848.4 jit_solution(17661334418010130889)
XLA Ops:
  1.9 291.1 %shard_map.152 = (bf16[16,16,128]{2,1,0:T(8,128)(2,1)}, bf16[16,96,3072]{2,1,0:T(8,128)(2,1)}, bf16[16,96,1536]{2,1,0:T(8,128)(2,1)}, bf16[16,96,8192]{2,1,0:T(8,128)(2,1)}, bf16[16,256,1536]{2,1,0:T(8,128)(2,1)}) custom-call(bf16[16,128]{1,0:T(8,128)(2,1)} %fusion.46.refs_0_, bf16[96,3072]{1,0:T(8,128)(2,1)} %bitcast.274, bf16[96,1536]{1,0:T(8,128)(2,1)} %bitcast.277, ...), custom_call_target="tpu_custom_call" | custom-call | tf_op jit(solution)/shard_map/pallas_call | solution.py:1057
  294.3 5.2 fusion.29
  302.5 1.9 copy.59
  313.5 18.0 %shard_map.153 = bf16[256,1536]{1,0:T(8,128)(2,1)S(1)} custom-call(f32[256,1536]{1,0:T(8,128)S(1)} %bitcast.204, f32[1,1536]{1,0:T(1,128)S(1)} %reshape.388.gain, f32[256,1]{1,0:T(8,128)S(1)} %copy.62.mask, bf16[1536,8192]{1,0:T(8,128)(2,1)} %bitcast.212, bf16[1536,8192]{1,0:T(8,128)(2,1)} %bitcast.213, bf16[4096,1536]{1,0:T(8,128)(2,1)} %bitcast.218), custom_call_target="tpu_custom_call" | custom-call | flops 9663676416 | bytes 37748736 | tf_op jit(solution)/shard_map/pallas_call | solution.py:231
  331.5 3.6 collective-permute-start
  336.5 15.4 %collective-permute-done = bf16[256,1536]{1,0:T(8,128)(2,1)S(1)} collective-permute-done((bf16[256,1536]{1,0:T(8,128)(2,1)S(1)}, bf16[256,1536]{1,0:T(8,128)(2,1)S(1)}, u32[]{:S(2)}, u32[]{:S(2)}) %collective-permute-start) | collective-permute-done | bytes 786464 | tf_op jit(solution)/shard_map/ppermute | solution.py:25
  352.8 5.4 fusion.59
  371.6 3.9 convolution_add_fusion
  375.5 23.5 %shard_map.154 = (f32[256,1536]{1,0:T(8,128)S(1)}, bf16[256,1536]{1,0:T(8,128)(2,1)S(1)}, f32[1,1536]{1,0:T(1,128)}) custom-call(f32[256,1536]{1,0:T(8,128)S(1)} %bitcast.202, bf16[256,1536]{1,0:T(8,128)(2,1)S(1)} %bitcast.207, f32[1,1536]{1,0:T(1,128)S(1)} %reshape.388.gain, f32[256,1]{1,0:T(8,128)S(1)} %copy.62.mask, bf16[1536,8192]{1,0:T(8,128)(2,1)} %bitcast.214, ...), custom_call_target="tpu_custom_call" | custom-call | flops 16106127360 | bytes 37748736 | tf_op jit(solution)/shard_map/pallas_call | solution.py:312
  400.1 2.3 convolution_convert_fusion.1
  404.0 2.5 fusion.3
  414.7 1.9 copy.74
  416.6 1.9 copy.75
  418.5 7.1 multiply_reduce_fusion.2
  428.3 2.0 copy.76
  432.5 15.4 %collective-permute-done.1 = bf16[2,128,1536]{2,1,0:T(8,128)(2,1)} collective-permute-done((bf16[2,128,1536]{2,1,0:T(8,128)(2,1)}, bf16[2,128,1536]{2,1,0:T(8,128)(2,1)}, u32[]{:S(2)}, u32[]{:S(2)}) %collective-permute-start.1) | collective-permute-done | bytes 786464 | tf_op jit(solution)/shard_map/ppermute | solution.py:25
  449.5 27.7 %shard_map.155 = (f32[256,1536]{1,0:T(8,128)S(1)}, bf16[256,1536]{1,0:T(8,128)(2,1)S(1)}, f32[1,1536]{1,0:T(1,128)S(1)}, bf16[4096,256]{1,0:T(8,128)(2,1)}, bf16...) custom-call(f32[256,1536]{1,0:T(8,128)S(1)} %bitcast.203, ...), custom_call_target="tpu_custom_call" | custom-call | flops 16106127360 | bytes 37748736 | tf_op jit(solution)/shard_map/pallas_call | solution.py:312
  479.2 4.0 convolution_convert_fusion
  484.3 2.3 fusion
  497.2 8.1 multiply_reduce_fusion
  510.8 315.4 %shard_map.156 = (bf16[384,11264]{1,0:T(8,128)(2,1)}, bf16[1408,1536]{1,0:T(8,128)(2,1)}, f32[8,1536]{1,0:T(8,128)}) custom-call(bf16[4096,256]{1,0:T(8,128)(2,1)} %get-tuple-element.40.at, bf16[1536,256]{1,0:T(8,128)(2,1)} %bitcast.266, bf16[1536,256]{1,0:T(8,128)(2,1)} %copy-done.6, bf16[1536,256]{1,0:T(8,128)(2,1)} %bitcast.267, ...), custom_call_target="tpu_custom_call" | custom-call | flops 13287555072 | bytes 40000000 | tf_op jit(solution)/shard_map/pallas_call | solution.py:832
  826.1 9.1 %bitcast_convert_fusion = f32[1,384,8192]{2,1,0:T(8,128)} fusion(bf16[384,11264]{1,0:T(8,128)(2,1)} %get-tuple-element.48), kind=kLoop, calls=%fused_computation | loop fusion | flops 3145728 | bytes 18874368 | tf_op jit(solution)/shard_map/broadcast_in_dim | solution.py:1155
  835.3 4.6 bitcast_convert_fusion.2
  839.8 3.6 bitcast_convert_fusion.1
  (188 shorter events, 70.9 us)
Async XLA Ops:
  1.9 292.1 %copy-start.10 = (bf16[2,128,1536]{2,1,0:T(8,128)(2,1)S(1)}, bf16[2,128,1536]{2,1,0:T(8,128)(2,1)}, u32[]{:S(2)}) copy-start(bf16[2,128,1536]{2,1,0:T(8,128)(2,1)} %param.9) | copy-start | bytes 2359300
  306.9 5.1 slice-start
  309.4 2.6 slice-start.1
  331.5 20.4 %collective-permute-start = (bf16[256,1536]{1,0:T(8,128)(2,1)S(1)}, bf16[256,1536]{1,0:T(8,128)(2,1)S(1)}, u32[]{:S(2)}, u32[]{:S(2)}) collective-permute-start(bf16[256,1536]{1,0:T(8,128)(2,1)S(1)} %shard_map.153), channel_id=1, source_target_pairs={{0,16},{1,17},{2,18},{3,19},{4,20},{5,21},{6,22},{7,23},{8,24},{9,... | collective-permute-start | bytes 2359304 | tf_op jit(solution)/shard_map/ppermute | solution.py:25
  352.8 5.4 copy-start.34
  364.0 3.0 copy-start.24
  364.0 3.0 copy-start.27
  371.1 4.4 copy-start.20
  371.6 28.5 %slice-start.2 = ((s8[4718592]{0:T(1024)(128)(4,1)}), s8[4194304]{0:T(1024)(128)(4,1)S(1)}, s32[]{:S(2)}) async-start(s8[4718592]{0:T(1024)(128)(4,1)} %bitcast.226), calls=%async_computation.2 | async-start | bytes 8388608
  375.5 24.6 %slice-start.3 = ((s8[4718592]{0:T(1024)(128)(4,1)}), s8[524288]{0:T(1024)(128)(4,1)S(1)}, s32[]{:S(2)}) async-start(s8[4718592]{0:T(1024)(128)(4,1)} %bitcast.226), calls=%async_computation.3 | async-start | bytes 1048576
  412.6 5.9 copy-start.14
  418.5 7.1 copy-start.4
  427.0 20.9 %collective-permute-start.1 = (bf16[2,128,1536]{2,1,0:T(8,128)(2,1)}, bf16[2,128,1536]{2,1,0:T(8,128)(2,1)}, u32[]{:S(2)}, u32[]{:S(2)}) collective-permute-start(bf16[2,128,1536]{2,1,0:T(8,128)(2,1)} %add_convert_fusion), channel_id=1, source_target_pairs={{16,0},{17,1},{18,2},{19,3},{20,4},{21,5},{22,6},{23,7},{24,8},{25... | collective-permute-start | bytes 2359304 | tf_op jit(solution)/shard_map/ppermute | solution.py:25
  428.3 3.0 copy-start.35
  431.3 16.6 %copy-start.36 = (bf16[2,128,1536]{2,1,0:T(8,128)(2,1)S(1)}, bf16[2,128,1536]{2,1,0:T(8,128)(2,1)}, u32[]{:S(2)}) copy-start(bf16[2,128,1536]{2,1,0:T(8,128)(2,1)} %param.10) | copy-start | bytes 2359300
  449.5 27.7 %copy-start = (bf16[2,128,1536]{2,1,0:T(8,128)(2,1)}, bf16[2,128,1536]{2,1,0:T(8,128)(2,1)S(1)}, u32[]{:S(2)}) copy-start(bf16[2,128,1536]{2,1,0:T(8,128)(2,1)S(1)} %fusion.28) | copy-start | bytes 2359300
  479.2 4.0 copy-start.5
  493.9 3.3 copy-start.11
  494.0 3.3 copy-start.15
  505.3 2.7 copy-start.30
  835.3 4.6 copy-start.23
  839.8 6.7 copy-start.43
  843.4 3.1 copy-start.2
  843.4 3.1 copy-start.16
  (31 other events, 43.2 us)

commit v5 on v4

--- a/solution.py
+++ b/solution.py
@@ -873,7 +873,7 @@
     )(at, ot, n2t, n1t, dz, dy, dgate, dup, dq, gain_parts)
 
 
-W_HOP = 2
+W_HOP = 5
 gather_families = (
     (1, True, False),
     (2, True, True),

time: 857 us -> 832 us (0.971)
  Pallas kernels: 676 us -> 650 us
    pallas_call x1, Pallas kernels: 291 us -> 267 us  [gathered(): pl.pallas_call(functools.partial(gather_kernel, groups, A, families), out...]
where the time goes in v5:
time: 832 us; the launch traced here: 823 us
  Pallas kernels  650 us (78%)
  matrix products  50.4 us (6%)
  local copies, waits for them, and re-layouts  44.9 us (5%)
  other arithmetic  40.3 us (5%)
  waiting for transfers between devices  30.7 us (4%)
    pallas_call x1, Pallas kernels, summed_grads(): pl.pallas_call(functools.partial(grad_kernel, plan), out_shape=(jax.Shape...  315 us
    pallas_call x1, Pallas kernels, gathered(): pl.pallas_call(functools.partial(gather_kernel, groups, A, families), out...  267 us
    pallas_call x2, Pallas kernels, ffn_backward(): pl.pallas_call(functools.partial(ffn_backward_kernel, keep), grid=(steps,...  51.2 us
    ppermute x2, waiting for transfers between devices, passed_along(): return lax.ppermute(value, axis, pairs)  30.7 us
    broadcast_in_dim x4, other arithmetic, body(): shard_sum[None]  19 us
    pallas_call x1, Pallas kernels, ffn_forward(): pl.pallas_call(ffn_forward_kernel, grid=(steps,), out_shape=jax.ShapeDtyp...  17.9 us
  transfers between devices with their start and end apart: 2, of which 2 were waited for; matrix products, arithmetic and copies ran while one was open for 1% of the time, Pallas kernels for 0%

profile of v5, /device:TPU:0, one launch (start us, length us, event | category | flops | bytes accessed | tf_op | source)
XLA Modules:
  0.0 823.2 jit_solution(199151537097706382)
XLA Ops:
  1.9 266.7 %shard_map.152 = (bf16[16,16,128]{2,1,0:T(8,128)(2,1)}, bf16[16,96,3072]{2,1,0:T(8,128)(2,1)}, bf16[16,96,1536]{2,1,0:T(8,128)(2,1)}, bf16[16,96,8192]{2,1,0:T(8,128)(2,1)}, bf16[16,256,1536]{2,1,0:T(8,128)(2,1)}) custom-call(bf16[16,128]{1,0:T(8,128)(2,1)} %fusion.46.refs_0_, bf16[96,3072]{1,0:T(8,128)(2,1)} %bitcast.274, bf16[96,1536]{1,0:T(8,128)(2,1)} %bitcast.277, ...), custom_call_target="tpu_custom_call" | custom-call | tf_op jit(solution)/shard_map/pallas_call | solution.py:1057
  269.8 5.2 fusion.29
  278.0 1.9 copy.59
  289.1 17.9 %shard_map.153 = bf16[256,1536]{1,0:T(8,128)(2,1)S(1)} custom-call(f32[256,1536]{1,0:T(8,128)S(1)} %bitcast.204, f32[1,1536]{1,0:T(1,128)S(1)} %reshape.388.gain, f32[256,1]{1,0:T(8,128)S(1)} %copy.62.mask, bf16[1536,8192]{1,0:T(8,128)(2,1)} %bitcast.212, bf16[1536,8192]{1,0:T(8,128)(2,1)} %bitcast.213, bf16[4096,1536]{1,0:T(8,128)(2,1)} %bitcast.218), custom_call_target="tpu_custom_call" | custom-call | flops 9663676416 | bytes 37748736 | tf_op jit(solution)/shard_map/pallas_call | solution.py:231
  307.0 3.7 collective-permute-start
  312.0 15.3 %collective-permute-done = bf16[256,1536]{1,0:T(8,128)(2,1)S(1)} collective-permute-done((bf16[256,1536]{1,0:T(8,128)(2,1)S(1)}, bf16[256,1536]{1,0:T(8,128)(2,1)S(1)}, u32[]{:S(2)}, u32[]{:S(2)}) %collective-permute-start) | collective-permute-done | bytes 786464 | tf_op jit(solution)/shard_map/ppermute | solution.py:25
  328.3 5.4 fusion.59
  347.1 3.9 convolution_add_fusion
  351.0 23.5 %shard_map.154 = (f32[256,1536]{1,0:T(8,128)S(1)}, bf16[256,1536]{1,0:T(8,128)(2,1)S(1)}, f32[1,1536]{1,0:T(1,128)}) custom-call(f32[256,1536]{1,0:T(8,128)S(1)} %bitcast.202, bf16[256,1536]{1,0:T(8,128)(2,1)S(1)} %bitcast.207, f32[1,1536]{1,0:T(1,128)S(1)} %reshape.388.gain, f32[256,1]{1,0:T(8,128)S(1)} %copy.62.mask, bf16[1536,8192]{1,0:T(8,128)(2,1)} %bitcast.214, ...), custom_call_target="tpu_custom_call" | custom-call | flops 16106127360 | bytes 37748736 | tf_op jit(solution)/shard_map/pallas_call | solution.py:312
  375.7 2.3 convolution_convert_fusion.1
  379.5 2.5 fusion.3
  390.2 1.9 copy.74
  392.1 1.9 copy.75
  394.0 7.1 multiply_reduce_fusion.2
  403.8 2.0 copy.76
  408.0 15.4 %collective-permute-done.1 = bf16[2,128,1536]{2,1,0:T(8,128)(2,1)} collective-permute-done((bf16[2,128,1536]{2,1,0:T(8,128)(2,1)}, bf16[2,128,1536]{2,1,0:T(8,128)(2,1)}, u32[]{:S(2)}, u32[]{:S(2)}) %collective-permute-start.1) | collective-permute-done | bytes 786464 | tf_op jit(solution)/shard_map/ppermute | solution.py:25
  425.0 27.7 %shard_map.155 = (f32[256,1536]{1,0:T(8,128)S(1)}, bf16[256,1536]{1,0:T(8,128)(2,1)S(1)}, f32[1,1536]{1,0:T(1,128)S(1)}, bf16[4096,256]{1,0:T(8,128)(2,1)}, bf16...) custom-call(f32[256,1536]{1,0:T(8,128)S(1)} %bitcast.203, ...), custom_call_target="tpu_custom_call" | custom-call | flops 16106127360 | bytes 37748736 | tf_op jit(solution)/shard_map/pallas_call | solution.py:312
  454.7 4.0 convolution_convert_fusion
  459.8 2.3 fusion
  472.7 8.1 multiply_reduce_fusion
  486.2 314.7 %shard_map.156 = (bf16[384,11264]{1,0:T(8,128)(2,1)}, bf16[1408,1536]{1,0:T(8,128)(2,1)}, f32[8,1536]{1,0:T(8,128)}) custom-call(bf16[4096,256]{1,0:T(8,128)(2,1)} %get-tuple-element.40.at, bf16[1536,256]{1,0:T(8,128)(2,1)} %bitcast.266, bf16[1536,256]{1,0:T(8,128)(2,1)} %copy-done.6, bf16[1536,256]{1,0:T(8,128)(2,1)} %bitcast.267, ...), custom_call_target="tpu_custom_call" | custom-call | flops 13287555072 | bytes 40000000 | tf_op jit(solution)/shard_map/pallas_call | solution.py:832
  800.9 9.1 %bitcast_convert_fusion = f32[1,384,8192]{2,1,0:T(8,128)} fusion(bf16[384,11264]{1,0:T(8,128)(2,1)} %get-tuple-element.48), kind=kLoop, calls=%fused_computation | loop fusion | flops 3145728 | bytes 18874368 | tf_op jit(solution)/shard_map/broadcast_in_dim | solution.py:1155
  810.1 4.6 bitcast_convert_fusion.2
  814.6 3.6 bitcast_convert_fusion.1
  (188 shorter events, 70.9 us)
Async XLA Ops:
  1.9 267.7 %copy-start.10 = (bf16[2,128,1536]{2,1,0:T(8,128)(2,1)S(1)}, bf16[2,128,1536]{2,1,0:T(8,128)(2,1)}, u32[]{:S(2)}) copy-start(bf16[2,128,1536]{2,1,0:T(8,128)(2,1)} %param.9) | copy-start | bytes 2359300
  282.5 5.1 slice-start
  285.0 2.6 slice-start.1
  307.0 20.4 %collective-permute-start = (bf16[256,1536]{1,0:T(8,128)(2,1)S(1)}, bf16[256,1536]{1,0:T(8,128)(2,1)S(1)}, u32[]{:S(2)}, u32[]{:S(2)}) collective-permute-start(bf16[256,1536]{1,0:T(8,128)(2,1)S(1)} %shard_map.153), channel_id=1, source_target_pairs={{0,16},{1,17},{2,18},{3,19},{4,20},{5,21},{6,22},{7,23},{8,24},{9,... | collective-permute-start | bytes 2359304 | tf_op jit(solution)/shard_map/ppermute | solution.py:25
  328.3 5.4 copy-start.34
  339.5 3.0 copy-start.24
  339.5 3.0 copy-start.27
  346.6 4.4 copy-start.20
  347.1 28.5 %slice-start.2 = ((s8[4718592]{0:T(1024)(128)(4,1)}), s8[4194304]{0:T(1024)(128)(4,1)S(1)}, s32[]{:S(2)}) async-start(s8[4718592]{0:T(1024)(128)(4,1)} %bitcast.226), calls=%async_computation.2 | async-start | bytes 8388608
  351.0 24.6 %slice-start.3 = ((s8[4718592]{0:T(1024)(128)(4,1)}), s8[524288]{0:T(1024)(128)(4,1)S(1)}, s32[]{:S(2)}) async-start(s8[4718592]{0:T(1024)(128)(4,1)} %bitcast.226), calls=%async_computation.3 | async-start | bytes 1048576
  388.1 5.9 copy-start.14
  394.0 7.1 copy-start.4
  402.5 20.9 %collective-permute-start.1 = (bf16[2,128,1536]{2,1,0:T(8,128)(2,1)}, bf16[2,128,1536]{2,1,0:T(8,128)(2,1)}, u32[]{:S(2)}, u32[]{:S(2)}) collective-permute-start(bf16[2,128,1536]{2,1,0:T(8,128)(2,1)} %add_convert_fusion), channel_id=1, source_target_pairs={{16,0},{17,1},{18,2},{19,3},{20,4},{21,5},{22,6},{23,7},{24,8},{25... | collective-permute-start | bytes 2359304 | tf_op jit(solution)/shard_map/ppermute | solution.py:25
  403.8 3.0 copy-start.35
  406.8 16.6 %copy-start.36 = (bf16[2,128,1536]{2,1,0:T(8,128)(2,1)S(1)}, bf16[2,128,1536]{2,1,0:T(8,128)(2,1)}, u32[]{:S(2)}) copy-start(bf16[2,128,1536]{2,1,0:T(8,128)(2,1)} %param.10) | copy-start | bytes 2359300
  425.0 27.7 %copy-start = (bf16[2,128,1536]{2,1,0:T(8,128)(2,1)}, bf16[2,128,1536]{2,1,0:T(8,128)(2,1)S(1)}, u32[]{:S(2)}) copy-start(bf16[2,128,1536]{2,1,0:T(8,128)(2,1)S(1)} %fusion.28) | copy-start | bytes 2359300
  454.7 4.0 copy-start.5
  469.4 3.3 copy-start.11
  469.4 3.3 copy-start.15
  480.8 2.7 copy-start.30
  810.1 4.6 copy-start.23
  814.6 6.7 copy-start.43
  818.2 3.1 copy-start.2
  818.2 3.1 copy-start.16
  (31 other events, 43.2 us)

commit v6 on v5

--- a/solution.py
+++ b/solution.py
@@ -10,13 +10,13 @@
 H = 16
 KVH = 8
 HD = 96
-FF = 4096
 
 
 norm_eps = 1e-05
 rope_base = 100000.0
 masked_score = -1e30
 across = (((1,), (1,)), ((), ()))
+down_rows = (((0,), (0,)), ((), ()))
 
 
 def passed_along(value, axis, by):
@@ -25,168 +25,14 @@
     return lax.ppermute(value, axis, pairs)
 
 
-def rope_tables(slot_count, head_width):
-    half_width = head_width // 2
-    frequency = rope_base ** (-(jnp.arange(half_width, dtype=jnp.float32) * 2.0 / head_width))
-    angles = jnp.arange(slot_count, dtype=jnp.float32)[:, None] * frequency[None, :]
-    return (jnp.cos(angles), jnp.sin(angles))
-
-
-def rotate(vector, cosines, sine_table):
-    half_width = vector.shape[-1] // 2
-    front_half = vector[..., :half_width]
-    back_half = vector[..., half_width:]
-    cos_wide = cosines[:, None, :]
-    sin_wide = sine_table[:, None, :]
-    return jnp.concatenate(
-        [
-            front_half * cos_wide - back_half * sin_wide,
-            back_half * cos_wide + front_half * sin_wide,
-        ],
-        -1,
-    )
-
-
-def norm_scale(vector):
-    return lax.rsqrt(jnp.mean(vector * vector, -1, keepdims=True) + norm_eps)
-
-
-def allowed_keys(lengths, slot_count):
-    position = jnp.arange(slot_count, dtype=jnp.int32)
-    causal = position[None, :] <= position[:, None]
-    return causal[None] & (position[None, None, :] < lengths[:, None, None])
-
-
 def padding(lengths, slot_count):
     position = jnp.arange(slot_count, dtype=jnp.int32)
     return (position[None, :] < lengths[:, None]).astype(jnp.float32)[..., None]
 
 
-def norm_back(vector, scale, gain, grad_normed):
-    scaled = grad_normed * gain.astype(jnp.float32)
-    gain_grad = jnp.sum(grad_normed * vector * scale, axis=(0, 1))
-    grad_vector = scale * scaled - vector * (scale * scale * scale) * jnp.mean(
-        vector * scaled, -1, keepdims=True
-    )
-    return (gain_grad, grad_vector)
-
-
-def score_block(query_heads, key_heads, lengths):
-    slot_count = query_heads.shape[1]
-    scores = jnp.einsum(
-        "rqkgh,rpkh->rkgqp", query_heads, key_heads, preferred_element_type=jnp.float32
-    ) * HD ** (-0.5)
-    allowed = allowed_keys(lengths, slot_count)
-    return jnp.where(allowed[:, None, None], scores, masked_score)
-
-
-def attention_forward(weights, input_rows, lengths):
-    gain_one, qkv_w, output_weight = weights[:3]
-    row_count, slot_count, width = input_rows.shape
-    groups = H // KVH
-    cosines, sine_table = rope_tables(slot_count, HD)
-    scale_one = norm_scale(input_rows)
-    normed_one = (input_rows * scale_one * gain_one.astype(jnp.float32)).astype(jnp.bfloat16)
-    qkv_all = jnp.einsum("rsd,de->rse", normed_one, qkv_w, preferred_element_type=jnp.float32)
-    query_heads = rotate(
-        qkv_all[..., : H * HD].reshape(row_count, slot_count, H, HD), cosines, sine_table
-    )
-    query_heads = query_heads.astype(jnp.bfloat16).reshape(row_count, slot_count, KVH, groups, HD)
-    key_heads = rotate(
-        qkv_all[..., H * HD : (H + KVH) * HD].reshape(row_count, slot_count, KVH, HD),
-        cosines,
-        sine_table,
-    )
-    key_heads = key_heads.astype(jnp.bfloat16)
-    value_heads = (
-        qkv_all[..., (H + KVH) * HD :].reshape(row_count, slot_count, KVH, HD).astype(jnp.bfloat16)
-    )
-    scores = score_block(query_heads, key_heads, lengths)
-    row_max = jnp.max(scores, -1, keepdims=True)
-    log_total = row_max + jnp.log(jnp.sum(jnp.exp(scores - row_max), -1, keepdims=True))
-    prob_low = jnp.exp(scores - log_total).astype(jnp.bfloat16)
-    attention_result = jnp.einsum(
-        "rkgqp,rpkh->rqkgh", prob_low, value_heads, preferred_element_type=jnp.float32
-    )
-    attention_result = attention_result.astype(jnp.bfloat16).reshape(row_count, slot_count, H * HD)
-    after_attention = input_rows + jnp.einsum(
-        "vao,oj->vaj", attention_result, output_weight, preferred_element_type=jnp.float32
-    )
-    kept_state = (
-        input_rows,
-        scale_one,
-        normed_one,
-        query_heads,
-        key_heads,
-        value_heads,
-        log_total,
-        attention_result,
-        lengths,
-    )
-    return (after_attention, kept_state)
-
-
-def attention_backward(weights, kept_state, grad_after, gradient_after_lowered):
-    gain_one, qkv_w, output_weight = weights[:3]
-    (
-        input_rows,
-        scale_one,
-        normed_one,
-        query_heads,
-        key_heads,
-        value_heads,
-        log_total,
-        attention_result,
-        lengths,
-    ) = kept_state
-    row_count, slot_count, width = input_rows.shape
-    groups = H // KVH
-    score_scale = HD ** (-0.5)
-    cosines, sine_table = rope_tables(slot_count, HD)
-    attention_gradient = jnp.einsum(
-        "vol,el->voe", gradient_after_lowered, output_weight, preferred_element_type=jnp.float32
-    )
-    attention_gradient = attention_gradient.astype(jnp.bfloat16).reshape(
-        row_count, slot_count, KVH, groups, HD
-    )
-    scores = score_block(query_heads, key_heads, lengths)
-    prob_full = jnp.exp(scores - log_total)
-    prob_low = prob_full.astype(jnp.bfloat16)
-    grad_values = jnp.einsum(
-        "rkgqp,rqkgh->rpkh", prob_low, attention_gradient, preferred_element_type=jnp.float32
-    )
-    grad_probs = jnp.einsum(
-        "rqkgh,rpkh->rkgqp", attention_gradient, value_heads, preferred_element_type=jnp.float32
-    )
-    row_dot = jnp.sum(prob_full * grad_probs, -1, keepdims=True)
-    grad_scores = (prob_full * (grad_probs - row_dot)).astype(jnp.bfloat16)
-    grad_query = (
-        jnp.einsum("rkgqp,rpkh->rqkgh", grad_scores, key_heads, preferred_element_type=jnp.float32)
-        * score_scale
-    )
-    grad_query = rotate(grad_query.reshape(row_count, slot_count, H, HD), cosines, -sine_table)
-    grad_keys = (
-        jnp.einsum(
-            "rkgqp,rqkgh->rpkh", grad_scores, query_heads, preferred_element_type=jnp.float32
-        )
-        * score_scale
-    )
-    grad_keys = rotate(grad_keys, cosines, -sine_table)
-    grad_qkv = jnp.concatenate(
-        [
-            grad_query.reshape(row_count, slot_count, H * HD),
-            grad_keys.reshape(row_count, slot_count, KVH * HD),
-            grad_values.reshape(row_count, slot_count, KVH * HD),
-        ],
-        -1,
-    ).astype(jnp.bfloat16)
-    grad_normed_one = jnp.einsum("rse,de->rsd", grad_qkv, qkv_w, preferred_element_type=jnp.float32)
-    attn_gain_part, grad_norm_one = norm_back(input_rows, scale_one, gain_one, grad_normed_one)
-    return (grad_after + grad_norm_one, attn_gain_part, grad_qkv)
-
-
 FF_CHUNK = 512
 across = (((1,), (1,)), ((), ()))
+down_rows = (((0,), (0,)), ((), ()))
 
 
 def scaled_norm(value, gain):
@@ -323,8 +169,216 @@
     )(y, dz, gain, mask, gate_up_w, gate_up_w, down_w)
 
 
-def turned(array):
-    return array.reshape(-1, array.shape[-1]).T
+def turned_tables(slots, rows):
+    half_width = HD // 2
+    frequency = rope_base ** (-(jnp.arange(half_width, dtype=jnp.float32) * 2.0 / HD))
+    angles = frequency[:, None] * jnp.arange(slots, dtype=jnp.float32)[None, :]
+    return jnp.tile(jnp.cos(angles), (1, rows)), jnp.tile(jnp.sin(angles), (1, rows))
+
+
+def pair_mask(length, slots):
+    groups = H // KVH
+    key = lax.broadcasted_iota(jnp.int32, (slots, groups * slots), 0)
+    query = lax.rem(lax.broadcasted_iota(jnp.int32, (slots, groups * slots), 1), slots)
+    return (key <= query) & (key < length)
+
+
+def pair_of(ref, k, row, slots):
+    groups = H // KVH
+    first = groups * k * HD
+    return jnp.concatenate(
+        [ref[first + g * HD : first + (g + 1) * HD, row * slots : (row + 1) * slots] for g in range(groups)], 1
+    )
+
+
+def key_value(qkvt, k, row, slots):
+    tokens = slice(row * slots, (row + 1) * slots)
+    keys = qkvt[(H + k) * HD : (H + k + 1) * HD, tokens]
+    values = qkvt[(H + KVH + k) * HD : (H + KVH + k + 1) * HD, tokens]
+    return keys, values
+
+
+def pair_scores(keys, queries, mask):
+    scores = lax.dot_general(keys, queries, down_rows, preferred_element_type=jnp.float32) * HD ** (-0.5)
+    return jnp.where(mask, scores, masked_score)
+
+
+def attention_forward_kernel(rows, info, x, gain, cosines, sines, w, wo, y, qkvt, lse, ot, n1t, n1):
+    j = pl.program_id(0)
+    bf16, f32 = jnp.bfloat16, jnp.float32
+    slots, part, half = x.shape[0] // rows, KVH * HD, HD // 2
+    groups = H // KVH
+
+    @pl.when(j == 0)
+    def _():
+        n = scaled_norm(x[...].astype(f32), gain[...])[1]
+        n1[...] = n
+        n1t[...] = n.T
+
+    chunk = jnp.dot(n1[...], w[...], preferred_element_type=f32).T
+
+    @pl.when(j <= groups)
+    def _():
+        for h in range(KVH):
+            front, back = chunk[h * HD : h * HD + half], chunk[h * HD + half : (h + 1) * HD]
+            base = j * part + h * HD
+            qkvt[pl.ds(pl.multiple_of(base, 16), half), :] = (front * cosines[...] - back * sines[...]).astype(bf16)
+            qkvt[pl.ds(pl.multiple_of(base + half, 16), half), :] = (
+                back * cosines[...] + front * sines[...]
+            ).astype(bf16)
+
+    @pl.when(j > groups)
+    def _():
+        qkvt[pl.ds(pl.multiple_of(j * part, 16), part), :] = chunk.astype(bf16)
+        for row in range(rows):
+            mask = pair_mask(info[row], slots)
+            for k in range(KVH):
+                keys, values = key_value(qkvt, k, row, slots)
+                scores = pair_scores(keys, pair_of(qkvt, k, row, slots), mask)
+                top = jnp.max(scores, 0, keepdims=True)
+                total = top + jnp.log(jnp.sum(jnp.exp(scores - top), 0, keepdims=True))
+                lse[row * KVH + k : row * KVH + k + 1, :] = total
+                probs = jnp.exp(scores - total).astype(bf16)
+                out = jnp.dot(values, probs, preferred_element_type=f32).astype(bf16)
+                for g in range(groups):
+                    first = (groups * k + g) * HD
+                    ot[first : first + HD, row * slots : (row + 1) * slots] = out[:, g * slots : (g + 1) * slots]
+        y[...] = x[...].astype(f32) + lax.dot_general(ot[...], wo[...], down_rows, preferred_element_type=f32)
+
+
+def attention_backward_kernel(
+    rows, keep, info, x, gain, dy, dyb, cosines, sines, qkvt, lse, wo, w, dx, *rest
+):
+    if keep:
+        gain_grad, dqkv, dot, dqkvt, acc = rest
+    else:
+        dqkv, dot, dqkvt, acc = rest
+    j = pl.program_id(0)
+    bf16, f32 = jnp.bfloat16, jnp.float32
+    slots, part, half = x.shape[0] // rows, KVH * HD, HD // 2
+    groups = H // KVH
+
+    def unrotated(grad, row, width):
+        tokens = slice(row * slots, (row + 1) * slots)
+        cos, sin = cosines[:, tokens], sines[:, tokens]
+        if width > slots:
+            cos, sin = jnp.concatenate([cos] * groups, 1), jnp.concatenate([sin] * groups, 1)
+        grad = grad * HD ** (-0.5)
+        front, back = grad[:half], grad[half:]
+        return (front * cos + back * sin).astype(bf16), (back * cos - front * sin).astype(bf16)
+
+    @pl.when(j == 0)
+    def _():
+        dot[...] = lax.dot_general(dyb[...], wo[...], across, preferred_element_type=f32).astype(bf16).T
+        acc[...] = jnp.zeros_like(acc)
+        for row in range(rows):
+            tokens = slice(row * slots, (row + 1) * slots)
+            mask = pair_mask(info[row], slots)
+            for k in range(KVH):
+                keys, values = key_value(qkvt, k, row, slots)
+                queries, grads = pair_of(qkvt, k, row, slots), pair_of(dot, k, row, slots)
+                scores = pair_scores(keys, queries, mask)
+                probs = jnp.exp(scores - lse[row * KVH + k : row * KVH + k + 1, :])
+                grad_probs = lax.dot_general(values, grads, down_rows, preferred_element_type=f32)
+                grad_scores = (
+                    probs * (grad_probs - jnp.sum(probs * grad_probs, 0, keepdims=True))
+                ).astype(bf16)
+                grad_values = lax.dot_general(grads, probs.astype(bf16), across, preferred_element_type=f32)
+                grad_keys = lax.dot_general(queries, grad_scores, across, preferred_element_type=f32)
+                grad_queries = jnp.dot(keys, grad_scores, preferred_element_type=f32)
+                front, back = unrotated(grad_queries, row, groups * slots)
+                for g in range(groups):
+                    first = (groups * k + g) * HD
+                    dqkvt[first : first + half, tokens] = front[:, g * slots : (g + 1) * slots]
+                    dqkvt[first + half : first + HD, tokens] = back[:, g * slots : (g + 1) * slots]
+                front, back = unrotated(grad_keys, row, slots)
+                first = (H + k) * HD
+                dqkvt[first : first + half, tokens] = front
+                dqkvt[first + half : first + HD, tokens] = back
+                first = (H + KVH + k) * HD
+                dqkvt[first : first + HD, tokens] = grad_values.astype(bf16)
+        for i in range(groups + 2):
+            dqkv[:, i * part : (i + 1) * part] = dqkvt[i * part : (i + 1) * part, :].T
+
+    columns = pl.ds(pl.multiple_of(j * part, 128), part)
+    acc[...] += lax.dot_general(dqkv[:, columns], w[...], across, preferred_element_type=f32)
+
+    @pl.when(j == pl.num_programs(0) - 1)
+    def _():
+        value, grad_normed = x[...].astype(f32), acc[...]
+        r = lax.rsqrt(jnp.mean(value * value, -1, keepdims=True) + norm_eps)
+        scaled = grad_normed * gain[...]
+        inner = jnp.mean(value * scaled, -1, keepdims=True)
+        total = dy[...] + (r * scaled - value * (r * r * r) * inner)
+        if keep:
+            gain_grad[...] = jnp.sum(grad_normed * value * r, axis=0, keepdims=True)
+            dx[...] = jnp.where(info[rows] == 1, total, total.astype(bf16).astype(f32))
+        else:
+            dx[...] = total.astype(bf16)
+
+
+def attention_specs(tokens, width):
+    part = KVH * HD
+    whole = lambda *shape: pl.BlockSpec(shape, lambda j: (0,) * len(shape))
+    return part, whole, pl.BlockSpec(memory_space=pltpu.SMEM), pl.BlockSpec((width, part), lambda j: (0, j))
+
+
+def attention_forward(info, x, gain, tables, qkv_w, output_weight, rows):
+    tokens, width = x.shape
+    cols, slots = qkv_w.shape[1], tokens // rows
+    part, whole, scalars, weight = attention_specs(tokens, width)
+    shape, bf16, f32 = jax.ShapeDtypeStruct, jnp.bfloat16, jnp.float32
+    stats = (rows * KVH, H // KVH * slots)
+    return pl.pallas_call(
+        functools.partial(attention_forward_kernel, rows),
+        grid=(cols // part,),
+        out_shape=(
+            shape((tokens, width), f32), shape((cols, tokens), bf16), shape(stats, f32),
+            shape((H * HD, tokens), bf16), shape((width, tokens), bf16),
+        ),
+        in_specs=[
+            scalars, whole(tokens, width), whole(1, width), whole(HD // 2, tokens), whole(HD // 2, tokens), weight,
+            whole(H * HD, width),
+        ],
+        out_specs=(
+            whole(tokens, width), whole(cols, tokens), whole(*stats), whole(H * HD, tokens), whole(width, tokens)
+        ),
+        scratch_shapes=[pltpu.VMEM((tokens, width), bf16)],
+        compiler_params=pltpu.CompilerParams(vmem_limit_bytes=40 * 1024 * 1024),
+        cost_estimate=pl.CostEstimate(
+            flops=2 * tokens * width * (cols + H * HD), bytes_accessed=2 * width * (cols + H * HD), transcendentals=0
+        ),
+    )(info, x, gain, *tables, qkv_w, output_weight)
+
+
+def attention_backward(info, x, gain, dy, dy_low, tables, qkvt, lse, output_weight, qkv_w, rows, keep):
+    tokens, width = x.shape
+    cols = qkv_w.shape[1]
+    part, whole, scalars, weight = attention_specs(tokens, width)
+    shape, bf16, f32 = jax.ShapeDtypeStruct, jnp.bfloat16, jnp.float32
+    scratch = [pltpu.VMEM((H * HD, tokens), bf16), pltpu.VMEM((cols, tokens), bf16), pltpu.VMEM((tokens, width), f32)]
+    outs, out_specs = [shape((tokens, width), f32 if keep else bf16)], [whole(tokens, width)]
+    if keep:
+        outs += [shape((1, width), f32), shape((tokens, cols), bf16)]
+        out_specs += [whole(1, width), whole(tokens, cols)]
+    else:
+        scratch = [pltpu.VMEM((tokens, cols), bf16)] + scratch
+    return pl.pallas_call(
+        functools.partial(attention_backward_kernel, rows, keep),
+        grid=(cols // part,),
+        out_shape=tuple(outs),
+        in_specs=[
+            scalars, whole(tokens, width), whole(1, width), whole(tokens, width), whole(tokens, width),
+            whole(HD // 2, tokens), whole(HD // 2, tokens), whole(cols, tokens), whole(*lse.shape), whole(H * HD, width),
+            weight,
+        ],
+        out_specs=tuple(out_specs),
+        scratch_shapes=scratch,
+        compiler_params=pltpu.CompilerParams(vmem_limit_bytes=48 * 1024 * 1024),
+        cost_estimate=pl.CostEstimate(
+            flops=2 * tokens * width * (cols + H * HD), bytes_accessed=2 * width * (cols + H * HD), transcendentals=0
+        ),
+    )(info, x, gain, dy, dy_low, *tables, qkvt, lse, output_weight, qkv_w)
 
 
 def flat(array):
@@ -1085,45 +1139,36 @@
         flat(gate_up_all),
         flat(down_all),
     )
-    slots = inputs_x.shape[1]
-    inputs_f = inputs_x.astype(jnp.float32)
-    mask = padding(lengths, slots)
-    mask_rows = mask.reshape(-1, 1)
-    ffn_gain_row = weights[3].astype(jnp.float32).reshape(1, -1)
-    gate_up_w, down_w = weights[4:]
-    dz_given = (cotangent.astype(jnp.float32) * mask).astype(jnp.bfloat16)
-    after_one, _ = attention_forward(weights, inputs_f, lengths)
-    first_out = ffn_forward(flat(after_one), ffn_gain_row, mask_rows, gate_up_w, down_w)
-    recv_act = passed_along(first_out, "section", 1).reshape(inputs_x.shape)
-    layer_in = jnp.where(is_first, inputs_f, recv_act.astype(jnp.float32))
-    after, kept_state = attention_forward(weights, layer_in, lengths)
-    dy, dy_low, _ = ffn_backward(
-        flat(after), flat(dz_given), ffn_gain_row, mask_rows, gate_up_w, down_w, False
-    )
-    second_dx, _, _ = attention_backward(
-        weights, kept_state, dy.reshape(inputs_x.shape), dy_low.reshape(inputs_x.shape)
-    )
-    recv_grad = passed_along(second_dx.astype(jnp.bfloat16), "section", -1)
-    normed_one, attention_result = kept_state[2], kept_state[7]
-    attention_turned, normed_turned = turned(attention_result), turned(normed_one)
-    recv_grad, attention_turned, normed_turned = lax.optimization_barrier(
-        (recv_grad, attention_turned, normed_turned)
-    )
+    rows, slots, width = inputs_x.shape
+    tables = turned_tables(slots, rows)
+    info = jnp.concatenate([lengths, is_first.astype(jnp.int32)[None]])
+    mask = padding(lengths, slots).reshape(-1, 1)
+    gain_one = weights[0].astype(jnp.float32).reshape(1, -1)
+    gain_two = weights[3].astype(jnp.float32).reshape(1, -1)
+    qkv_w, output_weight, _, gate_up_w, down_w = weights[1:]
+    dz_given = (flat(cotangent).astype(jnp.float32) * mask).astype(jnp.bfloat16)
+    after_one = attention_forward(info, flat(inputs_x), gain_one, tables, qkv_w, output_weight, rows)[0]
+    first_out = ffn_forward(after_one, gain_two, mask, gate_up_w, down_w)
+    recv_act = passed_along(first_out, "section", 1)
+    layer_in = jnp.where(is_first, flat(inputs_x), recv_act)
+    after, heads, log_total, attention_turned, normed_turned = attention_forward(
+        info, layer_in, gain_one, tables, qkv_w, output_weight, rows
+    )
+    dy, dy_low, _ = ffn_backward(after, dz_given, gain_two, mask, gate_up_w, down_w, False)
+    (second_dx,) = attention_backward(
+        info, layer_in, gain_one, dy, dy_low, tables, heads, log_total, output_weight, qkv_w, rows, False
+    )
+    recv_grad = passed_along(second_dx, "section", -1)
     dz = jnp.where(is_first, (recv_grad.astype(jnp.float32) * mask).astype(jnp.bfloat16), dz_given)
-    dz = flat(dz)
     dy, dy_low, ffn_gain_part, hidden_turned, grad_gate, grad_up, normed_two_turned, result = ffn_backward(
-        flat(after), dz, ffn_gain_row, mask_rows, gate_up_w, down_w, True
+        after, dz, gain_two, mask, gate_up_w, down_w, True
     )
     grad_x, attn_gain_part, grad_qkv = attention_backward(
-        weights, kept_state, dy.reshape(inputs_x.shape), dy_low.reshape(inputs_x.shape)
+        info, layer_in, gain_one, dy, dy_low, tables, heads, log_total, output_weight, qkv_w, rows, True
     )
     section_out = result.reshape((1,) + inputs_x.shape)
-    input_grads = jnp.where(
-        is_first, grad_x, grad_x.astype(jnp.bfloat16).astype(jnp.float32)
-    )[None]
-    gain_parts = jnp.pad(
-        jnp.concatenate([attn_gain_part[None], ffn_gain_part], 0), ((0, 6), (0, 0))
-    )
+    input_grads = grad_x.reshape((1,) + inputs_x.shape)
+    gain_parts = jnp.pad(jnp.concatenate([attn_gain_part, ffn_gain_part], 0), ((0, 6), (0, 0)))
     gate_qkv_sum, down_out_sum, gain_sums = summed_grads(
         lax.axis_size("group"),
         lax.axis_size("dp"),
@@ -1135,7 +1180,7 @@
         dy_low,
         grad_gate,
         grad_up,
-        flat(grad_qkv),
+        grad_qkv,
         gain_parts,
     )
     gain_cols = attn_gain.shape[1] * lax.axis_size("dp")

time: 832 us -> 793 us (0.953)
  Pallas kernels: 650 us -> 716 us
  matrix products: 50.4 us -> 0 us
  local copies, waits for them, and re-layouts: 44.9 us -> 6.16 us
  other arithmetic: 40.3 us -> 24.3 us
    pallas_call x0 -> x4, Pallas kernels: none -> 56.2 us  [the longest x2 29.5 us: attention_backward(): pl.pallas_call(functools.partial(attention_backward_kernel, rows, keep),...]
    dot_general x20 -> x0, matrix products: 50.4 us -> none  [the longest x2 15.2 us: attention_backward(): jnp.einsum('rse,de->rsd', grad_qkv, qkv_w, preferred_element_type=jnp.flo...]
    slice x14 -> x0, local copies, waits for them, and re-layouts: 11.7 us -> none  [the longest x4 5.06 us: attention_forward(): qkv_all[..., :H * HD].reshape(row_count, slot_count, H, HD)]
    reshape x7 -> x0, local copies, waits for them, and re-layouts: 9.44 us -> none  [the longest x2 3.08 us: attention_backward(): grad_values.reshape(row_count, slot_count, KVH * HD)]
    pallas_call x2, Pallas kernels: 51.2 us -> 60.4 us  [ffn_backward(): pl.pallas_call(functools.partial(ffn_backward_kernel, keep), grid=(steps,...]
  transfers between devices with their start and end apart: 2 -> 2, of which waited for: 2 -> 2; matrix products, arithmetic and copies ran while one was open for 1% -> 0% of each run, Pallas kernels for 0% -> 0%
where the time goes in v6:
time: 793 us; the launch traced here: 789 us
  Pallas kernels  716 us (90%)
  waiting for transfers between devices  35.8 us (5%)
  other arithmetic  24.3 us (3%)
    pallas_call x1, Pallas kernels, summed_grads(): pl.pallas_call(functools.partial(grad_kernel, plan), out_shape=(jax.Shape...  315 us
    pallas_call x1, Pallas kernels, gathered(): pl.pallas_call(functools.partial(gather_kernel, groups, A, families), out...  267 us
    pallas_call x2, Pallas kernels, ffn_backward(): pl.pallas_call(functools.partial(ffn_backward_kernel, keep), grid=(steps,...  60.4 us
    ppermute x2, waiting for transfers between devices, passed_along(): return lax.ppermute(value, axis, pairs)  35.8 us
    pallas_call x2, Pallas kernels, attention_backward(): pl.pallas_call(functools.partial(attention_backward_kernel, rows, keep),...  29.5 us
    pallas_call x2, Pallas kernels, attention_forward(): pl.pallas_call(functools.partial(attention_forward_kernel, rows), grid=(c...  26.7 us
    broadcast_in_dim x4, other arithmetic, body(): shard_sum[None]  19 us
    pallas_call x1, Pallas kernels, ffn_forward(): pl.pallas_call(ffn_forward_kernel, grid=(steps,), out_shape=jax.ShapeDtyp...  18.2 us
  transfers between devices with their start and end apart: 2, of which 2 were waited for; matrix products, arithmetic and copies ran while one was open for 0% of the time, Pallas kernels for 0%

profile of v6, /device:TPU:0, one launch (start us, length us, event | category | flops | bytes accessed | tf_op | source)
XLA Modules:
  0.0 788.8 jit_solution(7374502526354137750)
XLA Ops:
  0.7 1.3 fusion.9.refs_0_
  2.0 266.7 %shard_map.152 = (bf16[16,16,128]{2,1,0:T(8,128)(2,1)}, bf16[16,96,3072]{2,1,0:T(8,128)(2,1)}, bf16[16,96,1536]{2,1,0:T(8,128)(2,1)}, bf16[16,96,8192]{2,1,0:T(8,128)(2,1)}, bf16[16,256,1536]{2,1,0:T(8,128)(2,1)}) custom-call(bf16[16,128]{1,0:T(8,128)(2,1)} %fusion.9.refs_0_, bf16[96,3072]{1,0:T(8,128)(2,1)} %bitcast.61, bf16[96,1536]{1,0:T(8,128)(2,1)} %bitcast.62, ...), custom_call_target="tpu_custom_call" | custom-call | tf_op jit(solution)/shard_map/pallas_call | solution.py:1111
  268.7 0.9 convert_reduce_fusion
  270.3 2.3 copy-done
  272.7 14.1 %shard_map.153 = (f32[256,1536]{1,0:T(8,128)S(1)}, bf16[3072,256]{1,0:T(8,128)(2,1)}, f32[16,256]{1,0:T(8,128)}, bf16[1536,256]{1,0:T(8,128)(2,1)}, bf16[1536,256]{1,0:T(8,128)(2,1)}) custom-call(s32[3]{0:T(128)S(1)} %pad_add_fusion.info, bf16[256,1536]{1,0:T(8,128)(2,1)S(1)} %bitcast.45, f32[1,1536]{1,0:T(1,128)S(1)} %reshape.156.gain, ...), custom_call_target="tpu_custom_call" | custom-call | flops 3623878656 | bytes 14155776 | tf_op jit(solution)/shard_map/pallas_call | solution.py:332
  286.8 18.2 %shard_map.154 = bf16[256,1536]{1,0:T(8,128)(2,1)S(1)} custom-call(f32[256,1536]{1,0:T(8,128)S(1)} %get-tuple-element.38.y, f32[1,1536]{1,0:T(1,128)S(1)} %reshape.157.gain, f32[256,1]{1,0:T(8,128)S(1)} %copy.17.mask, bf16[1536,8192]{1,0:T(8,128)(2,1)} %bitcast.46, bf16[1536,8192]{1,0:T(8,128)(2,1)} %bitcast.47, bf16[4096,1536]{1,0:T(8,128)(2,1)} %bitcast.56), custom_call_target="tpu_custom_call" | custom-call | flops 9663676416 | bytes 37748736 | tf_op jit(solution)/shard_map/pallas_call | solution.py:77
  305.0 3.7 collective-permute-start
  308.9 16.4 %collective-permute-done = bf16[256,1536]{1,0:T(8,128)(2,1)S(1)} collective-permute-done((bf16[256,1536]{1,0:T(8,128)(2,1)S(1)}, bf16[256,1536]{1,0:T(8,128)(2,1)S(1)}, u32[]{:S(2)}, u32[]{:S(2)}) %collective-permute-start) | collective-permute-done | bytes 786464 | tf_op jit(solution)/shard_map/ppermute | solution.py:25
  325.5 12.6 %shard_map.155 = (f32[256,1536]{1,0:T(8,128)S(1)}, bf16[3072,256]{1,0:T(8,128)(2,1)S(1)}, f32[16,256]{1,0:T(8,128)S(1)}, bf16[1536,256]{1,0:T(8,128)(2,1)S(1)}, bf16[1536,256]{1,0:T(8,128)(2,1)S(1)}) custom-call(s32[3]{0:T(128)S(1)} %pad_add_fusion.info, bf16[256,1536]{1,0:T(8,128)(2,1)S(1)} %broadcast_select_fusion.x, f32[1,1536]{1,0:T(1,128)S(1)} %reshape.156.gain, ...), custom_call_target="tpu_custom_call" | custom-call | flops 3623878656 | bytes 14155776 | tf_op jit(solution)/shard_map/pallas_call | solution.py:332
  338.1 0.9 copy-done.9
  338.9 24.8 %shard_map.156 = (f32[256,1536]{1,0:T(8,128)S(1)}, bf16[256,1536]{1,0:T(8,128)(2,1)S(1)}, f32[1,1536]{1,0:T(1,128)}) custom-call(f32[256,1536]{1,0:T(8,128)S(1)} %get-tuple-element.41.y, bf16[256,1536]{1,0:T(8,128)(2,1)S(1)} %fusion.dz, f32[1,1536]{1,0:T(1,128)S(1)} %reshape.157.gain, f32[256,1]{1,0:T(8,128)S(1)} %copy.17.mask, bf16[1536,8192]{1,0:T(8,128)(2,1)} %bitcast.48, ...), custom_call_target="tpu_custom_call" | custom-call | flops 16106127360 | bytes 37748736 | tf_op jit(solution)/shard_map/pallas_call | solution.py:158
  363.8 13.5 %shard_map.157 = bf16[256,1536]{1,0:T(8,128)(2,1)S(1)} custom-call(s32[3]{0:T(128)S(1)} %pad_add_fusion.info, bf16[256,1536]{1,0:T(8,128)(2,1)S(1)} %broadcast_select_fusion.x, f32[1,1536]{1,0:T(1,128)S(1)} %reshape.156.gain, f32[256,1536]{1,0:T(8,128)S(1)} %get-tuple-element.42.dy, bf16[256,1536]{1,0:T(8,128)(2,1)S(1)} %get-tuple-element.43.dyb, ...), custom_call_target="tpu_custom_call" | custom-call | flops 3623878656 | bytes 14155776 | tf_op jit(solution)/shard_map/pallas_call | solution.py:366
  377.3 1.4 collective-permute-start.1
  378.7 19.4 %collective-permute-done.1 = bf16[256,1536]{1,0:T(8,128)(2,1)} collective-permute-done((bf16[256,1536]{1,0:T(8,128)(2,1)S(1)}, bf16[256,1536]{1,0:T(8,128)(2,1)}, u32[]{:S(2)}, u32[]{:S(2)}) %collective-permute-start.1) | collective-permute-done | bytes 786464 | tf_op jit(solution)/shard_map/ppermute | solution.py:25
  398.1 1.8 fusion.1.dz
  399.9 35.6 %shard_map.158 = (f32[256,1536]{1,0:T(8,128)S(1)}, bf16[256,1536]{1,0:T(8,128)(2,1)S(1)}, f32[1,1536]{1,0:T(1,128)S(1)}, bf16[4096,256]{1,0:T(8,128)(2,1)}, bf16...) custom-call(f32[256,1536]{1,0:T(8,128)S(1)} %copy-done.3, ...), custom_call_target="tpu_custom_call" | custom-call | flops 16106127360 | bytes 37748736 | tf_op jit(solution)/shard_map/pallas_call | solution.py:158
  435.6 16.0 %shard_map.159 = (f32[256,1536]{1,0:T(8,128)}, f32[1,1536]{1,0:T(1,128)S(1)}, bf16[256,3072]{1,0:T(8,128)(2,1)S(1)}) custom-call(s32[3]{0:T(128)S(1)} %pad_add_fusion.info, bf16[256,1536]{1,0:T(8,128)(2,1)S(1)} %broadcast_select_fusion.x, f32[1,1536]{1,0:T(1,128)S(1)} %reshape.156.gain, f32[256,1536]{1,0:T(8,128)S(1)} %get-tuple-element.47.dy, ...), custom_call_target="tpu_custom_call" | custom-call | flops 3623878656 | bytes 14155776 | tf_op jit(solution)/shard_map/pallas_call | solution.py:366
  451.6 1.1 copy-done.7
  453.4 314.9 %shard_map.160 = (bf16[384,11264]{1,0:T(8,128)(2,1)}, bf16[1408,1536]{1,0:T(8,128)(2,1)}, f32[8,1536]{1,0:T(8,128)}) custom-call(bf16[4096,256]{1,0:T(8,128)(2,1)} %get-tuple-element.50.at, bf16[1536,256]{1,0:T(8,128)(2,1)} %copy-done.8, bf16[1536,256]{1,0:T(8,128)(2,1)} %copy-done.10, bf16[1536,256]{1,0:T(8,128)(2,1)} %copy-done.9, ...), custom_call_target="tpu_custom_call" | custom-call | flops 13287555072 | bytes 40000000 | tf_op jit(solution)/shard_map/pallas_call | solution.py:886
  768.2 9.1 %bitcast_convert_fusion = f32[1,384,8192]{2,1,0:T(8,128)} fusion(bf16[384,11264]{1,0:T(8,128)(2,1)} %get-tuple-element.60), kind=kLoop, calls=%fused_computation | loop fusion | flops 3145728 | bytes 18874368 | tf_op jit(solution)/shard_map/broadcast_in_dim | solution.py:1200
  777.3 4.6 bitcast_convert_fusion.2
  781.9 3.6 bitcast_convert_fusion.1
  785.5 1.7 bitcast_convert_fusion.3
  787.2 1.4 fusion.11
  (43 shorter events, 1.7 us)
Async XLA Ops:
  0.6 269.2 %copy-start.13 = (s32[2]{0:T(128)S(1)}, s32[2]{0:T(128)}, u32[]{:S(2)}) copy-start(s32[2]{0:T(128)} %param.11) | copy-start | bytes 28
  0.6 269.7 %copy-start.5 = (bf16[2,128,1536]{2,1,0:T(8,128)(2,1)S(1)}, bf16[2,128,1536]{2,1,0:T(8,128)(2,1)}, u32[]{:S(2)}) copy-start(bf16[2,128,1536]{2,1,0:T(8,128)(2,1)} %param.9) | copy-start | bytes 2359300
  270.3 2.3 copy-start
  286.8 38.7 %slice-start = ((s8[4718592]{0:T(1024)(128)(4,1)}), s8[4194304]{0:T(1024)(128)(4,1)S(1)}, s32[]{:S(2)}) async-start(s8[4718592]{0:T(1024)(128)(4,1)} %bitcast.42), calls=%async_computation | async-start | bytes 8388608
  286.8 21.9 %copy-start.12 = (bf16[2,128,1536]{2,1,0:T(8,128)(2,1)S(1)}, bf16[2,128,1536]{2,1,0:T(8,128)(2,1)}, u32[]{:S(2)}) copy-start(bf16[2,128,1536]{2,1,0:T(8,128)(2,1)} %param.10) | copy-start | bytes 2359300
  286.8 38.7 %slice-start.1 = ((s8[4718592]{0:T(1024)(128)(4,1)}), s8[524288]{0:T(1024)(128)(4,1)S(1)}, s32[]{:S(2)}) async-start(s8[4718592]{0:T(1024)(128)(4,1)} %bitcast.42), calls=%async_computation.1 | async-start | bytes 1048576
  305.0 20.3 %collective-permute-start = (bf16[256,1536]{1,0:T(8,128)(2,1)S(1)}, bf16[256,1536]{1,0:T(8,128)(2,1)S(1)}, u32[]{:S(2)}, u32[]{:S(2)}) collective-permute-start(bf16[256,1536]{1,0:T(8,128)(2,1)S(1)} %shard_map.154), channel_id=1, source_target_pairs={{0,16},{1,17},{2,18},{3,19},{4,20},{5,21},{6,22},{7,23},{8,24},{9,... | collective-permute-start | bytes 2359304 | tf_op jit(solution)/shard_map/ppermute | solution.py:25
  338.1 0.9 copy-start.9
  338.9 24.8 %copy-start.2 = (f32[256,1536]{1,0:T(8,128)}, f32[256,1536]{1,0:T(8,128)S(1)}, u32[]{:S(2)}) copy-start(f32[256,1536]{1,0:T(8,128)S(1)} %get-tuple-element.41.y) | copy-start | bytes 4718596
  338.9 24.9 %copy-start.8 = (bf16[1536,256]{1,0:T(8,128)(2,1)}, bf16[1536,256]{1,0:T(8,128)(2,1)S(1)}, u32[]{:S(2)}) copy-start(bf16[1536,256]{1,0:T(8,128)(2,1)S(1)} %get-tuple-element.51.ot) | copy-start | bytes 2359300
  338.9 24.9 %copy-start.1 = (bf16[3072,256]{1,0:T(8,128)(2,1)}, bf16[3072,256]{1,0:T(8,128)(2,1)S(1)}, u32[]{:S(2)}) copy-start(bf16[3072,256]{1,0:T(8,128)(2,1)S(1)} %get-tuple-element.44.qkvt) | copy-start | bytes 4718596
  377.3 22.6 %copy-start.3 = (f32[256,1536]{1,0:T(8,128)S(1)}, f32[256,1536]{1,0:T(8,128)}, u32[]{:S(2)}) copy-start(f32[256,1536]{1,0:T(8,128)} %copy-done.2) | copy-start | bytes 4718596
  377.3 20.8 %collective-permute-start.1 = (bf16[256,1536]{1,0:T(8,128)(2,1)S(1)}, bf16[256,1536]{1,0:T(8,128)(2,1)}, u32[]{:S(2)}, u32[]{:S(2)}) collective-permute-start(bf16[256,1536]{1,0:T(8,128)(2,1)S(1)} %shard_map.157), channel_id=1, source_target_pairs={{16,0},{17,1},{18,2},{19,3},{20,4},{21,5},{22,6},{23,7},{24,8},{25... | collective-permute-start | bytes 2359304 | tf_op jit(solution)/shard_map/ppermute | solution.py:25
  399.9 35.6 %copy-start.4 = (bf16[256,1536]{1,0:T(8,128)(2,1)}, bf16[256,1536]{1,0:T(8,128)(2,1)S(1)}, u32[]{:S(2)}) copy-start(bf16[256,1536]{1,0:T(8,128)(2,1)S(1)} %fusion.1.dz) | copy-start | bytes 2359300
  435.6 16.0 %copy-start.6 = (bf16[256,1536]{1,0:T(8,128)(2,1)}, bf16[256,1536]{1,0:T(8,128)(2,1)S(1)}, u32[]{:S(2)}) copy-start(bf16[256,1536]{1,0:T(8,128)(2,1)S(1)} %get-tuple-element.48.dyb.dy) | copy-start | bytes 2359300
  435.6 16.0 %copy-start.10 = (bf16[1536,256]{1,0:T(8,128)(2,1)}, bf16[1536,256]{1,0:T(8,128)(2,1)S(1)}, u32[]{:S(2)}) copy-start(bf16[1536,256]{1,0:T(8,128)(2,1)S(1)} %get-tuple-element.52.n2t) | copy-start | bytes 2359300
  451.6 1.1 copy-start.7
  777.3 4.6 copy-start.11

commit v7 on v6

--- a/solution.py
+++ b/solution.py
@@ -927,20 +927,29 @@
     )(at, ot, n2t, n1t, dz, dy, dgate, dup, dq, gain_parts)
 
 
-W_HOP = 5
+W_HOP = 4
+AFTER = 1
+ROOMS = 3
 gather_families = (
-    (1, True, False),
-    (2, True, True),
-    (1, True, False),
+    (1, False, False),
+    (2, False, True),
+    (1, False, False),
     (8, True, False),
     (4, False, False),
 )
 
 
-def gather_kernel(groups, pairs, families, *refs):
+def gather_kernel(groups, pairs, families, rows, *refs):
     G, A, F = groups, pairs, len(families)
-    shards, wholes = refs[:F], refs[F : 2 * F]
-    sems = refs[2 * F :]
+    shards, refs = refs[:F], refs[F:]
+    if rows:
+        (x, mask, cosines, sines), refs = refs[:4], refs[4:]
+    wholes, refs = refs[:F], refs[F:]
+    if rows:
+        (gain_rows, first_out), refs = refs[:2], refs[2:]
+    sems, refs = refs[: 9 * F], refs[9 * F :]
+    if rows:
+        in_gain, in_wide, in_gate, in_down, in_sem, n1, qkvt, ot, y, n2, gate, inner = refs
     s, z, d = lax.axis_index("section"), lax.axis_index("group"), lax.axis_index("dp")
     c, a = lax.rem(d, 2), lax.div(d, 2)
     sib = (s, z, 2 * a + 1 - c)
@@ -955,16 +964,15 @@
         pl.semaphore_signal(barrier, inc=1, device_id=dev, device_id_type=MESH)
     pl.semaphore_wait(barrier, A + 2)
 
+    def columns(f, i):
+        pieces, halves, _ = families[f]
+        size = shards[f].shape[1] // pieces
+        if halves:
+            i = lax.rem(i, 2) * (pieces // 2) + lax.div(i, 2)
+        return pl.ds(pl.multiple_of(i * size, 128), size)
+
     def cut(f, ref, i):
-        pieces, by_columns, _ = families[f]
-        rows, cols = ref.shape
-        if pieces == 1:
-            return ref
-        if by_columns:
-            size = cols // pieces
-            return ref.at[:, pl.ds(pl.multiple_of(i * size, 128), size)]
-        size = rows // pieces
-        return ref.at[pl.ds(pl.multiple_of(i * size, 16), size), :]
+        return ref.at[:, columns(f, i)]
 
     def placed(f, i, o, part, core):
         return cut(f, wholes[f].at[(o * A + part) * 2 + core], i)
@@ -1015,6 +1023,136 @@
     for pieces, _, _ in families:
         first.append(total)
         total += pieces
+
+    def into(f, i, room):
+        return pltpu.make_async_copy(wholes[f].at[:, :, columns(f, i)], room, in_sem.at[first[f] + i])
+
+    def arrived(f, i, room):
+        own_copy(f, i).wait()
+
+        @pl.loop(0, G)
+        def _(o):
+            for k in range(A):
+                from_core(f, i, o, k).wait_recv()
+
+        into(f, i, room).start()
+
+    def one_matrix(room):
+        return room.reshape(room.shape[0] * room.shape[1], room.shape[2])
+
+    def forward(t):
+        f32, bf16 = jnp.float32, jnp.bfloat16
+        slots, part, half, ratio = x.shape[0] // max(rows, 1), KVH * HD, HD // 2, H // KVH
+        after = W_HOP * G + AFTER
+        places = [(1, i) for i in range(families[1][0])] + [(2, 0)]
+
+        @pl.when(t == first[0] + after)
+        def _():
+            arrived(0, 0, in_gain)
+            into(0, 0, in_gain).wait()
+            turned = one_matrix(in_gain[...]).astype(f32).T
+            gain_rows[...] = turned[:8]
+            n1[...] = scaled_norm(x[...].astype(f32), gain_rows[0:1, :])[1]
+
+        for slot, (f, i) in enumerate(places):
+            @pl.when(t == first[f] + i + after)
+            def _(slot=slot, f=f, i=i):
+                arrived(f, i, in_wide.at[slot])
+
+        i3 = t - first[3] - after
+
+        @pl.when((i3 >= 0) & (i3 < families[3][0]))
+        def _():
+            arrived(3, i3, in_gate.at[lax.rem(i3, ROOMS)])
+
+        i4 = t - first[4] - after
+
+        @pl.when((i4 >= 0) & (i4 < families[4][0]))
+        def _():
+            arrived(4, i4, in_down.at[lax.rem(i4, ROOMS)])
+
+        for i in range(families[1][0]):
+            @pl.when(t == first[1] + i + after + 1)
+            def _(i=i):
+                into(1, i, in_wide.at[i]).wait()
+                for j in range(in_wide.shape[3] // part):
+                    weight = one_matrix(in_wide[i, :, :, j * part : (j + 1) * part])
+                    chunk = jnp.dot(n1[...], weight, preferred_element_type=f32).T
+                    top = (i * (in_wide.shape[3] // part) + j) * part
+                    if top >= (H + KVH) * HD:
+                        qkvt[top : top + part, :] = chunk.astype(bf16)
+                        continue
+                    for h in range(KVH):
+                        base = top + h * HD
+                        front, back = chunk[h * HD : h * HD + half], chunk[h * HD + half : (h + 1) * HD]
+                        qkvt[base : base + half, :] = (front * cosines[...] - back * sines[...]).astype(bf16)
+                        qkvt[base + half : base + HD, :] = (back * cosines[...] + front * sines[...]).astype(bf16)
+
+        def heads(index, carry):
+            row, k = lax.div(index, KVH), lax.rem(index, KVH)
+            tokens = pl.ds(pl.multiple_of(row * slots, 128), slots)
+
+            def band(head):
+                return pl.ds(pl.multiple_of(head * HD, 16), HD)
+
+            keys, values = qkvt[band(H + k), tokens], qkvt[band(H + KVH + k), tokens]
+            queries = jnp.concatenate([qkvt[band(ratio * k + g), tokens] for g in range(ratio)], 1)
+            key = lax.broadcasted_iota(jnp.int32, (slots, ratio * slots), 0)
+            query = lax.rem(lax.broadcasted_iota(jnp.int32, (slots, ratio * slots), 1), slots)
+            valid = mask[pl.ds(pl.multiple_of(row * slots, 128), slots), :] > 0.0
+            scores = pair_scores(keys, queries, (key <= query) & valid)
+            top = jnp.max(scores, 0, keepdims=True)
+            total = top + jnp.log(jnp.sum(jnp.exp(scores - top), 0, keepdims=True))
+            probs = jnp.exp(scores - total).astype(bf16)
+            out = jnp.dot(values, probs, preferred_element_type=f32).astype(bf16)
+            for g in range(ratio):
+                ot[band(ratio * k + g), tokens] = out[:, g * slots : (g + 1) * slots]
+            return carry
+
+        split = rows * KVH // 2
+        turn = t - first[2] - after
+
+        @pl.when((turn >= 1) & (turn <= 2))
+        def _():
+            lax.fori_loop((turn - 1) * split, turn * split, heads, 0)
+
+        @pl.when(turn == 2)
+        def _():
+            into(2, 0, in_wide.at[len(places) - 1]).wait()
+            y[...] = x[...].astype(f32) + lax.dot_general(
+                ot[...], one_matrix(in_wide[len(places) - 1]), down_rows, preferred_element_type=f32
+            )
+            n2[...] = scaled_norm(y[...], gain_rows[1:2, :])[1]
+
+        c3 = i3 - 2
+        size = in_gate.shape[3]
+
+        @pl.when((c3 >= 0) & (c3 < families[3][0]))
+        def _():
+            room = lax.rem(c3, ROOMS)
+            into(3, c3, in_gate.at[room]).wait()
+            value = jnp.dot(n2[...], one_matrix(in_gate[room]), preferred_element_type=f32)
+
+            @pl.when(lax.rem(c3, 2) == 0)
+            def _():
+                gate[...] = value
+
+            @pl.when(lax.rem(c3, 2) == 1)
+            def _():
+                opened = gate[...]
+                inner[:, pl.ds(pl.multiple_of(lax.div(c3, 2) * size, 128), size)] = (
+                    opened / (1.0 + jnp.exp(-opened)) * value
+                ).astype(bf16)
+
+        c4 = i4 - 2
+
+        @pl.when((c4 >= 0) & (c4 < families[4][0]))
+        def _():
+            room = lax.rem(c4, ROOMS)
+            into(4, c4, in_down.at[room]).wait()
+            place = columns(4, c4)
+            value = y[:, place] + jnp.dot(inner[...], one_matrix(in_down[room]), preferred_element_type=f32)
+            first_out[:, place] = (value * mask[...]).astype(bf16)
 
     def step(t, carry):
         for f, (pieces, _, parts_first) in enumerate(families):
@@ -1065,19 +1203,23 @@
                             if parts_first:
                                 along(f, i, o, part, False, True, True)
                             to_core(f, i, o, part).start()
+        if rows:
+            forward(t)
         return carry
 
-    lax.fori_loop(0, total + W_HOP * (G + 1), step, 0)
+    lax.fori_loop(0, total + max(W_HOP * (G + 1), W_HOP * G + AFTER + 2), step, 0)
 
     for f, (pieces, _, parts_first) in enumerate(families):
         def drain(i, carry, f=f, parts_first=parts_first):
-            own_copy(f, i).wait()
+            if not rows:
+                own_copy(f, i).wait()
 
             def by_group(o, carry):
                 for k in range(A):
                     part = lax.rem(a + k, A)
                     to_core(f, i, o, part).wait_send()
-                    from_core(f, i, o, k).wait_recv()
+                    if not rows:
+                        from_core(f, i, o, k).wait_recv()
                     if parts_first or k == 0:
                         @pl.when((z < G - 1) & (o <= z))
                         def _(part=part):
@@ -1100,55 +1242,74 @@
         lax.fori_loop(0, pieces, drain, 0)
 
 
-def gathered(groups, dp, shards, families):
-    A, DMA = dp // 2, pltpu.SemaphoreType.DMA
-    any_space = pl.BlockSpec(memory_space=pl.ANY)
+def gathered(groups, dp, shards, families, tokens):
+    A, DMA, bf16, f32 = dp // 2, pltpu.SemaphoreType.DMA, jnp.bfloat16, jnp.float32
+    any_space, in_vmem = pl.BlockSpec(memory_space=pl.ANY), pl.BlockSpec(memory_space=pltpu.VMEM)
+    devices, shape = groups * dp, jax.ShapeDtypeStruct
     scratch = []
     for pieces, _, parts_first in families:
         on_line = (pieces, groups, A if parts_first else 1)
         scratch += [DMA(on_line)] * 4 + [DMA((pieces, groups, max(A - 1, 1)))] * 2 + [DMA((pieces, groups, A))] * 2
         scratch += [DMA((pieces,))]
+    outs = tuple(shape((devices,) + x.shape, x.dtype) for x in shards)
+    extra, rows = (), 0
+    if tokens is not None:
+        x, mask, tables, rows = tokens
+        extra = (x, mask) + tables
+        count, width = x.shape
+        hidden = devices * shards[4].shape[0]
+        outs += (shape((8, width), f32), shape((count, width), bf16))
+
+        def room(f, rooms):
+            return pltpu.VMEM((rooms, devices, shards[f].shape[0], shards[f].shape[1] // families[f][0]), bf16)
+
+        scratch += [
+            pltpu.VMEM((devices,) + shards[0].shape, bf16), room(1, families[1][0] + 1), room(3, ROOMS), room(4, ROOMS),
+            DMA((sum(family[0] for family in families),)),
+            pltpu.VMEM((count, width), bf16), pltpu.VMEM((shards[1].shape[1], count), bf16),
+            pltpu.VMEM((width, count), bf16), pltpu.VMEM((count, width), f32), pltpu.VMEM((count, width), bf16),
+            pltpu.VMEM((count, shards[3].shape[1] // families[3][0]), f32), pltpu.VMEM((count, hidden), bf16),
+        ]
     return pl.pallas_call(
-        functools.partial(gather_kernel, groups, A, families),
-        out_shape=tuple(jax.ShapeDtypeStruct((groups * dp,) + x.shape, x.dtype) for x in shards),
-        in_specs=[any_space] * len(shards),
-        out_specs=(any_space,) * len(shards),
+        functools.partial(gather_kernel, groups, A, families, rows),
+        out_shape=outs,
+        in_specs=[any_space] * len(shards) + [in_vmem] * len(extra),
+        out_specs=(any_space,) * len(shards) + (in_vmem,) * (2 if rows else 0),
         scratch_shapes=scratch,
-        compiler_params=pltpu.CompilerParams(collective_id=5, has_side_effects=True),
-    )(*shards)
+        compiler_params=pltpu.CompilerParams(
+            collective_id=5, has_side_effects=True, vmem_limit_bytes=56 * 1024 * 1024
+        ),
+    )(*shards, *extra)
 
 
 def body(
     inputs_x, cotangent, lengths, attn_gain, qkv_weight, out_weight, ffn_gain, gate_up, down_weight
 ):
     is_first = lax.axis_index("section") == 0
-    gains = jnp.concatenate([attn_gain, ffn_gain], 0)
-    gains = jnp.pad(gains, ((0, 14), (0, -gains.shape[1] % 128)))
-    gains, qkv_all, out_all, gate_up_all, down_all = gathered(
-        lax.axis_size("group"),
-        lax.axis_size("dp"),
-        (gains, qkv_weight[0], out_weight[0], gate_up[0], down_weight[0]),
-        gather_families,
-    )
-    gain_part = attn_gain.shape[1]
-    weights = (
-        gains[:, 0, :gain_part].reshape(-1),
-        flat(qkv_all),
-        flat(out_all),
-        gains[:, 1, :gain_part].reshape(-1),
-        flat(gate_up_all),
-        flat(down_all),
-    )
     rows, slots, width = inputs_x.shape
     tables = turned_tables(slots, rows)
     info = jnp.concatenate([lengths, is_first.astype(jnp.int32)[None]])
     mask = padding(lengths, slots).reshape(-1, 1)
-    gain_one = weights[0].astype(jnp.float32).reshape(1, -1)
-    gain_two = weights[3].astype(jnp.float32).reshape(1, -1)
-    qkv_w, output_weight, _, gate_up_w, down_w = weights[1:]
+    gains = jnp.concatenate([attn_gain, ffn_gain], 0).T
+    gains = jnp.pad(gains, ((0, 0), (0, 128 - gains.shape[1])))
+    shards = (gains, qkv_weight[0], out_weight[0], gate_up[0], down_weight[0])
+    together = gains.shape[0] % 16 == 0
+    tokens = (flat(inputs_x), mask, tables, rows) if together else None
+    gathered_all = gathered(
+        lax.axis_size("group"), lax.axis_size("dp"), shards, gather_families, tokens
+    )
+    gains_all, qkv_w, output_weight, gate_up_w, down_w = (flat(x) for x in gathered_all[:5])
+    if together:
+        gain_rows, first_out = gathered_all[5:]
+    else:
+        gain_rows = gains_all[:, :2].astype(jnp.float32).T
+    gain_one, gain_two = gain_rows[0:1], gain_rows[1:2]
     dz_given = (flat(cotangent).astype(jnp.float32) * mask).astype(jnp.bfloat16)
-    after_one = attention_forward(info, flat(inputs_x), gain_one, tables, qkv_w, output_weight, rows)[0]
-    first_out = ffn_forward(after_one, gain_two, mask, gate_up_w, down_w)
+    if not together:
+        after_one = attention_forward(
+            info, flat(inputs_x), gain_one, tables, qkv_w, output_weight, rows
+        )[0]
+        first_out = ffn_forward(after_one, gain_two, mask, gate_up_w, down_w)
     recv_act = passed_along(first_out, "section", 1)
     layer_in = jnp.where(is_first, flat(inputs_x), recv_act)
     after, heads, log_total, attention_turned, normed_turned = attention_forward(

time: 793 us -> 778 us (0.981)
  Pallas kernels: 716 us -> 702 us
    pallas_call x2 -> x1, Pallas kernels: 26.7 us -> 12.5 us  [attention_forward(): pl.pallas_call(functools.partial(attention_forward_kernel, rows), grid=(c...]
    pallas_call x2 -> x1, Pallas kernels: 285 us -> 284 us  [gathered(): pl.pallas_call(functools.partial(gather_kernel, groups, A, families, rows...]
where the time goes in v7:
time: 778 us; the launch traced here: 774 us
  Pallas kernels  702 us (90%)
  waiting for transfers between devices  33.5 us (4%)
  other arithmetic  23.4 us (3%)
  local copies, waits for them, and re-layouts  8.07 us (1%)
    pallas_call x1, Pallas kernels, summed_grads(): pl.pallas_call(functools.partial(grad_kernel, plan), out_shape=(jax.Shape...  315 us
    pallas_call x1, Pallas kernels, gathered(): pl.pallas_call(functools.partial(gather_kernel, groups, A, families, rows...  284 us
    pallas_call x2, Pallas kernels, ffn_backward(): pl.pallas_call(functools.partial(ffn_backward_kernel, keep), grid=(steps,...  60.6 us
    ppermute x2, waiting for transfers between devices, passed_along(): return lax.ppermute(value, axis, pairs)  33.5 us
    pallas_call x2, Pallas kernels, attention_backward(): pl.pallas_call(functools.partial(attention_backward_kernel, rows, keep),...  29.5 us
    broadcast_in_dim x4, other arithmetic, body(): shard_sum[None]  19 us
  transfers between devices with their start and end apart: 2, of which 2 were waited for; matrix products, arithmetic and copies ran while one was open for 0% of the time, Pallas kernels for 0%

profile of v7, /device:TPU:0, one launch (start us, length us, event | category | flops | bytes accessed | tf_op | source)
XLA Modules:
  0.0 773.7 jit_solution(3572055398805762133)
XLA Ops:
  0.8 0.7 fusion.4
  1.5 0.8 copy.25.refs_6_.mask
  2.4 0.7 pad_maximum_fusion
  3.2 0.6 copy_bitcast_fusion
  4.5 284.4 %shard_map.152 = (bf16[16,96,128]{2,1,0:T(8,128)(2,1)}, bf16[16,96,3072]{2,1,0:T(8,128)(2,1)}, bf16[16,96,1536]{2,1,0:T(8,128)(2,1)}, bf16[16,96,8192]{2,1,0:T(8...) custom-call(bf16[96,128]{1,0:T(8,128)(2,1)} %pad.8.refs_0_, ...), custom_call_target="tpu_custom_call" | custom-call | tf_op jit(solution)/shard_map/pallas_call | solution.py:1273
  288.9 3.8 collective-permute-start
  292.8 0.9 fusion.6
  294.0 15.0 %collective-permute-done = bf16[256,1536]{1,0:T(8,128)(2,1)S(1)} collective-permute-done((bf16[256,1536]{1,0:T(8,128)(2,1)}, bf16[256,1536]{1,0:T(8,128)(2,1)S(1)}, u32[]{:S(2)}, u32[]{:S(2)}) %collective-permute-start) | collective-permute-done | bytes 786464 | tf_op jit(solution)/shard_map/ppermute | solution.py:25
  309.2 2.3 copy-done
  311.5 12.5 %shard_map.153 = (f32[256,1536]{1,0:T(8,128)S(1)}, bf16[3072,256]{1,0:T(8,128)(2,1)S(1)}, f32[16,256]{1,0:T(8,128)S(1)}, bf16[1536,256]{1,0:T(8,128)(2,1)S(1)}, bf16[1536,256]{1,0:T(8,128)(2,1)S(1)}) custom-call(s32[3]{0:T(128)S(1)} %pad_add_fusion.info, bf16[256,1536]{1,0:T(8,128)(2,1)S(1)} %broadcast_select_fusion.x, ...), custom_call_target="tpu_custom_call" | custom-call | flops 3623878656 | bytes 14155776 | tf_op jit(solution)/shard_map/pallas_call | solution.py:332
  324.1 24.8 %shard_map.154 = (f32[256,1536]{1,0:T(8,128)S(1)}, bf16[256,1536]{1,0:T(8,128)(2,1)S(1)}, f32[1,1536]{1,0:T(1,128)}) custom-call(f32[256,1536]{1,0:T(8,128)S(1)} %get-tuple-element.39.y, bf16[256,1536]{1,0:T(8,128)(2,1)S(1)} %fusion.dz, f32[1,1536]{1,0:T(1,128)S(1)} %get-tuple-element.64.gain, f32[256,1]{1,0:T(8,128)S(1)} %copy-done.5, ...), custom_call_target="tpu_custom_call" | custom-call | flops 16106127360 | bytes 37748736 | tf_op jit(solution)/shard_map/pallas_call | solution.py:158
  349.0 13.5 %shard_map.155 = bf16[256,1536]{1,0:T(8,128)(2,1)S(1)} custom-call(s32[3]{0:T(128)S(1)} %pad_add_fusion.info, bf16[256,1536]{1,0:T(8,128)(2,1)S(1)} %broadcast_select_fusion.x, f32[1,1536]{1,0:T(1,128)S(1)} %get-tuple-element.65.gain, f32[256,1536]{1,0:T(8,128)S(1)} %get-tuple-element.42.dy, bf16[256,1536]{1,0:T(8,128)(2,1)S(1)} %get-tuple-element.43.dyb, ...), custom_call_target="tpu_custom_call" | custom-call | flops 3623878656 | bytes 14155776 | tf_op jit(solution)/shard_map/pallas_call | solution.py:366
  362.5 1.4 collective-permute-start.1
  363.9 18.5 %collective-permute-done.1 = bf16[256,1536]{1,0:T(8,128)(2,1)} collective-permute-done((bf16[256,1536]{1,0:T(8,128)(2,1)S(1)}, bf16[256,1536]{1,0:T(8,128)(2,1)}, u32[]{:S(2)}, u32[]{:S(2)}) %collective-permute-start.1) | collective-permute-done | bytes 786464 | tf_op jit(solution)/shard_map/ppermute | solution.py:25
  382.4 1.8 fusion.1.dz
  384.2 35.8 %shard_map.156 = (f32[256,1536]{1,0:T(8,128)S(1)}, bf16[256,1536]{1,0:T(8,128)(2,1)S(1)}, f32[1,1536]{1,0:T(1,128)S(1)}, bf16[4096,256]{1,0:T(8,128)(2,1)}, bf16...) custom-call(f32[256,1536]{1,0:T(8,128)S(1)} %copy-done.3, ...), custom_call_target="tpu_custom_call" | custom-call | flops 16106127360 | bytes 37748736 | tf_op jit(solution)/shard_map/pallas_call | solution.py:158
  420.0 16.0 %shard_map.157 = (f32[256,1536]{1,0:T(8,128)}, f32[1,1536]{1,0:T(1,128)S(1)}, bf16[256,3072]{1,0:T(8,128)(2,1)S(1)}) custom-call(s32[3]{0:T(128)S(1)} %pad_add_fusion.info, bf16[256,1536]{1,0:T(8,128)(2,1)S(1)} %broadcast_select_fusion.x, f32[1,1536]{1,0:T(1,128)S(1)} %get-tuple-element.65.gain, f32[256,1536]{1,0:T(8,128)S(1)} %get-tuple-element.47.dy, ...), custom_call_target="tpu_custom_call" | custom-call | flops 3623878656 | bytes 14155776 | tf_op jit(solution)/shard_map/pallas_call | solution.py:366
  436.0 1.1 copy-done.9
  437.8 315.3 %shard_map.158 = (bf16[384,11264]{1,0:T(8,128)(2,1)}, bf16[1408,1536]{1,0:T(8,128)(2,1)}, f32[8,1536]{1,0:T(8,128)}) custom-call(bf16[4096,256]{1,0:T(8,128)(2,1)} %get-tuple-element.50.at, bf16[1536,256]{1,0:T(8,128)(2,1)} %copy-done.10, bf16[1536,256]{1,0:T(8,128)(2,1)} %copy-done.12, bf16[1536,256]{1,0:T(8,128)(2,1)} %copy-done.11, ...), custom_call_target="tpu_custom_call" | custom-call | flops 13287555072 | bytes 40000000 | tf_op jit(solution)/shard_map/pallas_call | solution.py:886
  753.1 9.1 %bitcast_convert_fusion = f32[1,384,8192]{2,1,0:T(8,128)} fusion(bf16[384,11264]{1,0:T(8,128)(2,1)} %get-tuple-element.60), kind=kLoop, calls=%fused_computation | loop fusion | flops 3145728 | bytes 18874368 | tf_op jit(solution)/shard_map/broadcast_in_dim | solution.py:1361
  762.2 4.6 bitcast_convert_fusion.2
  766.8 3.6 bitcast_convert_fusion.1
  770.4 1.7 bitcast_convert_fusion.3
  772.0 1.4 fusion.5
  (42 shorter events, 2.1 us)
Async XLA Ops:
  3.2 289.6 %copy-start.16 = (s32[2]{0:T(128)S(1)}, s32[2]{0:T(128)}, u32[]{:S(2)}) copy-start(s32[2]{0:T(128)} %param.11) | copy-start | bytes 28
  3.2 290.6 %copy-start.15 = (bf16[2,128,1536]{2,1,0:T(8,128)(2,1)S(1)}, bf16[2,128,1536]{2,1,0:T(8,128)(2,1)}, u32[]{:S(2)}) copy-start(bf16[2,128,1536]{2,1,0:T(8,128)(2,1)} %param.10) | copy-start | bytes 2359300
  4.5 304.5 %copy-start.14 = (bf16[2,128,1536]{2,1,0:T(8,128)(2,1)S(1)}, bf16[2,128,1536]{2,1,0:T(8,128)(2,1)}, u32[]{:S(2)}) copy-start(bf16[2,128,1536]{2,1,0:T(8,128)(2,1)} %param.9) | copy-start | bytes 2359300
  288.9 20.3 %copy-start.6 = (f32[48,256]{1,0:T(8,128)S(1)}, f32[48,256]{1,0:T(8,128)}, u32[]{:S(2)}) copy-start(f32[48,256]{1,0:T(8,128)} %get-tuple-element.70.refs_8_.sines) | copy-start | bytes 147460
  288.9 20.2 %copy-start.7 = (f32[48,256]{1,0:T(8,128)S(1)}, f32[48,256]{1,0:T(8,128)}, u32[]{:S(2)}) copy-start(f32[48,256]{1,0:T(8,128)} %get-tuple-element.71.refs_7_.cosines) | copy-start | bytes 147460
  288.9 20.1 %collective-permute-start = (bf16[256,1536]{1,0:T(8,128)(2,1)}, bf16[256,1536]{1,0:T(8,128)(2,1)S(1)}, u32[]{:S(2)}, u32[]{:S(2)}) collective-permute-start(bf16[256,1536]{1,0:T(8,128)(2,1)} %get-tuple-element.35), channel_id=1, source_target_pairs={{0,16},{1,17},{2,18},{3,19},{4,20},{5,21},{6,22},{7,23},{8,24},{9,... | collective-permute-start | bytes 2359304 | tf_op jit(solution)/shard_map/ppermute | solution.py:25
  309.2 2.3 copy-start
  311.5 12.6 %copy-start.5 = (f32[256,1]{1,0:T(8,128)S(1)}, f32[256,1]{1,0:T(8,128)}, u32[]{:S(2)}) copy-start(f32[256,1]{1,0:T(8,128)} %copy.25.refs_6_.mask) | copy-start | bytes 3076
  324.1 24.9 %copy-start.2 = (f32[256,1536]{1,0:T(8,128)}, f32[256,1536]{1,0:T(8,128)S(1)}, u32[]{:S(2)}) copy-start(f32[256,1536]{1,0:T(8,128)S(1)} %get-tuple-element.39.y) | copy-start | bytes 4718596
  324.1 24.9 %copy-start.10 = (bf16[1536,256]{1,0:T(8,128)(2,1)}, bf16[1536,256]{1,0:T(8,128)(2,1)S(1)}, u32[]{:S(2)}) copy-start(bf16[1536,256]{1,0:T(8,128)(2,1)S(1)} %get-tuple-element.51.ot) | copy-start | bytes 2359300
  324.1 24.9 %copy-start.11 = (bf16[1536,256]{1,0:T(8,128)(2,1)}, bf16[1536,256]{1,0:T(8,128)(2,1)S(1)}, u32[]{:S(2)}) copy-start(bf16[1536,256]{1,0:T(8,128)(2,1)S(1)} %get-tuple-element.53.n1t) | copy-start | bytes 2359300
  324.1 24.9 %copy-start.1 = (bf16[3072,256]{1,0:T(8,128)(2,1)}, bf16[3072,256]{1,0:T(8,128)(2,1)S(1)}, u32[]{:S(2)}) copy-start(bf16[3072,256]{1,0:T(8,128)(2,1)S(1)} %get-tuple-element.44.qkvt) | copy-start | bytes 4718596
  362.5 21.7 %copy-start.3 = (f32[256,1536]{1,0:T(8,128)S(1)}, f32[256,1536]{1,0:T(8,128)}, u32[]{:S(2)}) copy-start(f32[256,1536]{1,0:T(8,128)} %copy-done.2) | copy-start | bytes 4718596
  362.5 19.9 %collective-permute-start.1 = (bf16[256,1536]{1,0:T(8,128)(2,1)S(1)}, bf16[256,1536]{1,0:T(8,128)(2,1)}, u32[]{:S(2)}, u32[]{:S(2)}) collective-permute-start(bf16[256,1536]{1,0:T(8,128)(2,1)S(1)} %shard_map.155), channel_id=1, source_target_pairs={{16,0},{17,1},{18,2},{19,3},{20,4},{21,5},{22,6},{23,7},{24,8},{25... | collective-permute-start | bytes 2359304 | tf_op jit(solution)/shard_map/ppermute | solution.py:25
  384.2 35.8 %copy-start.4 = (bf16[256,1536]{1,0:T(8,128)(2,1)}, bf16[256,1536]{1,0:T(8,128)(2,1)S(1)}, u32[]{:S(2)}) copy-start(bf16[256,1536]{1,0:T(8,128)(2,1)S(1)} %fusion.1.dz) | copy-start | bytes 2359300
  420.0 16.0 %copy-start.8 = (bf16[256,1536]{1,0:T(8,128)(2,1)}, bf16[256,1536]{1,0:T(8,128)(2,1)S(1)}, u32[]{:S(2)}) copy-start(bf16[256,1536]{1,0:T(8,128)(2,1)S(1)} %get-tuple-element.48.dyb.dy) | copy-start | bytes 2359300
  420.0 16.0 %copy-start.12 = (bf16[1536,256]{1,0:T(8,128)(2,1)}, bf16[1536,256]{1,0:T(8,128)(2,1)S(1)}, u32[]{:S(2)}) copy-start(bf16[1536,256]{1,0:T(8,128)(2,1)S(1)} %get-tuple-element.52.n2t) | copy-start | bytes 2359300
  436.0 1.1 copy-start.9
  762.2 4.6 copy-start.13

commit v8 on v7

--- a/solution.py
+++ b/solution.py
@@ -23,6 +23,10 @@
     length = lax.axis_size(axis)
     pairs = [(i, i + by) for i in range(length) if 0 <= i + by < length]
     return lax.ppermute(value, axis, pairs)
+
+
+def swapped(value, axis):
+    return lax.ppermute(value, axis, [(i, i ^ 1) for i in range(lax.axis_size(axis))])
 
 
 def padding(lengths, slot_count):
@@ -88,85 +92,126 @@
     )(y, gain, mask, gate_up_w, gate_up_w, down_w)
 
 
-def ffn_backward_kernel(keep, y, dz, gain, mask, wg, wu, wd, dy, dyb, gain_grad, *rest):
-    if keep:
-        at, dgate, dup, n2t, out, n2, scale, acc, zacc = rest
-    else:
-        n2, scale, acc = rest
+def ffn_prepare_kernel(y, gain, mask, wg, wu, wd, at, by_gate, by_up, n2t, out, n2, acc):
     j = pl.program_id(0)
     bf16, f32 = jnp.bfloat16, jnp.float32
 
     @pl.when(j == 0)
     def _():
-        r, n = scaled_norm(y[...], gain[...])
+        n = scaled_norm(y[...], gain[...])[1]
         n2[...] = n
-        scale[...] = r
-        acc[...] = jnp.zeros_like(acc)
-        if keep:
-            n2t[...] = n.T
-            zacc[...] = y[...]
+        n2t[...] = n.T
+        acc[...] = y[...]
 
     gate = jnp.dot(n2[...], wg[...], preferred_element_type=f32)
     up = jnp.dot(n2[...], wu[...], preferred_element_type=f32)
-    grad = lax.dot_general(dz[...], wd[...], across, preferred_element_type=f32)
     sig = 1.0 / (1.0 + jnp.exp(-gate))
     silu = gate * sig
-    grad_gate = (grad * up * sig * (1.0 + gate * (1.0 - sig))).astype(bf16)
-    grad_up = (grad * silu).astype(bf16)
-    if keep:
-        hidden = (silu * up).astype(bf16)
-        at[...] = hidden.T
+    hidden = (silu * up).astype(bf16)
+    at[...] = hidden.T
+    by_gate[...] = (up * sig * (1.0 + gate * (1.0 - sig))).astype(bf16)
+    by_up[...] = silu.astype(bf16)
+    acc[...] += jnp.dot(hidden, wd[...], preferred_element_type=f32)
+
+    @pl.when(j == pl.num_programs(0) - 1)
+    def _():
+        out[...] = (acc[...] * mask[...]).astype(bf16)
+
+
+def ffn_prepare(y, gain, mask, gate_up_w, down_w):
+    tokens, width = y.shape
+    hidden = down_w.shape[0]
+    steps, whole, row, weights = ffn_specs(tokens, width, hidden)
+    shape, bf16 = jax.ShapeDtypeStruct, jnp.bfloat16
+    part = pl.BlockSpec((tokens, FF_CHUNK), lambda j: (0, j))
+    return pl.pallas_call(
+        ffn_prepare_kernel,
+        grid=(steps,),
+        out_shape=(
+            shape((hidden, tokens), bf16), shape((tokens, hidden), bf16), shape((tokens, hidden), bf16),
+            shape((width, tokens), bf16), shape((tokens, width), bf16),
+        ),
+        in_specs=[whole, row, pl.BlockSpec((tokens, 1), lambda j: (0, 0))] + weights,
+        out_specs=(
+            pl.BlockSpec((FF_CHUNK, tokens), lambda j: (j, 0)), part, part,
+            pl.BlockSpec((width, tokens), lambda j: (0, 0)), whole,
+        ),
+        scratch_shapes=[pltpu.VMEM((tokens, width), bf16), pltpu.VMEM((tokens, width), jnp.float32)],
+        compiler_params=pltpu.CompilerParams(vmem_limit_bytes=48 * 1024 * 1024),
+        cost_estimate=pl.CostEstimate(
+            flops=6 * tokens * width * hidden, bytes_accessed=6 * width * hidden, transcendentals=tokens * hidden
+        ),
+    )(y, gain, mask, gate_up_w, gate_up_w, down_w)
+
+
+def ffn_backward_kernel(prepared, y, dz, gain, wg, wu, wd, *rest):
+    bf16, f32 = jnp.bfloat16, jnp.float32
+    if prepared:
+        by_gate, by_up, dy, dyb, gain_grad, dgate, dup, acc = rest
+    else:
+        dy, dyb, gain_grad, n2, acc = rest
+    j = pl.program_id(0)
+
+    @pl.when(j == 0)
+    def _():
+        acc[...] = jnp.zeros_like(acc)
+        if not prepared:
+            n2[...] = scaled_norm(y[...], gain[...])[1]
+
+    grad = lax.dot_general(dz[...], wd[...], across, preferred_element_type=f32)
+    if prepared:
+        grad_gate = (grad * by_gate[...].astype(f32)).astype(bf16)
+        grad_up = (grad * by_up[...].astype(f32)).astype(bf16)
         dgate[...] = grad_gate
         dup[...] = grad_up
-        zacc[...] += jnp.dot(hidden, wd[...], preferred_element_type=f32)
+    else:
+        gate = jnp.dot(n2[...], wg[...], preferred_element_type=f32)
+        up = jnp.dot(n2[...], wu[...], preferred_element_type=f32)
+        sig = 1.0 / (1.0 + jnp.exp(-gate))
+        grad_gate = (grad * up * sig * (1.0 + gate * (1.0 - sig))).astype(bf16)
+        grad_up = (grad * (gate * sig)).astype(bf16)
     acc[...] += lax.dot_general(grad_gate, wg[...], across, preferred_element_type=f32) + lax.dot_general(
         grad_up, wu[...], across, preferred_element_type=f32
     )
 
     @pl.when(j == pl.num_programs(0) - 1)
     def _():
-        value, r, grad_normed = y[...], scale[...], acc[...]
+        value, grad_normed = y[...], acc[...]
+        r = lax.rsqrt(jnp.mean(value * value, -1, keepdims=True) + norm_eps)
         scaled = grad_normed * gain[...]
         gain_grad[...] = jnp.sum(grad_normed * value * r, axis=0, keepdims=True)
         inner = jnp.mean(value * scaled, -1, keepdims=True)
         total = dz[...].astype(f32) + r * scaled - value * (r * r * r) * inner
         dy[...] = total
         dyb[...] = total.astype(bf16)
-        if keep:
-            out[...] = (zacc[...] * mask[...]).astype(bf16)
-
-
-def ffn_backward(y, dz, gain, mask, gate_up_w, down_w, keep):
+
+
+def ffn_backward(y, dz, gain, gate_up_w, down_w, factors=()):
     tokens, width = y.shape
     hidden = down_w.shape[0]
     steps, whole, row, weights = ffn_specs(tokens, width, hidden)
     shape, bf16, f32 = jax.ShapeDtypeStruct, jnp.bfloat16, jnp.float32
     outs = [shape((tokens, width), f32), shape((tokens, width), bf16), shape((1, width), f32)]
     out_specs = [whole, whole, row]
-    scratch = [pltpu.VMEM((tokens, width), bf16), pltpu.VMEM((tokens, 1), f32), pltpu.VMEM((tokens, width), f32)]
-    if keep:
-        part = pl.BlockSpec((tokens, FF_CHUNK), lambda j: (0, j))
-        outs += [
-            shape((hidden, tokens), bf16), shape((tokens, hidden), bf16), shape((tokens, hidden), bf16),
-            shape((width, tokens), bf16), shape((tokens, width), bf16),
-        ]
-        out_specs += [
-            pl.BlockSpec((FF_CHUNK, tokens), lambda j: (j, 0)), part, part,
-            pl.BlockSpec((width, tokens), lambda j: (0, 0)), whole,
-        ]
-        scratch += [pltpu.VMEM((tokens, width), f32)]
+    scratch = [pltpu.VMEM((tokens, width), f32)]
+    parts = [pl.BlockSpec((tokens, FF_CHUNK), lambda j: (0, j))] * len(factors)
+    if factors:
+        outs += [shape((tokens, hidden), bf16)] * 2
+        out_specs += parts
+    else:
+        scratch = [pltpu.VMEM((tokens, width), bf16)] + scratch
     return pl.pallas_call(
-        functools.partial(ffn_backward_kernel, keep),
+        functools.partial(ffn_backward_kernel, bool(factors)),
         grid=(steps,),
         out_shape=tuple(outs),
-        in_specs=[whole, whole, row, pl.BlockSpec((tokens, 1), lambda j: (0, 0))] + weights,
+        in_specs=[whole, whole, row] + weights + parts,
         out_specs=tuple(out_specs),
         scratch_shapes=scratch,
         compiler_params=pltpu.CompilerParams(vmem_limit_bytes=48 * 1024 * 1024),
         cost_estimate=pl.CostEstimate(
             flops=10 * tokens * width * hidden, bytes_accessed=6 * width * hidden, transcendentals=tokens * hidden
         ),
-    )(y, dz, gain, mask, gate_up_w, gate_up_w, down_w)
+    )(y, dz, gain, gate_up_w, gate_up_w, down_w, *factors)
 
 
 def turned_tables(slots, rows):
@@ -420,7 +465,7 @@
 
 
 def grad_kernel(
-    plan, at, ot, n2t, n1t, dz, dy, dgate, dup, dq, gp, outy, outz, outg,
+    plan, at, ot, n2t, n1t, at2, ot2, n2t2, n1t2, dz, dy, dgate, dup, dq, gp, outy, outz, outg,
     LT, RH, YS, YR, YRT, YLT, ZRT, ZLT, ZX,
     own_sem, xs, xr, ys_s, ys_r, yr_s, yr_r, yl_s, yl_r, zr_s, zr_r, zl_s, zl_r,
     zx_s, zx_r, ag_s, ag_r, sib_s, sib_r, lo,
@@ -448,13 +493,15 @@
         pl.semaphore_signal(barrier, inc=1, device_id=dev, device_id_type=MESH)
     pl.semaphore_wait(barrier, A + 2)
 
-    lhs = [(at, 0, hidden), (ot, hidden, width), (n2t, hidden + width, width), (n1t, hidden + 2 * width, width)]
+    lhs = [
+        (at, at2, 0, hidden), (ot, ot2, hidden, width), (n2t, n2t2, hidden + width, width),
+        (n1t, n1t2, hidden + 2 * width, width),
+    ]
     rhs = [(dz, 0, half), (dy, half, half), (None, width, hidden), (dq, width + hidden, plan["qkv_cols"] // 2)]
-    order = [(0, 0), (2, 2), (1, 1), (3, 3)]
     own, cross = {}, {}
-    for i, (ref, row, rows) in enumerate(lhs):
+    for i, (ref, theirs, row, rows) in enumerate(lhs):
         own[0, i] = pltpu.make_async_copy(ref, LT.at[pl.ds(row, rows), pl.ds(0, T)], own_sem.at[i])
-        cross[0, i] = remote(ref, LT.at[pl.ds(row, rows), pl.ds(T, T)], xs.at[i], xr.at[i], sib)
+        own[2, i] = pltpu.make_async_copy(theirs, LT.at[pl.ds(row, rows), pl.ds(T, T)], own_sem.at[8 + i])
     for i, (ref, col, cols) in enumerate(rhs):
         if ref is None:
             continue
@@ -467,22 +514,26 @@
         own[1, 2, core] = pltpu.make_async_copy(mine, RH.at[pl.ds(0, T), pl.ds(col, cols)], own_sem.at[6])
         cross[1, 2, core] = remote(theirs, RH.at[pl.ds(T, T), pl.ds(col, cols)], xs.at[6], xr.at[6], sib)
     own[1, 2], cross[1, 2] = own[1, 2, 0], cross[1, 2, 0]
-    for i, _ in order:
-        for side in (0, 1):
-            if (side, i) == (1, 2):
-                for core in (0, 1):
-                    @pl.when(c == core)
-                    def _(core=core):
-                        own[1, 2, core].start()
-                        cross[1, 2, core].start()
-            else:
-                own[side, i].start()
-                cross[side, i].start()
+    def fetch(i):
+        if i == 2:
+            for core in (0, 1):
+                @pl.when(c == core)
+                def _(core=core):
+                    cross[1, 2, core].start()
+                    own[1, 2, core].start()
+        else:
+            cross[1, i].start()
+            own[1, i].start()
+        own[0, i].start()
+        own[2, i].start()
+
+    fetch(0)
+    fetch(2)
 
     def operands_here(i):
-        for side in (0, 1):
+        for side in (0, 2, 1):
             own[side, i].wait()
-            cross[side, i].wait_recv()
+        cross[1, i].wait_recv()
 
     def product(row, rows, col, cols):
         return jnp.dot(
@@ -663,8 +714,10 @@
         def _():
             operands_here(0)
             operands_here(2)
-
-        @pl.when(t == 1)
+            fetch(1)
+            fetch(3)
+
+        @pl.when(t == jnp.minimum(plan["pieces_gate"], plan["down_chunks"] * plan["z_split"]) - 1)
         def _():
             operands_here(1)
             operands_here(3)
@@ -837,8 +890,7 @@
         gain_left().wait_send()
 
     for i in range(4):
-        for side in (0, 1):
-            cross[side, i].wait_send()
+        cross[1, i].wait_send()
 
     def drain_y(q, carry):
         for k in range(1, A):
@@ -874,9 +926,9 @@
     lax.fori_loop(0, nZ, drain_z, 0)
 
 
-def summed_grads(groups, dp, at, ot, n2t, n1t, dz, dy, dgate, dup, dq, gain_parts):
-    hidden, tokens = at.shape
-    width, qkv_cols = ot.shape[0], dq.shape[1]
+def summed_grads(groups, dp, activations, others, dz, dy, dgate, dup, dq, gain_parts):
+    hidden, tokens = activations[0].shape
+    width, qkv_cols = dz.shape[1], dq.shape[1]
     plan = grad_plan(groups, dp, tokens, width, hidden, qkv_cols)
     G, A, nY, nZ = groups, plan["pairs"], plan["pieces"], plan["z_pieces"]
     block, zr, zc = plan["block"], plan["z_rows"], plan["z_cols"]
@@ -890,7 +942,7 @@
             jax.ShapeDtypeStruct((plan["down_block"] + block, width), bf16),
             jax.ShapeDtypeStruct(gain_parts.shape, f32),
         ),
-        in_specs=[any_space] * 9 + [in_vmem],
+        in_specs=[any_space] * 13 + [in_vmem],
         out_specs=(any_space, any_space, in_vmem),
         scratch_shapes=[
             pltpu.VMEM((hidden + 3 * width, 2 * tokens), bf16),
@@ -902,7 +954,7 @@
             pltpu.VMEM((nZ, G - 1, zr, zc), bf16),
             pltpu.VMEM((nZ, G - 1, zr, zc), bf16),
             pltpu.VMEM((nZ, A, zr, zc), bf16),
-            DMA((8,)), DMA((8,)), DMA((8,)),
+            DMA((12,)), DMA((8,)), DMA((8,)),
             DMA((nY, A - 1)), DMA((nY, A - 1)),
             DMA((nY,)), DMA((nY,)), DMA((nY,)), DMA((nY,)),
             DMA((nZ,)), DMA((nZ,)), DMA((nZ,)), DMA((nZ,)),
@@ -924,7 +976,7 @@
             flops=2 * 2 * tokens * (width * (2 * hidden + qkv_cols + width) + hidden * width) // 2,
             bytes_accessed=40_000_000, transcendentals=0,
         ),
-    )(at, ot, n2t, n1t, dz, dy, dgate, dup, dq, gain_parts)
+    )(*activations, *others, dz, dy, dgate, dup, dq, gain_parts)
 
 
 W_HOP = 4
@@ -946,10 +998,10 @@
         (x, mask, cosines, sines), refs = refs[:4], refs[4:]
     wholes, refs = refs[:F], refs[F:]
     if rows:
-        (gain_rows, first_out), refs = refs[:2], refs[2:]
+        (gain_rows, first_out, handed), refs = refs[:3], refs[3:]
     sems, refs = refs[: 9 * F], refs[9 * F :]
     if rows:
-        in_gain, in_wide, in_gate, in_down, in_sem, n1, qkvt, ot, y, n2, gate, inner = refs
+        in_gain, in_wide, in_gate, in_down, in_sem, hand_s, hand_r, n1, qkvt, ot, y, n2, gate, inner = refs
     s, z, d = lax.axis_index("section"), lax.axis_index("group"), lax.axis_index("dp")
     c, a = lax.rem(d, 2), lax.div(d, 2)
     sib = (s, z, 2 * a + 1 - c)
@@ -960,9 +1012,12 @@
 
     barrier = pltpu.get_barrier_semaphore()
     others = [peer(lax.rem(a + k, A)) for k in range(1, A)]
-    for dev in [sib, (s, lax.rem(z + 1, G), d), (s, lax.rem(z + G - 1, G), d)] + others:
+    if rows:
+        others.append((1 - s, z, d))
+    others += [sib, (s, lax.rem(z + 1, G), d), (s, lax.rem(z + G - 1, G), d)]
+    for dev in others:
         pl.semaphore_signal(barrier, inc=1, device_id=dev, device_id_type=MESH)
-    pl.semaphore_wait(barrier, A + 2)
+    pl.semaphore_wait(barrier, len(others))
 
     def columns(f, i):
         pieces, halves, _ = families[f]
@@ -1036,6 +1091,13 @@
                 from_core(f, i, o, k).wait_recv()
 
         into(f, i, room).start()
+
+    def hand_over(i):
+        place = columns(4, i)
+        return pltpu.make_async_remote_copy(
+            src_ref=first_out.at[:, place], dst_ref=handed.at[:, place], send_sem=hand_s.at[i], recv_sem=hand_r.at[i],
+            device_id=(1 - s, z, d), device_id_type=MESH,
+        )
 
     def one_matrix(room):
         return room.reshape(room.shape[0] * room.shape[1], room.shape[2])
@@ -1153,6 +1215,7 @@
             place = columns(4, c4)
             value = y[:, place] + jnp.dot(inner[...], one_matrix(in_down[room]), preferred_element_type=f32)
             first_out[:, place] = (value * mask[...]).astype(bf16)
+            hand_over(c4).start()
 
     def step(t, carry):
         for f, (pieces, _, parts_first) in enumerate(families):
@@ -1208,6 +1271,10 @@
         return carry
 
     lax.fori_loop(0, total + max(W_HOP * (G + 1), W_HOP * G + AFTER + 2), step, 0)
+
+    if rows:
+        for i in range(families[4][0]):
+            hand_over(i).wait()
 
     for f, (pieces, _, parts_first) in enumerate(families):
         def drain(i, carry, f=f, parts_first=parts_first):
@@ -1258,14 +1325,14 @@
         extra = (x, mask) + tables
         count, width = x.shape
         hidden = devices * shards[4].shape[0]
-        outs += (shape((8, width), f32), shape((count, width), bf16))
+        outs += (shape((8, width), f32), shape((count, width), bf16), shape((count, width), bf16))
 
         def room(f, rooms):
             return pltpu.VMEM((rooms, devices, shards[f].shape[0], shards[f].shape[1] // families[f][0]), bf16)
 
         scratch += [
             pltpu.VMEM((devices,) + shards[0].shape, bf16), room(1, families[1][0] + 1), room(3, ROOMS), room(4, ROOMS),
-            DMA((sum(family[0] for family in families),)),
+            DMA((sum(family[0] for family in families),)), DMA((families[4][0],)), DMA((families[4][0],)),
             pltpu.VMEM((count, width), bf16), pltpu.VMEM((shards[1].shape[1], count), bf16),
             pltpu.VMEM((width, count), bf16), pltpu.VMEM((count, width), f32), pltpu.VMEM((count, width), bf16),
             pltpu.VMEM((count, shards[3].shape[1] // families[3][0]), f32), pltpu.VMEM((count, hidden), bf16),
@@ -1274,7 +1341,7 @@
         functools.partial(gather_kernel, groups, A, families, rows),
         out_shape=outs,
         in_specs=[any_space] * len(shards) + [in_vmem] * len(extra),
-        out_specs=(any_space,) * len(shards) + (in_vmem,) * (2 if rows else 0),
+        out_specs=(any_space,) * len(shards) + ((in_vmem, in_vmem, any_space) if rows else ()),
         scratch_shapes=scratch,
         compiler_params=pltpu.CompilerParams(
             collective_id=5, has_side_effects=True, vmem_limit_bytes=56 * 1024 * 1024
@@ -1300,7 +1367,7 @@
     )
     gains_all, qkv_w, output_weight, gate_up_w, down_w = (flat(x) for x in gathered_all[:5])
     if together:
-        gain_rows, first_out = gathered_all[5:]
+        gain_rows, _, recv_act = gathered_all[5:]
     else:
         gain_rows = gains_all[:, :2].astype(jnp.float32).T
     gain_one, gain_two = gain_rows[0:1], gain_rows[1:2]
@@ -1310,19 +1377,26 @@
             info, flat(inputs_x), gain_one, tables, qkv_w, output_weight, rows
         )[0]
         first_out = ffn_forward(after_one, gain_two, mask, gate_up_w, down_w)
-    recv_act = passed_along(first_out, "section", 1)
+        recv_act = passed_along(first_out, "section", 1)
     layer_in = jnp.where(is_first, flat(inputs_x), recv_act)
     after, heads, log_total, attention_turned, normed_turned = attention_forward(
         info, layer_in, gain_one, tables, qkv_w, output_weight, rows
     )
-    dy, dy_low, _ = ffn_backward(after, dz_given, gain_two, mask, gate_up_w, down_w, False)
+    dy, dy_low, _ = ffn_backward(after, dz_given, gain_two, gate_up_w, down_w)
     (second_dx,) = attention_backward(
         info, layer_in, gain_one, dy, dy_low, tables, heads, log_total, output_weight, qkv_w, rows, False
     )
     recv_grad = passed_along(second_dx, "section", -1)
+    after, second_dx = lax.optimization_barrier((after, second_dx))
+    hidden_turned, by_gate, by_up, normed_two_turned, result = ffn_prepare(
+        after, gain_two, mask, gate_up_w, down_w
+    )
+    activations = (hidden_turned, attention_turned, normed_two_turned, normed_turned)
+    recv_grad, activations, by_gate = lax.optimization_barrier((recv_grad, activations, by_gate))
+    others = tuple(swapped(x, "dp") for x in activations)
     dz = jnp.where(is_first, (recv_grad.astype(jnp.float32) * mask).astype(jnp.bfloat16), dz_given)
-    dy, dy_low, ffn_gain_part, hidden_turned, grad_gate, grad_up, normed_two_turned, result = ffn_backward(
-        after, dz, gain_two, mask, gate_up_w, down_w, True
+    dy, dy_low, ffn_gain_part, grad_gate, grad_up = ffn_backward(
+        after, dz, gain_two, gate_up_w, down_w, (by_gate, by_up)
     )
     grad_x, attn_gain_part, grad_qkv = attention_backward(
         info, layer_in, gain_one, dy, dy_low, tables, heads, log_total, output_weight, qkv_w, rows, True
@@ -1333,10 +1407,8 @@
     gate_qkv_sum, down_out_sum, gain_sums = summed_grads(
         lax.axis_size("group"),
         lax.axis_size("dp"),
-        hidden_turned,
-        attention_turned,
-        normed_two_turned,
-        normed_turned,
+        activations,
+        others,
         dz,
         dy_low,
         grad_gate,

time: 778 us -> 761 us (0.978)
  waiting for transfers between devices: 33.5 us -> 0.01 us
  Pallas kernels: 702 us -> 713 us
    ppermute x2 -> x1, waiting for transfers between devices: 33.5 us -> 0.01 us  [passed_along(): return lax.ppermute(value, axis, pairs)]
    pallas_call x1, Pallas kernels: 284 us -> 295 us  [gathered(): pl.pallas_call(functools.partial(gather_kernel, groups, A, families, rows...]
    pallas_call x2 -> x3, Pallas kernels: 60.6 us -> 64.6 us  [the longest x2 44.3 us: ffn_backward(): pl.pallas_call(functools.partial(ffn_backward_kernel, bool(factors)), gri...]
  transfers between devices with their start and end apart: 2 -> 5, of which waited for: 2 -> 0; matrix products, arithmetic and copies ran while one was open for 0% -> 0% of each run, Pallas kernels for 0% -> 8%
where the time goes in v8:
time: 761 us; the launch traced here: 752 us
  Pallas kernels  713 us (94%)
  other arithmetic  24.9 us (3%)
  local copies, waits for them, and re-layouts  10.8 us (1%)
    pallas_call x1, Pallas kernels, summed_grads(): pl.pallas_call(functools.partial(grad_kernel, plan), out_shape=(jax.Shape...  312 us
    pallas_call x1, Pallas kernels, gathered(): pl.pallas_call(functools.partial(gather_kernel, groups, A, families, rows...  295 us
    pallas_call x2, Pallas kernels, ffn_backward(): pl.pallas_call(functools.partial(ffn_backward_kernel, bool(factors)), gri...  44.3 us
    pallas_call x2, Pallas kernels, attention_backward(): pl.pallas_call(functools.partial(attention_backward_kernel, rows, keep),...  29.3 us
    pallas_call x1, Pallas kernels, ffn_prepare(): pl.pallas_call(ffn_prepare_kernel, grid=(steps,), out_shape=(shape((hidde...  20.3 us
    broadcast_in_dim x4, other arithmetic, body(): shard_sum[None]  19 us
  transfers between devices with their start and end apart: 5, of which 0 were waited for; matrix products, arithmetic and copies ran while one was open for 0% of the time, Pallas kernels for 8%

profile of v8, /device:TPU:0, one launch (start us, length us, event | category | flops | bytes accessed | tf_op | source)
XLA Modules:
  0.0 752.2 jit_solution(2072186776531763821)
XLA Ops:
  0.7 0.7 fusion.4
  1.4 0.7 pad_add_fusion.info
  2.1 0.7 pad_maximum_fusion
  2.9 0.8 copy.24.refs_6_.mask
  5.2 294.5 %shard_map.152 = (bf16[16,96,128]{2,1,0:T(8,128)(2,1)}, bf16[16,96,3072]{2,1,0:T(8,128)(2,1)}, bf16[16,96,1536]{2,1,0:T(8,128)(2,1)}, bf16[16,96,8192]{2,1,0:T(8...) custom-call(bf16[96,128]{1,0:T(8,128)(2,1)} %pad.8.refs_0_, ...), custom_call_target="tpu_custom_call" | custom-call | tf_op jit(solution)/shard_map/pallas_call | solution.py:1340
  299.9 0.9 fusion.6
  301.1 2.3 copy-done
  303.5 12.7 %shard_map.153 = (f32[256,1536]{1,0:T(8,128)S(1)}, bf16[3072,256]{1,0:T(8,128)(2,1)S(1)}, f32[16,256]{1,0:T(8,128)S(1)}, bf16[1536,256]{1,0:T(8,128)(2,1)S(1)}, bf16[1536,256]{1,0:T(8,128)(2,1)S(1)}) custom-call(s32[3]{0:T(128)S(1)} %pad_add_fusion.info, bf16[256,1536]{1,0:T(8,128)(2,1)S(1)} %broadcast_select_fusion.x, ...), custom_call_target="tpu_custom_call" | custom-call | flops 3623878656 | bytes 14155776 | tf_op jit(solution)/shard_map/pallas_call | solution.py:377
  316.2 0.9 copy-done.11
  317.0 23.7 %shard_map.154 = (f32[256,1536]{1,0:T(8,128)S(1)}, bf16[256,1536]{1,0:T(8,128)(2,1)S(1)}, f32[1,1536]{1,0:T(1,128)}) custom-call(f32[256,1536]{1,0:T(8,128)S(1)} %get-tuple-element.55.y, bf16[256,1536]{1,0:T(8,128)(2,1)S(1)} %fusion.dz, f32[1,1536]{1,0:T(1,128)S(1)} %get-tuple-element.82.gain, bf16[1536,8192]{1,0:T(8,128)(2,1)} %bitcast.43, ...), custom_call_target="tpu_custom_call" | custom-call | flops 16106127360 | bytes 37748736 | tf_op jit(solution)/shard_map/pallas_call | solution.py:203
  340.7 13.6 %shard_map.155 = bf16[256,1536]{1,0:T(8,128)(2,1)S(1)} custom-call(s32[3]{0:T(128)S(1)} %pad_add_fusion.info, bf16[256,1536]{1,0:T(8,128)(2,1)S(1)} %broadcast_select_fusion.x, f32[1,1536]{1,0:T(1,128)S(1)} %get-tuple-element.83.gain, f32[256,1536]{1,0:T(8,128)S(1)} %get-tuple-element.51.dy, bf16[256,1536]{1,0:T(8,128)(2,1)S(1)} %get-tuple-element.52.dyb, ...), custom_call_target="tpu_custom_call" | custom-call | flops 3623878656 | bytes 14155776 | tf_op jit(solution)/shard_map/pallas_call | solution.py:411
  354.3 1.3 collective-permute-start
  355.6 20.3 %shard_map.156 = (bf16[4096,256]{1,0:T(8,128)(2,1)S(1)}, bf16[256,4096]{1,0:T(8,128)(2,1)}, bf16[256,4096]{1,0:T(8,128)(2,1)}, bf16[1536,256]{1,0:T(8,128)(2,1)S(1)}, bf16[256,1536]{1,0:T(8,128)(2,1)}) custom-call(f32[256,1536]{1,0:T(8,128)S(1)} %get-tuple-element.55.y, f32[1,1536]{1,0:T(1,128)S(1)} %get-tuple-element.82.gain, f32[256,1]{1,0:T(8,128)S(1)} %copy-done.5, ...), custom_call_target="tpu_custom_call" | custom-call | flops 9663676416 | bytes 37748736 | tf_op jit(solution)/shard_map/pallas_call | solution.py:127
  376.0 2.6 fusion.1.dz
  379.4 20.7 %shard_map.157 = (f32[256,1536]{1,0:T(8,128)S(1)}, bf16[256,1536]{1,0:T(8,128)(2,1)S(1)}, f32[1,1536]{1,0:T(1,128)S(1)}, bf16[256,4096]{1,0:T(8,128)(2,1)}, bf16[256,4096]{1,0:T(8,128)(2,1)}) custom-call(f32[256,1536]{1,0:T(8,128)S(1)} %get-tuple-element.55.y, bf16[256,1536]{1,0:T(8,128)(2,1)S(1)} %fusion.1.dz, f32[1,1536]{1,0:T(1,128)S(1)} %get-tuple-element.82.gain, ...), custom_call_target="tpu_custom_call" | custom-call | flops 16106127360 | bytes 37748736 | tf_op jit(solution)/shard_map/pallas_call | solution.py:203
  400.1 15.7 %shard_map.158 = (f32[256,1536]{1,0:T(8,128)}, f32[1,1536]{1,0:T(1,128)S(1)}, bf16[256,3072]{1,0:T(8,128)(2,1)S(1)}) custom-call(s32[3]{0:T(128)S(1)} %pad_add_fusion.info, bf16[256,1536]{1,0:T(8,128)(2,1)S(1)} %broadcast_select_fusion.x, f32[1,1536]{1,0:T(1,128)S(1)} %get-tuple-element.83.gain, f32[256,1536]{1,0:T(8,128)S(1)} %get-tuple-element.65.dy, ...), custom_call_target="tpu_custom_call" | custom-call | flops 3623878656 | bytes 14155776 | tf_op jit(solution)/shard_map/pallas_call | solution.py:411
  415.8 1.1 copy-done.8
  417.6 1.3 copy-done.17
  419.4 311.9 %shard_map.159 = (bf16[384,11264]{1,0:T(8,128)(2,1)}, bf16[1408,1536]{1,0:T(8,128)(2,1)}, f32[8,1536]{1,0:T(8,128)}) custom-call(bf16[4096,256]{1,0:T(8,128)(2,1)} %copy-done.7, bf16[1536,256]{1,0:T(8,128)(2,1)} %copy-done.9, bf16[1536,256]{1,0:T(8,128)(2,1)} %copy-done.13, bf16[1536,256]{1,0:T(8,128)(2,1)} %copy-done.11, bf16[4096,256]{1,0:T(8,128)(2,1)} %copy-done.17, ...), custom_call_target="tpu_custom_call" | custom-call | flops 13287555072 | bytes 40000000 | tf_op jit(solution)/shard_map/pallas_call | solution.py:938
  731.3 4.6 bitcast_convert_fusion.2
  735.9 9.2 %bitcast_convert_fusion = f32[1,384,8192]{2,1,0:T(8,128)} fusion(bf16[384,11264]{1,0:T(8,128)(2,1)} %get-tuple-element.78), kind=kLoop, calls=%fused_computation | loop fusion | flops 3145728 | bytes 18874368 | tf_op jit(solution)/shard_map/broadcast_in_dim | solution.py:1433
  745.1 1.7 bitcast_convert_fusion.3
  746.8 3.6 bitcast_convert_fusion.1
  750.4 1.4 fusion.5
  (60 shorter events, 3.9 us)
Async XLA Ops:
  5.2 294.6 %copy-start.14 = (bf16[2,128,1536]{2,1,0:T(8,128)(2,1)S(1)}, bf16[2,128,1536]{2,1,0:T(8,128)(2,1)}, u32[]{:S(2)}) copy-start(bf16[2,128,1536]{2,1,0:T(8,128)(2,1)} %param.9) | copy-start | bytes 2359300
  299.8 1.3 copy-start.3
  299.8 1.3 copy-start.4
  301.1 2.3 copy-start
  317.0 23.7 %copy-start.9 = (bf16[1536,256]{1,0:T(8,128)(2,1)}, bf16[1536,256]{1,0:T(8,128)(2,1)S(1)}, u32[]{:S(2)}) copy-start(bf16[1536,256]{1,0:T(8,128)(2,1)S(1)} %get-tuple-element.69.ot) | copy-start | bytes 2359300
  317.0 23.7 %copy-start.1 = (bf16[3072,256]{1,0:T(8,128)(2,1)}, bf16[3072,256]{1,0:T(8,128)(2,1)S(1)}, u32[]{:S(2)}) copy-start(bf16[3072,256]{1,0:T(8,128)(2,1)S(1)} %get-tuple-element.53.qkvt) | copy-start | bytes 4718596
  340.7 14.9 %copy-start.5 = (f32[256,1]{1,0:T(8,128)S(1)}, f32[256,1]{1,0:T(8,128)}, u32[]{:S(2)}) copy-start(f32[256,1]{1,0:T(8,128)} %copy.24.refs_6_.mask) | copy-start | bytes 3076
  354.3 21.6 %collective-permute-start = (bf16[256,1536]{1,0:T(8,128)(2,1)S(1)}, bf16[256,1536]{1,0:T(8,128)(2,1)}, u32[]{:S(2)}, u32[]{:S(2)}) collective-permute-start(bf16[256,1536]{1,0:T(8,128)(2,1)S(1)} %shard_map.155), channel_id=1, source_target_pairs={{16,0},{17,1},{18,2},{19,3},{20,4},{21,5},{22,6},{23,7},{24,8},{25... | collective-permute-start | bytes 2359304 | tf_op jit(solution)/shard_map/ppermute | solution.py:25
  355.6 20.4 %copy-start.16 = (bf16[2,128,1536]{2,1,0:T(8,128)(2,1)S(1)}, bf16[2,128,1536]{2,1,0:T(8,128)(2,1)}, u32[]{:S(2)}) copy-start(bf16[2,128,1536]{2,1,0:T(8,128)(2,1)} %param.10) | copy-start | bytes 2359300
  375.9 24.1 %copy-start.7 = (bf16[4096,256]{1,0:T(8,128)(2,1)}, bf16[4096,256]{1,0:T(8,128)(2,1)S(1)}, u32[]{:S(2)}) copy-start(bf16[4096,256]{1,0:T(8,128)(2,1)S(1)} %get-tuple-element.68.at) | copy-start | bytes 6291460
  375.9 24.1 %copy-start.13 = (bf16[1536,256]{1,0:T(8,128)(2,1)}, bf16[1536,256]{1,0:T(8,128)(2,1)S(1)}, u32[]{:S(2)}) copy-start(bf16[1536,256]{1,0:T(8,128)(2,1)S(1)} %get-tuple-element.70.n2t) | copy-start | bytes 2359300
  375.9 2.8 copy-start.10
  375.9 3.4 copy-start.12
  375.9 41.7 %collective-permute-start.1 = (bf16[4096,256]{1,0:T(8,128)(2,1)S(1)}, bf16[4096,256]{1,0:T(8,128)(2,1)S(1)}, u32[]{:S(2)}, u32[]{:S(2)}) collective-permute-start(bf16[4096,256]{1,0:T(8,128)(2,1)S(1)} %get-tuple-element.68.at), channel_id=1, source_target_pairs={{0,1},{1,0},{2,3},{3,2},{4,5},{5,4},{6,7},{7,6},{8,9},{9,8},{10,11... | collective-permute-start | bytes 6291464 | tf_op jit(solution)/shard_map/ppermute | solution.py:29
  378.7 21.4 %copy-start.2 = (bf16[256,1536]{1,0:T(8,128)(2,1)}, bf16[256,1536]{1,0:T(8,128)(2,1)S(1)}, u32[]{:S(2)}) copy-start(bf16[256,1536]{1,0:T(8,128)(2,1)S(1)} %fusion.1.dz) | copy-start | bytes 2359300
  378.7 38.9 %collective-permute-start.2 = (bf16[1536,256]{1,0:T(8,128)(2,1)S(1)}, bf16[1536,256]{1,0:T(8,128)(2,1)S(1)}, u32[]{:S(2)}, u32[]{:S(2)}) collective-permute-start(bf16[1536,256]{1,0:T(8,128)(2,1)S(1)} %copy-done.10), channel_id=1, source_target_pairs={{0,1},{1,0},{2,3},{3,2},{4,5},{5,4},{6,7},{7,6},{8,9},{9,8},{10,11... | collective-permute-start | bytes 2359304 | tf_op jit(solution)/shard_map/ppermute | solution.py:29
  378.8 38.8 %collective-permute-start.3 = (bf16[1536,256]{1,0:T(8,128)(2,1)S(1)}, bf16[1536,256]{1,0:T(8,128)(2,1)S(1)}, u32[]{:S(2)}, u32[]{:S(2)}) collective-permute-start(bf16[1536,256]{1,0:T(8,128)(2,1)S(1)} %get-tuple-element.70.n2t), channel_id=1, source_target_pairs={{0,1},{1,0},{2,3},{3,2},{4,5},{5,4},{6,7},{7,6},{8,9},{9,8},{10,11... | collective-permute-start | bytes 2359304 | tf_op jit(solution)/shard_map/ppermute | solution.py:29
  379.3 38.3 %collective-permute-start.4 = (bf16[1536,256]{1,0:T(8,128)(2,1)S(1)}, bf16[1536,256]{1,0:T(8,128)(2,1)}, u32[]{:S(2)}, u32[]{:S(2)}) collective-permute-start(bf16[1536,256]{1,0:T(8,128)(2,1)S(1)} %copy-done.12), channel_id=1, source_target_pairs={{0,1},{1,0},{2,3},{3,2},{4,5},{5,4},{6,7},{7,6},{8,9},{9,8},{10,11... | collective-permute-start | bytes 2359304 | tf_op jit(solution)/shard_map/ppermute | solution.py:29
  400.1 15.7 %copy-start.6 = (bf16[256,1536]{1,0:T(8,128)(2,1)}, bf16[256,1536]{1,0:T(8,128)(2,1)S(1)}, u32[]{:S(2)}) copy-start(bf16[256,1536]{1,0:T(8,128)(2,1)S(1)} %get-tuple-element.66.dyb.dy) | copy-start | bytes 2359300
  417.6 1.6 copy-start.18
  417.6 1.8 copy-start.19
  417.6 1.4 copy-start.17
  731.3 13.7 %slice-start = ((s8[4325376]{0:T(1024)(128)(4,1)}), s8[4194304]{0:T(1024)(128)(4,1)S(1)}, s32[]{:S(2)}) async-start(s8[4325376]{0:T(1024)(128)(4,1)} %bitcast.55), calls=%async_computation | async-start | bytes 8388608
  735.9 9.2 %slice-start.1 = ((s8[4325376]{0:T(1024)(128)(4,1)}), s8[131072]{0:T(1024)(128)(4,1)S(1)}, s32[]{:S(2)}) async-start(s8[4325376]{0:T(1024)(128)(4,1)} %bitcast.55), calls=%async_computation.1 | async-start | bytes 262144
  (3 other events, 3.2 us)

commit v9 on v8

--- a/solution.py
+++ b/solution.py
@@ -34,7 +34,7 @@
     return (position[None, :] < lengths[:, None]).astype(jnp.float32)[..., None]
 
 
-FF_CHUNK = 512
+FF_CHUNK = 1024
 across = (((1,), (1,)), ((), ()))
 down_rows = (((0,), (0,)), ((), ()))
 
@@ -987,7 +987,7 @@
     (2, False, True),
     (1, False, False),
     (8, True, False),
-    (4, False, False),
+    (6, False, False),
 )
 
 

time: 761 us -> 755 us (level)
  transfers between devices with their start and end apart: 5 -> 5, of which waited for: 0 -> 1; matrix products, arithmetic and copies ran while one was open for 0% -> 0% of each run, Pallas kernels for 8% -> 7%
where the time goes in v9:
time: 755 us; the launch traced here: 746 us
  Pallas kernels  707 us (94%)
  other arithmetic  24.6 us (3%)
  local copies, waits for them, and re-layouts  10.8 us (1%)
    pallas_call x1, Pallas kernels, summed_grads(): pl.pallas_call(functools.partial(grad_kernel, plan), out_shape=(jax.Shape...  313 us
    pallas_call x1, Pallas kernels, gathered(): pl.pallas_call(functools.partial(gather_kernel, groups, A, families, rows...  290 us
    pallas_call x2, Pallas kernels, ffn_backward(): pl.pallas_call(functools.partial(ffn_backward_kernel, bool(factors)), gri...  43.5 us
    pallas_call x2, Pallas kernels, attention_backward(): pl.pallas_call(functools.partial(attention_backward_kernel, rows, keep),...  29.5 us
    broadcast_in_dim x4, other arithmetic, body(): shard_sum[None]  19 us
    pallas_call x1, Pallas kernels, ffn_prepare(): pl.pallas_call(ffn_prepare_kernel, grid=(steps,), out_shape=(shape((hidde...  18.6 us
  transfers between devices with their start and end apart: 5, of which 1 were waited for; matrix products, arithmetic and copies ran while one was open for 0% of the time, Pallas kernels for 7%

profile of v9, /device:TPU:0, one launch (start us, length us, event | category | flops | bytes accessed | tf_op | source)
XLA Modules:
  0.0 746.3 jit_solution(12349455806563123973)
XLA Ops:
  0.7 0.7 fusion.4
  1.4 0.7 pad_add_fusion.info
  2.9 0.8 copy.24.refs_6_.mask
  5.2 289.7 %shard_map.152 = (bf16[16,96,128]{2,1,0:T(8,128)(2,1)}, bf16[16,96,3072]{2,1,0:T(8,128)(2,1)}, bf16[16,96,1536]{2,1,0:T(8,128)(2,1)}, bf16[16,96,8192]{2,1,0:T(8...) custom-call(bf16[96,128]{1,0:T(8,128)(2,1)} %pad.8.refs_0_, ...), custom_call_target="tpu_custom_call" | custom-call | tf_op jit(solution)/shard_map/pallas_call | solution.py:1340
  295.1 0.9 fusion.6
  296.3 2.3 copy-done
  298.6 12.7 %shard_map.153 = (f32[256,1536]{1,0:T(8,128)S(1)}, bf16[3072,256]{1,0:T(8,128)(2,1)S(1)}, f32[16,256]{1,0:T(8,128)S(1)}, bf16[1536,256]{1,0:T(8,128)(2,1)S(1)}, bf16[1536,256]{1,0:T(8,128)(2,1)S(1)}) custom-call(s32[3]{0:T(128)S(1)} %pad_add_fusion.info, bf16[256,1536]{1,0:T(8,128)(2,1)S(1)} %broadcast_select_fusion.x, ...), custom_call_target="tpu_custom_call" | custom-call | flops 3623878656 | bytes 14155776 | tf_op jit(solution)/shard_map/pallas_call | solution.py:377
  311.3 0.9 copy-done.11
  312.2 24.4 %shard_map.154 = (f32[256,1536]{1,0:T(8,128)S(1)}, bf16[256,1536]{1,0:T(8,128)(2,1)S(1)}, f32[1,1536]{1,0:T(1,128)}) custom-call(f32[256,1536]{1,0:T(8,128)S(1)} %get-tuple-element.55.y, bf16[256,1536]{1,0:T(8,128)(2,1)S(1)} %fusion.dz, f32[1,1536]{1,0:T(1,128)S(1)} %get-tuple-element.82.gain, bf16[1536,8192]{1,0:T(8,128)(2,1)} %bitcast.43, ...), custom_call_target="tpu_custom_call" | custom-call | flops 16106127360 | bytes 37748736 | tf_op jit(solution)/shard_map/pallas_call | solution.py:203
  336.6 13.8 %shard_map.155 = bf16[256,1536]{1,0:T(8,128)(2,1)S(1)} custom-call(s32[3]{0:T(128)S(1)} %pad_add_fusion.info, bf16[256,1536]{1,0:T(8,128)(2,1)S(1)} %broadcast_select_fusion.x, f32[1,1536]{1,0:T(1,128)S(1)} %get-tuple-element.83.gain, f32[256,1536]{1,0:T(8,128)S(1)} %get-tuple-element.51.dy, bf16[256,1536]{1,0:T(8,128)(2,1)S(1)} %get-tuple-element.52.dyb, ...), custom_call_target="tpu_custom_call" | custom-call | flops 3623878656 | bytes 14155776 | tf_op jit(solution)/shard_map/pallas_call | solution.py:411
  350.3 1.3 collective-permute-start
  351.7 18.6 %shard_map.156 = (bf16[4096,256]{1,0:T(8,128)(2,1)S(1)}, bf16[256,4096]{1,0:T(8,128)(2,1)}, bf16[256,4096]{1,0:T(8,128)(2,1)}, bf16[1536,256]{1,0:T(8,128)(2,1)S(1)}, bf16[256,1536]{1,0:T(8,128)(2,1)}) custom-call(f32[256,1536]{1,0:T(8,128)S(1)} %get-tuple-element.55.y, f32[1,1536]{1,0:T(1,128)S(1)} %get-tuple-element.82.gain, f32[256,1]{1,0:T(8,128)S(1)} %copy-done.5, ...), custom_call_target="tpu_custom_call" | custom-call | flops 9663676416 | bytes 37748736 | tf_op jit(solution)/shard_map/pallas_call | solution.py:127
  370.3 0.8 collective-permute-done
  371.1 2.3 fusion.1.dz
  374.1 19.2 %shard_map.157 = (f32[256,1536]{1,0:T(8,128)S(1)}, bf16[256,1536]{1,0:T(8,128)(2,1)S(1)}, f32[1,1536]{1,0:T(1,128)S(1)}, bf16[256,4096]{1,0:T(8,128)(2,1)}, bf16[256,4096]{1,0:T(8,128)(2,1)}) custom-call(f32[256,1536]{1,0:T(8,128)S(1)} %get-tuple-element.55.y, bf16[256,1536]{1,0:T(8,128)(2,1)S(1)} %fusion.1.dz, f32[1,1536]{1,0:T(1,128)S(1)} %get-tuple-element.82.gain, ...), custom_call_target="tpu_custom_call" | custom-call | flops 16106127360 | bytes 37748736 | tf_op jit(solution)/shard_map/pallas_call | solution.py:203
  393.3 15.7 %shard_map.158 = (f32[256,1536]{1,0:T(8,128)}, f32[1,1536]{1,0:T(1,128)S(1)}, bf16[256,3072]{1,0:T(8,128)(2,1)S(1)}) custom-call(s32[3]{0:T(128)S(1)} %pad_add_fusion.info, bf16[256,1536]{1,0:T(8,128)(2,1)S(1)} %broadcast_select_fusion.x, f32[1,1536]{1,0:T(1,128)S(1)} %get-tuple-element.83.gain, f32[256,1536]{1,0:T(8,128)S(1)} %get-tuple-element.65.dy, ...), custom_call_target="tpu_custom_call" | custom-call | flops 3623878656 | bytes 14155776 | tf_op jit(solution)/shard_map/pallas_call | solution.py:411
  409.0 1.1 copy-done.8
  410.8 1.3 copy-done.17
  412.6 312.8 %shard_map.159 = (bf16[384,11264]{1,0:T(8,128)(2,1)}, bf16[1408,1536]{1,0:T(8,128)(2,1)}, f32[8,1536]{1,0:T(8,128)}) custom-call(bf16[4096,256]{1,0:T(8,128)(2,1)} %copy-done.7, bf16[1536,256]{1,0:T(8,128)(2,1)} %copy-done.9, bf16[1536,256]{1,0:T(8,128)(2,1)} %copy-done.13, bf16[1536,256]{1,0:T(8,128)(2,1)} %copy-done.11, bf16[4096,256]{1,0:T(8,128)(2,1)} %copy-done.17, ...), custom_call_target="tpu_custom_call" | custom-call | flops 13287555072 | bytes 40000000 | tf_op jit(solution)/shard_map/pallas_call | solution.py:938
  725.4 4.6 bitcast_convert_fusion.2
  730.0 9.2 %bitcast_convert_fusion = f32[1,384,8192]{2,1,0:T(8,128)} fusion(bf16[384,11264]{1,0:T(8,128)(2,1)} %get-tuple-element.78), kind=kLoop, calls=%fused_computation | loop fusion | flops 3145728 | bytes 18874368 | tf_op jit(solution)/shard_map/broadcast_in_dim | solution.py:1433
  739.2 1.7 bitcast_convert_fusion.3
  740.9 3.6 bitcast_convert_fusion.1
  744.4 1.4 fusion.5
  (60 shorter events, 4.5 us)
Async XLA Ops:
  5.2 289.7 %copy-start.14 = (bf16[2,128,1536]{2,1,0:T(8,128)(2,1)S(1)}, bf16[2,128,1536]{2,1,0:T(8,128)(2,1)}, u32[]{:S(2)}) copy-start(bf16[2,128,1536]{2,1,0:T(8,128)(2,1)} %param.9) | copy-start | bytes 2359300
  294.9 1.3 copy-start.3
  294.9 1.3 copy-start.4
  296.3 2.3 copy-start
  312.2 24.4 %copy-start.9 = (bf16[1536,256]{1,0:T(8,128)(2,1)}, bf16[1536,256]{1,0:T(8,128)(2,1)S(1)}, u32[]{:S(2)}) copy-start(bf16[1536,256]{1,0:T(8,128)(2,1)S(1)} %get-tuple-element.69.ot) | copy-start | bytes 2359300
  312.2 24.4 %copy-start.1 = (bf16[3072,256]{1,0:T(8,128)(2,1)}, bf16[3072,256]{1,0:T(8,128)(2,1)S(1)}, u32[]{:S(2)}) copy-start(bf16[3072,256]{1,0:T(8,128)(2,1)S(1)} %get-tuple-element.53.qkvt) | copy-start | bytes 4718596
  336.6 15.1 %copy-start.5 = (f32[256,1]{1,0:T(8,128)S(1)}, f32[256,1]{1,0:T(8,128)}, u32[]{:S(2)}) copy-start(f32[256,1]{1,0:T(8,128)} %copy.24.refs_6_.mask) | copy-start | bytes 3076
  350.3 20.8 %collective-permute-start = (bf16[256,1536]{1,0:T(8,128)(2,1)S(1)}, bf16[256,1536]{1,0:T(8,128)(2,1)}, u32[]{:S(2)}, u32[]{:S(2)}) collective-permute-start(bf16[256,1536]{1,0:T(8,128)(2,1)S(1)} %shard_map.155), channel_id=1, source_target_pairs={{16,0},{17,1},{18,2},{19,3},{20,4},{21,5},{22,6},{23,7},{24,8},{25... | collective-permute-start | bytes 2359304 | tf_op jit(solution)/shard_map/ppermute | solution.py:25
  351.6 19.5 %copy-start.16 = (bf16[2,128,1536]{2,1,0:T(8,128)(2,1)S(1)}, bf16[2,128,1536]{2,1,0:T(8,128)(2,1)}, u32[]{:S(2)}) copy-start(bf16[2,128,1536]{2,1,0:T(8,128)(2,1)} %param.10) | copy-start | bytes 2359300
  370.3 22.9 %copy-start.7 = (bf16[4096,256]{1,0:T(8,128)(2,1)}, bf16[4096,256]{1,0:T(8,128)(2,1)S(1)}, u32[]{:S(2)}) copy-start(bf16[4096,256]{1,0:T(8,128)(2,1)S(1)} %get-tuple-element.68.at) | copy-start | bytes 6291460
  370.3 22.9 %copy-start.13 = (bf16[1536,256]{1,0:T(8,128)(2,1)}, bf16[1536,256]{1,0:T(8,128)(2,1)S(1)}, u32[]{:S(2)}) copy-start(bf16[1536,256]{1,0:T(8,128)(2,1)S(1)} %get-tuple-element.70.n2t) | copy-start | bytes 2359300
  370.3 3.1 copy-start.10
  370.3 3.6 copy-start.12
  371.1 39.7 %collective-permute-start.1 = (bf16[4096,256]{1,0:T(8,128)(2,1)S(1)}, bf16[4096,256]{1,0:T(8,128)(2,1)S(1)}, u32[]{:S(2)}, u32[]{:S(2)}) collective-permute-start(bf16[4096,256]{1,0:T(8,128)(2,1)S(1)} %get-tuple-element.68.at), channel_id=1, source_target_pairs={{0,1},{1,0},{2,3},{3,2},{4,5},{5,4},{6,7},{7,6},{8,9},{9,8},{10,11... | collective-permute-start | bytes 6291464 | tf_op jit(solution)/shard_map/ppermute | solution.py:29
  373.4 19.9 %copy-start.2 = (bf16[256,1536]{1,0:T(8,128)(2,1)}, bf16[256,1536]{1,0:T(8,128)(2,1)S(1)}, u32[]{:S(2)}) copy-start(bf16[256,1536]{1,0:T(8,128)(2,1)S(1)} %fusion.1.dz) | copy-start | bytes 2359300
  373.4 37.4 %collective-permute-start.2 = (bf16[1536,256]{1,0:T(8,128)(2,1)S(1)}, bf16[1536,256]{1,0:T(8,128)(2,1)S(1)}, u32[]{:S(2)}, u32[]{:S(2)}) collective-permute-start(bf16[1536,256]{1,0:T(8,128)(2,1)S(1)} %copy-done.10), channel_id=1, source_target_pairs={{0,1},{1,0},{2,3},{3,2},{4,5},{5,4},{6,7},{7,6},{8,9},{9,8},{10,11... | collective-permute-start | bytes 2359304 | tf_op jit(solution)/shard_map/ppermute | solution.py:29
  373.5 37.3 %collective-permute-start.3 = (bf16[1536,256]{1,0:T(8,128)(2,1)S(1)}, bf16[1536,256]{1,0:T(8,128)(2,1)S(1)}, u32[]{:S(2)}, u32[]{:S(2)}) collective-permute-start(bf16[1536,256]{1,0:T(8,128)(2,1)S(1)} %get-tuple-element.70.n2t), channel_id=1, source_target_pairs={{0,1},{1,0},{2,3},{3,2},{4,5},{5,4},{6,7},{7,6},{8,9},{9,8},{10,11... | collective-permute-start | bytes 2359304 | tf_op jit(solution)/shard_map/ppermute | solution.py:29
  374.0 36.8 %collective-permute-start.4 = (bf16[1536,256]{1,0:T(8,128)(2,1)S(1)}, bf16[1536,256]{1,0:T(8,128)(2,1)}, u32[]{:S(2)}, u32[]{:S(2)}) collective-permute-start(bf16[1536,256]{1,0:T(8,128)(2,1)S(1)} %copy-done.12), channel_id=1, source_target_pairs={{0,1},{1,0},{2,3},{3,2},{4,5},{5,4},{6,7},{7,6},{8,9},{9,8},{10,11... | collective-permute-start | bytes 2359304 | tf_op jit(solution)/shard_map/ppermute | solution.py:29
  393.2 15.7 %copy-start.6 = (bf16[256,1536]{1,0:T(8,128)(2,1)}, bf16[256,1536]{1,0:T(8,128)(2,1)S(1)}, u32[]{:S(2)}) copy-start(bf16[256,1536]{1,0:T(8,128)(2,1)S(1)} %get-tuple-element.66.dyb.dy) | copy-start | bytes 2359300
  410.8 1.6 copy-start.18
  410.8 1.8 copy-start.19
  410.8 1.4 copy-start.17
  725.4 13.7 %slice-start = ((s8[4325376]{0:T(1024)(128)(4,1)}), s8[4194304]{0:T(1024)(128)(4,1)S(1)}, s32[]{:S(2)}) async-start(s8[4325376]{0:T(1024)(128)(4,1)} %bitcast.55), calls=%async_computation | async-start | bytes 8388608
  730.0 9.2 %slice-start.1 = ((s8[4325376]{0:T(1024)(128)(4,1)}), s8[131072]{0:T(1024)(128)(4,1)S(1)}, s32[]{:S(2)}) async-start(s8[4325376]{0:T(1024)(128)(4,1)} %bitcast.55), calls=%async_computation.1 | async-start | bytes 262144
  (3 other events, 3.2 us)

commit v10 on v9

--- a/solution.py
+++ b/solution.py
@@ -462,6 +462,7 @@
 YS_RING = 4
 HOP = 2
 LEAD = 2
+YLAG = 2
 
 
 def grad_kernel(
@@ -722,7 +723,7 @@
             operands_here(1)
             operands_here(3)
 
-        q1 = t
+        q1 = t - YLAG
 
         @pl.when(live(q1, nY))
         def _():
@@ -775,7 +776,7 @@
 
             at_place(out_l, lambda copy: copy.start())
 
-        q2 = t - LEAD
+        q2 = t - YLAG - LEAD
 
         @pl.when(live(q2, nY))
         def _():
@@ -789,7 +790,7 @@
                     total += YR[q2, k - 1, b].astype(f32)
                 YR[q2, 0, b] = total.astype(bf16)
 
-        qr = t - LEAD - HOP * z
+        qr = t - YLAG - LEAD - HOP * z
 
         @pl.when(live(qr, nY))
         def _():
@@ -804,7 +805,7 @@
 
             at_place(out_r, lambda copy: copy.start())
 
-        qL = t - LEAD - HOP * (G - 1 - z)
+        qL = t - YLAG - LEAD - HOP * (G - 1 - z)
 
         @pl.when(live(qL, nY))
         def _():
@@ -849,7 +850,7 @@
             own_z(pg).start()
             sib_z(pg).start()
 
-        qf = t - LEAD - HOP * far
+        qf = t - YLAG - LEAD - HOP * far
 
         @pl.when(live(qf, nY))
         def _():
@@ -863,7 +864,7 @@
             own_y(qf).start()
             sib_own(qf).start()
 
-        qg = t - LEAD - HOP * far - LEAD
+        qg = t - YLAG - LEAD - HOP * far - LEAD
 
         @pl.when(live(qg, nY))
         def _():
@@ -874,7 +875,7 @@
 
         return carry
 
-    steps = max(nY, nZ) + 2 * LEAD + HOP * (G - 1)
+    steps = max(nY + YLAG, nZ) + 2 * LEAD + HOP * (G - 1)
     lax.fori_loop(0, steps, step, 0)
 
     gain_core().wait_send()
@@ -1347,6 +1348,27 @@
             collective_id=5, has_side_effects=True, vmem_limit_bytes=56 * 1024 * 1024
         ),
     )(*shards, *extra)
+
+
+def widen_kernel(source, *parts):
+    start = 0
+    for part in parts:
+        part[...] = source[:, start : start + part.shape[1]].astype(jnp.float32)
+        start += part.shape[1]
+
+
+def widened(source, widths):
+    rows, cols = source.shape
+    band = 32 if rows % 32 == 0 else 16
+    return pl.pallas_call(
+        widen_kernel,
+        grid=(rows // band,),
+        out_shape=tuple(jax.ShapeDtypeStruct((rows, width), jnp.float32) for width in widths),
+        in_specs=[pl.BlockSpec((band, cols), lambda i: (i, 0))],
+        out_specs=tuple(pl.BlockSpec((band, width), lambda i: (i, 0)) for width in widths),
+        compiler_params=pltpu.CompilerParams(vmem_limit_bytes=32 * 1024 * 1024),
+        cost_estimate=pl.CostEstimate(flops=0, bytes_accessed=6 * rows * cols, transcendentals=0),
+    )(source)
 
 
 def body(
@@ -1420,14 +1442,14 @@
     gain_sums = lax.dynamic_slice_in_dim(
         gain_sums, lax.axis_index("group") * gain_cols, gain_cols, 1
     )
-    gate_width = gate_up.shape[2]
+    gate_sum, qkv_sum = widened(gate_qkv_sum, (gate_up.shape[2], qkv_weight.shape[2]))
     down_rows = down_weight.shape[1] * lax.axis_size("dp")
     reduced = (
         gain_sums[0],
-        gate_qkv_sum[:, gate_width:].astype(jnp.float32),
+        qkv_sum,
         down_out_sum[down_rows:].astype(jnp.float32),
         gain_sums[1],
-        gate_qkv_sum[:, :gate_width].astype(jnp.float32),
+        gate_sum,
         down_out_sum[:down_rows].astype(jnp.float32),
     )
     return (section_out, input_grads) + tuple((shard_sum[None] for shard_sum in reduced))

time: 755 us -> 750 us (level)
  other arithmetic: 24.6 us -> 14.4 us
    broadcast_in_dim x4 -> x2, other arithmetic: 19 us -> 8.58 us  [body(): shard_sum[None]]
where the time goes in v10:
time: 750 us; the launch traced here: 742 us
  Pallas kernels  712 us (95%)
  other arithmetic  14.4 us (2%)
  local copies, waits for them, and re-layouts  11 us (1%)
    pallas_call x1, Pallas kernels, summed_grads(): pl.pallas_call(functools.partial(grad_kernel, plan), out_shape=(jax.Shape...  311 us
    pallas_call x1, Pallas kernels, gathered(): pl.pallas_call(functools.partial(gather_kernel, groups, A, families, rows...  290 us
    pallas_call x2, Pallas kernels, ffn_backward(): pl.pallas_call(functools.partial(ffn_backward_kernel, bool(factors)), gri...  43.6 us
    pallas_call x2, Pallas kernels, attention_backward(): pl.pallas_call(functools.partial(attention_backward_kernel, rows, keep),...  29.4 us
    pallas_call x1, Pallas kernels, ffn_prepare(): pl.pallas_call(ffn_prepare_kernel, grid=(steps,), out_shape=(shape((hidde...  18.9 us
  transfers between devices with their start and end apart: 5, of which 1 were waited for; matrix products, arithmetic and copies ran while one was open for 0% of the time, Pallas kernels for 7%

profile of v10, /device:TPU:0, one launch (start us, length us, event | category | flops | bytes accessed | tf_op | source)
XLA Modules:
  0.0 741.5 jit_solution(1665699499110535239)
XLA Ops:
  0.7 0.7 fusion.4
  1.4 0.7 pad_add_fusion.info
  2.1 0.7 pad_maximum_fusion
  2.9 0.8 copy.24.refs_6_.mask
  4.6 0.6 copy_bitcast_fusion
  5.2 289.7 %shard_map.152 = (bf16[16,96,128]{2,1,0:T(8,128)(2,1)}, bf16[16,96,3072]{2,1,0:T(8,128)(2,1)}, bf16[16,96,1536]{2,1,0:T(8,128)(2,1)}, bf16[16,96,8192]{2,1,0:T(8...) custom-call(bf16[96,128]{1,0:T(8,128)(2,1)} %pad.8.refs_0_, ...), custom_call_target="tpu_custom_call" | custom-call | tf_op jit(solution)/shard_map/pallas_call | solution.py:1341
  295.1 0.9 fusion.6
  296.3 2.3 copy-done
  298.6 12.7 %shard_map.153 = (f32[256,1536]{1,0:T(8,128)S(1)}, bf16[3072,256]{1,0:T(8,128)(2,1)S(1)}, f32[16,256]{1,0:T(8,128)S(1)}, bf16[1536,256]{1,0:T(8,128)(2,1)S(1)}, bf16[1536,256]{1,0:T(8,128)(2,1)S(1)}) custom-call(s32[3]{0:T(128)S(1)} %pad_add_fusion.info, bf16[256,1536]{1,0:T(8,128)(2,1)S(1)} %broadcast_select_fusion.x, ...), custom_call_target="tpu_custom_call" | custom-call | flops 3623878656 | bytes 14155776 | tf_op jit(solution)/shard_map/pallas_call | solution.py:377
  311.3 0.9 copy-done.12
  312.2 24.4 %shard_map.154 = (f32[256,1536]{1,0:T(8,128)S(1)}, bf16[256,1536]{1,0:T(8,128)(2,1)S(1)}, f32[1,1536]{1,0:T(1,128)}) custom-call(f32[256,1536]{1,0:T(8,128)S(1)} %get-tuple-element.57.y, bf16[256,1536]{1,0:T(8,128)(2,1)S(1)} %fusion.dz, f32[1,1536]{1,0:T(1,128)S(1)} %get-tuple-element.86.gain, bf16[1536,8192]{1,0:T(8,128)(2,1)} %bitcast.39, ...), custom_call_target="tpu_custom_call" | custom-call | flops 16106127360 | bytes 37748736 | tf_op jit(solution)/shard_map/pallas_call | solution.py:203
  336.6 13.7 %shard_map.155 = bf16[256,1536]{1,0:T(8,128)(2,1)S(1)} custom-call(s32[3]{0:T(128)S(1)} %pad_add_fusion.info, bf16[256,1536]{1,0:T(8,128)(2,1)S(1)} %broadcast_select_fusion.x, f32[1,1536]{1,0:T(1,128)S(1)} %get-tuple-element.87.gain, f32[256,1536]{1,0:T(8,128)S(1)} %get-tuple-element.53.dy, bf16[256,1536]{1,0:T(8,128)(2,1)S(1)} %get-tuple-element.54.dyb, ...), custom_call_target="tpu_custom_call" | custom-call | flops 3623878656 | bytes 14155776 | tf_op jit(solution)/shard_map/pallas_call | solution.py:411
  350.3 1.3 collective-permute-start
  351.6 18.9 %shard_map.156 = (bf16[4096,256]{1,0:T(8,128)(2,1)S(1)}, bf16[256,4096]{1,0:T(8,128)(2,1)}, bf16[256,4096]{1,0:T(8,128)(2,1)}, bf16[1536,256]{1,0:T(8,128)(2,1)S(1)}, bf16[256,1536]{1,0:T(8,128)(2,1)}) custom-call(f32[256,1536]{1,0:T(8,128)S(1)} %get-tuple-element.57.y, f32[1,1536]{1,0:T(1,128)S(1)} %get-tuple-element.86.gain, f32[256,1]{1,0:T(8,128)S(1)} %copy-done.6, ...), custom_call_target="tpu_custom_call" | custom-call | flops 9663676416 | bytes 37748736 | tf_op jit(solution)/shard_map/pallas_call | solution.py:127
  371.1 2.5 fusion.1.dz
  374.3 19.2 %shard_map.157 = (f32[256,1536]{1,0:T(8,128)S(1)}, bf16[256,1536]{1,0:T(8,128)(2,1)S(1)}, f32[1,1536]{1,0:T(1,128)S(1)}, bf16[256,4096]{1,0:T(8,128)(2,1)}, bf16[256,4096]{1,0:T(8,128)(2,1)}) custom-call(f32[256,1536]{1,0:T(8,128)S(1)} %get-tuple-element.57.y, bf16[256,1536]{1,0:T(8,128)(2,1)S(1)} %fusion.1.dz, f32[1,1536]{1,0:T(1,128)S(1)} %get-tuple-element.86.gain, ...), custom_call_target="tpu_custom_call" | custom-call | flops 16106127360 | bytes 37748736 | tf_op jit(solution)/shard_map/pallas_call | solution.py:203
  393.5 15.7 %shard_map.158 = (f32[256,1536]{1,0:T(8,128)}, f32[1,1536]{1,0:T(1,128)S(1)}, bf16[256,3072]{1,0:T(8,128)(2,1)S(1)}) custom-call(s32[3]{0:T(128)S(1)} %pad_add_fusion.info, bf16[256,1536]{1,0:T(8,128)(2,1)S(1)} %broadcast_select_fusion.x, f32[1,1536]{1,0:T(1,128)S(1)} %get-tuple-element.87.gain, f32[256,1536]{1,0:T(8,128)S(1)} %get-tuple-element.67.dy, ...), custom_call_target="tpu_custom_call" | custom-call | flops 3623878656 | bytes 14155776 | tf_op jit(solution)/shard_map/pallas_call | solution.py:411
  409.2 1.1 copy-done.9
  411.1 1.4 copy-done.18
  413.1 310.7 %shard_map.159 = (bf16[384,11264]{1,0:T(8,128)(2,1)}, bf16[1408,1536]{1,0:T(8,128)(2,1)}, f32[8,1536]{1,0:T(8,128)}) custom-call(bf16[4096,256]{1,0:T(8,128)(2,1)} %copy-done.8, bf16[1536,256]{1,0:T(8,128)(2,1)} %copy-done.10, bf16[1536,256]{1,0:T(8,128)(2,1)} %copy-done.14, bf16[1536,256]{1,0:T(8,128)(2,1)} %copy-done.12, bf16[4096,256]{1,0:T(8,128)(2,1)} %copy-done.18, ...), custom_call_target="tpu_custom_call" | custom-call | flops 13287555072 | bytes 40000000 | tf_op jit(solution)/shard_map/pallas_call | solution.py:939
  723.7 3.0 bitcast_convert_fusion.1
  726.7 5.6 bitcast_convert_fusion
  732.3 7.3 shard_map.160
  739.6 1.4 fusion.5
  (58 shorter events, 3.9 us)
Async XLA Ops:
  5.2 289.7 %copy-start.15 = (bf16[2,128,1536]{2,1,0:T(8,128)(2,1)S(1)}, bf16[2,128,1536]{2,1,0:T(8,128)(2,1)}, u32[]{:S(2)}) copy-start(bf16[2,128,1536]{2,1,0:T(8,128)(2,1)} %param.9) | copy-start | bytes 2359300
  294.9 1.3 copy-start.4
  294.9 1.3 copy-start.5
  296.3 2.3 copy-start
  312.2 24.4 %copy-start.10 = (bf16[1536,256]{1,0:T(8,128)(2,1)}, bf16[1536,256]{1,0:T(8,128)(2,1)S(1)}, u32[]{:S(2)}) copy-start(bf16[1536,256]{1,0:T(8,128)(2,1)S(1)} %get-tuple-element.71.ot) | copy-start | bytes 2359300
  312.2 24.4 %copy-start.2 = (bf16[3072,256]{1,0:T(8,128)(2,1)}, bf16[3072,256]{1,0:T(8,128)(2,1)S(1)}, u32[]{:S(2)}) copy-start(bf16[3072,256]{1,0:T(8,128)(2,1)S(1)} %get-tuple-element.55.qkvt) | copy-start | bytes 4718596
  336.6 15.0 %copy-start.6 = (f32[256,1]{1,0:T(8,128)S(1)}, f32[256,1]{1,0:T(8,128)}, u32[]{:S(2)}) copy-start(f32[256,1]{1,0:T(8,128)} %copy.24.refs_6_.mask) | copy-start | bytes 3076
  350.3 20.8 %collective-permute-start = (bf16[256,1536]{1,0:T(8,128)(2,1)S(1)}, bf16[256,1536]{1,0:T(8,128)(2,1)}, u32[]{:S(2)}, u32[]{:S(2)}) collective-permute-start(bf16[256,1536]{1,0:T(8,128)(2,1)S(1)} %shard_map.155), channel_id=1, source_target_pairs={{16,0},{17,1},{18,2},{19,3},{20,4},{21,5},{22,6},{23,7},{24,8},{25... | collective-permute-start | bytes 2359304 | tf_op jit(solution)/shard_map/ppermute | solution.py:25
  351.6 19.5 %copy-start.17 = (bf16[2,128,1536]{2,1,0:T(8,128)(2,1)S(1)}, bf16[2,128,1536]{2,1,0:T(8,128)(2,1)}, u32[]{:S(2)}) copy-start(bf16[2,128,1536]{2,1,0:T(8,128)(2,1)} %param.10) | copy-start | bytes 2359300
  370.5 23.0 %copy-start.8 = (bf16[4096,256]{1,0:T(8,128)(2,1)}, bf16[4096,256]{1,0:T(8,128)(2,1)S(1)}, u32[]{:S(2)}) copy-start(bf16[4096,256]{1,0:T(8,128)(2,1)S(1)} %get-tuple-element.70.at) | copy-start | bytes 6291460
  370.5 22.9 %copy-start.14 = (bf16[1536,256]{1,0:T(8,128)(2,1)}, bf16[1536,256]{1,0:T(8,128)(2,1)S(1)}, u32[]{:S(2)}) copy-start(bf16[1536,256]{1,0:T(8,128)(2,1)S(1)} %get-tuple-element.72.n2t) | copy-start | bytes 2359300
  370.5 3.1 copy-start.11
  370.5 3.6 copy-start.13
  371.1 40.0 %collective-permute-start.1 = (bf16[4096,256]{1,0:T(8,128)(2,1)S(1)}, bf16[4096,256]{1,0:T(8,128)(2,1)S(1)}, u32[]{:S(2)}, u32[]{:S(2)}) collective-permute-start(bf16[4096,256]{1,0:T(8,128)(2,1)S(1)} %get-tuple-element.70.at), channel_id=1, source_target_pairs={{0,1},{1,0},{2,3},{3,2},{4,5},{5,4},{6,7},{7,6},{8,9},{9,8},{10,11... | collective-permute-start | bytes 6291464 | tf_op jit(solution)/shard_map/ppermute | solution.py:29
  373.6 19.9 %copy-start.3 = (bf16[256,1536]{1,0:T(8,128)(2,1)}, bf16[256,1536]{1,0:T(8,128)(2,1)S(1)}, u32[]{:S(2)}) copy-start(bf16[256,1536]{1,0:T(8,128)(2,1)S(1)} %fusion.1.dz) | copy-start | bytes 2359300
  373.6 37.4 %collective-permute-start.2 = (bf16[1536,256]{1,0:T(8,128)(2,1)S(1)}, bf16[1536,256]{1,0:T(8,128)(2,1)S(1)}, u32[]{:S(2)}, u32[]{:S(2)}) collective-permute-start(bf16[1536,256]{1,0:T(8,128)(2,1)S(1)} %copy-done.11), channel_id=1, source_target_pairs={{0,1},{1,0},{2,3},{3,2},{4,5},{5,4},{6,7},{7,6},{8,9},{9,8},{10,11... | collective-permute-start | bytes 2359304 | tf_op jit(solution)/shard_map/ppermute | solution.py:29
  373.7 37.3 %collective-permute-start.3 = (bf16[1536,256]{1,0:T(8,128)(2,1)S(1)}, bf16[1536,256]{1,0:T(8,128)(2,1)S(1)}, u32[]{:S(2)}, u32[]{:S(2)}) collective-permute-start(bf16[1536,256]{1,0:T(8,128)(2,1)S(1)} %get-tuple-element.72.n2t), channel_id=1, source_target_pairs={{0,1},{1,0},{2,3},{3,2},{4,5},{5,4},{6,7},{7,6},{8,9},{9,8},{10,11... | collective-permute-start | bytes 2359304 | tf_op jit(solution)/shard_map/ppermute | solution.py:29
  374.2 36.8 %collective-permute-start.4 = (bf16[1536,256]{1,0:T(8,128)(2,1)S(1)}, bf16[1536,256]{1,0:T(8,128)(2,1)S(1)}, u32[]{:S(2)}, u32[]{:S(2)}) collective-permute-start(bf16[1536,256]{1,0:T(8,128)(2,1)S(1)} %copy-done.13), channel_id=1, source_target_pairs={{0,1},{1,0},{2,3},{3,2},{4,5},{5,4},{6,7},{7,6},{8,9},{9,8},{10,11... | collective-permute-start | bytes 2359304 | tf_op jit(solution)/shard_map/ppermute | solution.py:29
  393.5 15.8 %copy-start.7 = (bf16[256,1536]{1,0:T(8,128)(2,1)}, bf16[256,1536]{1,0:T(8,128)(2,1)S(1)}, u32[]{:S(2)}) copy-start(bf16[256,1536]{1,0:T(8,128)(2,1)S(1)} %get-tuple-element.68.dyb.dy) | copy-start | bytes 2359300
  411.0 2.1 copy-start.19
  411.0 1.6 copy-start.20
  411.0 1.8 copy-start.21
  411.1 1.4 copy-start.18
  726.7 5.6 copy-start.1
  (3 other events, 3.2 us)

commit v11 on v10

--- a/solution.py
+++ b/solution.py
@@ -1359,7 +1359,7 @@
 
 def widened(source, widths):
     rows, cols = source.shape
-    band = 32 if rows % 32 == 0 else 16
+    band = 64 if rows % 64 == 0 else 16
     return pl.pallas_call(
         widen_kernel,
         grid=(rows // band,),

time: 750 us -> 749 us (level)
  no operation moved by 1% of the time
where the time goes in v11:
time: 749 us; the launch traced here: 740 us
  Pallas kernels  711 us (95%)
  other arithmetic  14.4 us (2%)
  local copies, waits for them, and re-layouts  11 us (1%)
    pallas_call x1, Pallas kernels, summed_grads(): pl.pallas_call(functools.partial(grad_kernel, plan), out_shape=(jax.Shape...  311 us
    pallas_call x1, Pallas kernels, gathered(): pl.pallas_call(functools.partial(gather_kernel, groups, A, families, rows...  290 us
    pallas_call x2, Pallas kernels, ffn_backward(): pl.pallas_call(functools.partial(ffn_backward_kernel, bool(factors)), gri...  43.6 us
    pallas_call x2, Pallas kernels, attention_backward(): pl.pallas_call(functools.partial(attention_backward_kernel, rows, keep),...  29.4 us
    pallas_call x1, Pallas kernels, ffn_prepare(): pl.pallas_call(ffn_prepare_kernel, grid=(steps,), out_shape=(shape((hidde...  18.9 us
  transfers between devices with their start and end apart: 5, of which 1 were waited for; matrix products, arithmetic and copies ran while one was open for 0% of the time, Pallas kernels for 7%

profile of v11, /device:TPU:0, one launch (start us, length us, event | category | flops | bytes accessed | tf_op | source)
XLA Modules:
  0.0 740.4 jit_solution(2098709786567376355)
XLA Ops:
  0.7 0.7 fusion.4
  1.4 0.7 pad_add_fusion.info
  2.1 0.7 pad_maximum_fusion
  2.9 0.8 copy.24.refs_6_.mask
  4.6 0.6 copy_bitcast_fusion
  5.2 289.7 %shard_map.152 = (bf16[16,96,128]{2,1,0:T(8,128)(2,1)}, bf16[16,96,3072]{2,1,0:T(8,128)(2,1)}, bf16[16,96,1536]{2,1,0:T(8,128)(2,1)}, bf16[16,96,8192]{2,1,0:T(8...) custom-call(bf16[96,128]{1,0:T(8,128)(2,1)} %pad.8.refs_0_, ...), custom_call_target="tpu_custom_call" | custom-call | tf_op jit(solution)/shard_map/pallas_call | solution.py:1341
  295.1 0.9 fusion.6
  296.3 2.3 copy-done
  298.6 12.7 %shard_map.153 = (f32[256,1536]{1,0:T(8,128)S(1)}, bf16[3072,256]{1,0:T(8,128)(2,1)S(1)}, f32[16,256]{1,0:T(8,128)S(1)}, bf16[1536,256]{1,0:T(8,128)(2,1)S(1)}, bf16[1536,256]{1,0:T(8,128)(2,1)S(1)}) custom-call(s32[3]{0:T(128)S(1)} %pad_add_fusion.info, bf16[256,1536]{1,0:T(8,128)(2,1)S(1)} %broadcast_select_fusion.x, ...), custom_call_target="tpu_custom_call" | custom-call | flops 3623878656 | bytes 14155776 | tf_op jit(solution)/shard_map/pallas_call | solution.py:377
  311.3 0.9 copy-done.12
  312.2 24.4 %shard_map.154 = (f32[256,1536]{1,0:T(8,128)S(1)}, bf16[256,1536]{1,0:T(8,128)(2,1)S(1)}, f32[1,1536]{1,0:T(1,128)}) custom-call(f32[256,1536]{1,0:T(8,128)S(1)} %get-tuple-element.57.y, bf16[256,1536]{1,0:T(8,128)(2,1)S(1)} %fusion.dz, f32[1,1536]{1,0:T(1,128)S(1)} %get-tuple-element.86.gain, bf16[1536,8192]{1,0:T(8,128)(2,1)} %bitcast.39, ...), custom_call_target="tpu_custom_call" | custom-call | flops 16106127360 | bytes 37748736 | tf_op jit(solution)/shard_map/pallas_call | solution.py:203
  336.6 13.7 %shard_map.155 = bf16[256,1536]{1,0:T(8,128)(2,1)S(1)} custom-call(s32[3]{0:T(128)S(1)} %pad_add_fusion.info, bf16[256,1536]{1,0:T(8,128)(2,1)S(1)} %broadcast_select_fusion.x, f32[1,1536]{1,0:T(1,128)S(1)} %get-tuple-element.87.gain, f32[256,1536]{1,0:T(8,128)S(1)} %get-tuple-element.53.dy, bf16[256,1536]{1,0:T(8,128)(2,1)S(1)} %get-tuple-element.54.dyb, ...), custom_call_target="tpu_custom_call" | custom-call | flops 3623878656 | bytes 14155776 | tf_op jit(solution)/shard_map/pallas_call | solution.py:411
  350.3 1.3 collective-permute-start
  351.6 18.9 %shard_map.156 = (bf16[4096,256]{1,0:T(8,128)(2,1)S(1)}, bf16[256,4096]{1,0:T(8,128)(2,1)}, bf16[256,4096]{1,0:T(8,128)(2,1)}, bf16[1536,256]{1,0:T(8,128)(2,1)S(1)}, bf16[256,1536]{1,0:T(8,128)(2,1)}) custom-call(f32[256,1536]{1,0:T(8,128)S(1)} %get-tuple-element.57.y, f32[1,1536]{1,0:T(1,128)S(1)} %get-tuple-element.86.gain, f32[256,1]{1,0:T(8,128)S(1)} %copy-done.6, ...), custom_call_target="tpu_custom_call" | custom-call | flops 9663676416 | bytes 37748736 | tf_op jit(solution)/shard_map/pallas_call | solution.py:127
  371.1 2.5 fusion.1.dz
  374.3 19.2 %shard_map.157 = (f32[256,1536]{1,0:T(8,128)S(1)}, bf16[256,1536]{1,0:T(8,128)(2,1)S(1)}, f32[1,1536]{1,0:T(1,128)S(1)}, bf16[256,4096]{1,0:T(8,128)(2,1)}, bf16[256,4096]{1,0:T(8,128)(2,1)}) custom-call(f32[256,1536]{1,0:T(8,128)S(1)} %get-tuple-element.57.y, bf16[256,1536]{1,0:T(8,128)(2,1)S(1)} %fusion.1.dz, f32[1,1536]{1,0:T(1,128)S(1)} %get-tuple-element.86.gain, ...), custom_call_target="tpu_custom_call" | custom-call | flops 16106127360 | bytes 37748736 | tf_op jit(solution)/shard_map/pallas_call | solution.py:203
  393.5 15.7 %shard_map.158 = (f32[256,1536]{1,0:T(8,128)}, f32[1,1536]{1,0:T(1,128)S(1)}, bf16[256,3072]{1,0:T(8,128)(2,1)S(1)}) custom-call(s32[3]{0:T(128)S(1)} %pad_add_fusion.info, bf16[256,1536]{1,0:T(8,128)(2,1)S(1)} %broadcast_select_fusion.x, f32[1,1536]{1,0:T(1,128)S(1)} %get-tuple-element.87.gain, f32[256,1536]{1,0:T(8,128)S(1)} %get-tuple-element.67.dy, ...), custom_call_target="tpu_custom_call" | custom-call | flops 3623878656 | bytes 14155776 | tf_op jit(solution)/shard_map/pallas_call | solution.py:411
  409.2 1.1 copy-done.9
  411.1 1.4 copy-done.18
  413.1 310.7 %shard_map.159 = (bf16[384,11264]{1,0:T(8,128)(2,1)}, bf16[1408,1536]{1,0:T(8,128)(2,1)}, f32[8,1536]{1,0:T(8,128)}) custom-call(bf16[4096,256]{1,0:T(8,128)(2,1)} %copy-done.8, bf16[1536,256]{1,0:T(8,128)(2,1)} %copy-done.10, bf16[1536,256]{1,0:T(8,128)(2,1)} %copy-done.14, bf16[1536,256]{1,0:T(8,128)(2,1)} %copy-done.12, bf16[4096,256]{1,0:T(8,128)(2,1)} %copy-done.18, ...), custom_call_target="tpu_custom_call" | custom-call | flops 13287555072 | bytes 40000000 | tf_op jit(solution)/shard_map/pallas_call | solution.py:939
  723.7 3.0 bitcast_convert_fusion.1
  726.7 5.6 bitcast_convert_fusion
  732.3 6.1 shard_map.160
  738.4 1.4 fusion.5
  (58 shorter events, 3.9 us)
Async XLA Ops:
  5.2 289.7 %copy-start.15 = (bf16[2,128,1536]{2,1,0:T(8,128)(2,1)S(1)}, bf16[2,128,1536]{2,1,0:T(8,128)(2,1)}, u32[]{:S(2)}) copy-start(bf16[2,128,1536]{2,1,0:T(8,128)(2,1)} %param.9) | copy-start | bytes 2359300
  294.9 1.3 copy-start.4
  294.9 1.3 copy-start.5
  296.3 2.3 copy-start
  312.2 24.4 %copy-start.10 = (bf16[1536,256]{1,0:T(8,128)(2,1)}, bf16[1536,256]{1,0:T(8,128)(2,1)S(1)}, u32[]{:S(2)}) copy-start(bf16[1536,256]{1,0:T(8,128)(2,1)S(1)} %get-tuple-element.71.ot) | copy-start | bytes 2359300
  312.2 24.4 %copy-start.2 = (bf16[3072,256]{1,0:T(8,128)(2,1)}, bf16[3072,256]{1,0:T(8,128)(2,1)S(1)}, u32[]{:S(2)}) copy-start(bf16[3072,256]{1,0:T(8,128)(2,1)S(1)} %get-tuple-element.55.qkvt) | copy-start | bytes 4718596
  336.6 15.0 %copy-start.6 = (f32[256,1]{1,0:T(8,128)S(1)}, f32[256,1]{1,0:T(8,128)}, u32[]{:S(2)}) copy-start(f32[256,1]{1,0:T(8,128)} %copy.24.refs_6_.mask) | copy-start | bytes 3076
  350.3 20.8 %collective-permute-start = (bf16[256,1536]{1,0:T(8,128)(2,1)S(1)}, bf16[256,1536]{1,0:T(8,128)(2,1)}, u32[]{:S(2)}, u32[]{:S(2)}) collective-permute-start(bf16[256,1536]{1,0:T(8,128)(2,1)S(1)} %shard_map.155), channel_id=1, source_target_pairs={{16,0},{17,1},{18,2},{19,3},{20,4},{21,5},{22,6},{23,7},{24,8},{25... | collective-permute-start | bytes 2359304 | tf_op jit(solution)/shard_map/ppermute | solution.py:25
  351.6 19.5 %copy-start.17 = (bf16[2,128,1536]{2,1,0:T(8,128)(2,1)S(1)}, bf16[2,128,1536]{2,1,0:T(8,128)(2,1)}, u32[]{:S(2)}) copy-start(bf16[2,128,1536]{2,1,0:T(8,128)(2,1)} %param.10) | copy-start | bytes 2359300
  370.5 23.0 %copy-start.8 = (bf16[4096,256]{1,0:T(8,128)(2,1)}, bf16[4096,256]{1,0:T(8,128)(2,1)S(1)}, u32[]{:S(2)}) copy-start(bf16[4096,256]{1,0:T(8,128)(2,1)S(1)} %get-tuple-element.70.at) | copy-start | bytes 6291460
  370.5 22.9 %copy-start.14 = (bf16[1536,256]{1,0:T(8,128)(2,1)}, bf16[1536,256]{1,0:T(8,128)(2,1)S(1)}, u32[]{:S(2)}) copy-start(bf16[1536,256]{1,0:T(8,128)(2,1)S(1)} %get-tuple-element.72.n2t) | copy-start | bytes 2359300
  370.5 3.1 copy-start.11
  370.5 3.6 copy-start.13
  371.1 40.0 %collective-permute-start.1 = (bf16[4096,256]{1,0:T(8,128)(2,1)S(1)}, bf16[4096,256]{1,0:T(8,128)(2,1)S(1)}, u32[]{:S(2)}, u32[]{:S(2)}) collective-permute-start(bf16[4096,256]{1,0:T(8,128)(2,1)S(1)} %get-tuple-element.70.at), channel_id=1, source_target_pairs={{0,1},{1,0},{2,3},{3,2},{4,5},{5,4},{6,7},{7,6},{8,9},{9,8},{10,11... | collective-permute-start | bytes 6291464 | tf_op jit(solution)/shard_map/ppermute | solution.py:29
  373.6 19.9 %copy-start.3 = (bf16[256,1536]{1,0:T(8,128)(2,1)}, bf16[256,1536]{1,0:T(8,128)(2,1)S(1)}, u32[]{:S(2)}) copy-start(bf16[256,1536]{1,0:T(8,128)(2,1)S(1)} %fusion.1.dz) | copy-start | bytes 2359300
  373.6 37.4 %collective-permute-start.2 = (bf16[1536,256]{1,0:T(8,128)(2,1)S(1)}, bf16[1536,256]{1,0:T(8,128)(2,1)S(1)}, u32[]{:S(2)}, u32[]{:S(2)}) collective-permute-start(bf16[1536,256]{1,0:T(8,128)(2,1)S(1)} %copy-done.11), channel_id=1, source_target_pairs={{0,1},{1,0},{2,3},{3,2},{4,5},{5,4},{6,7},{7,6},{8,9},{9,8},{10,11... | collective-permute-start | bytes 2359304 | tf_op jit(solution)/shard_map/ppermute | solution.py:29
  373.7 37.3 %collective-permute-start.3 = (bf16[1536,256]{1,0:T(8,128)(2,1)S(1)}, bf16[1536,256]{1,0:T(8,128)(2,1)S(1)}, u32[]{:S(2)}, u32[]{:S(2)}) collective-permute-start(bf16[1536,256]{1,0:T(8,128)(2,1)S(1)} %get-tuple-element.72.n2t), channel_id=1, source_target_pairs={{0,1},{1,0},{2,3},{3,2},{4,5},{5,4},{6,7},{7,6},{8,9},{9,8},{10,11... | collective-permute-start | bytes 2359304 | tf_op jit(solution)/shard_map/ppermute | solution.py:29
  374.2 36.8 %collective-permute-start.4 = (bf16[1536,256]{1,0:T(8,128)(2,1)S(1)}, bf16[1536,256]{1,0:T(8,128)(2,1)S(1)}, u32[]{:S(2)}, u32[]{:S(2)}) collective-permute-start(bf16[1536,256]{1,0:T(8,128)(2,1)S(1)} %copy-done.13), channel_id=1, source_target_pairs={{0,1},{1,0},{2,3},{3,2},{4,5},{5,4},{6,7},{7,6},{8,9},{9,8},{10,11... | collective-permute-start | bytes 2359304 | tf_op jit(solution)/shard_map/ppermute | solution.py:29
  393.5 15.8 %copy-start.7 = (bf16[256,1536]{1,0:T(8,128)(2,1)}, bf16[256,1536]{1,0:T(8,128)(2,1)S(1)}, u32[]{:S(2)}) copy-start(bf16[256,1536]{1,0:T(8,128)(2,1)S(1)} %get-tuple-element.68.dyb.dy) | copy-start | bytes 2359300
  411.0 2.1 copy-start.19
  411.0 1.6 copy-start.20
  411.0 1.8 copy-start.21
  411.1 1.4 copy-start.18
  726.7 5.6 copy-start.1
  (3 other events, 3.2 us)
